TPU v7x, 128 devices: a whole 4x4x4 slice. The times are simulated.
128 devices in a mesh: row: 8 (over y_hi, z), col: 16 (over x, y_lo, core).
Axes of the slice: x: 4, y: 4 (y_hi: 2, y_lo: 2; y = y_hi * 2 + y_lo), z: 4, core: 2. Of those that a mesh axis runs over, the one named last changes fastest.
Arguments:
- integrals: float32 [16384, 32768], P('row', 'col'), may hold values from -0.03125 to 0.03125
- amplitudes: float32 [32768, 1024], P('col', 'row'), may hold values from -6 to 6
- source_order: int32 [1024], replicated, may hold values from 0 to 1023, each once
- target_order: int32 [1024], replicated, may hold values from 0 to 1023, each once
Outputs:
- ladder: float32 [1024, 16384], P('col', 'row')
Inputs may be any that keep to these rules, and one draw needn't show every extreme that they name: `source_order`: each of 0 .. 1023 appears exactly once. `target_order`: each of 0 .. 1023 appears exactly once.
All inputs are finite; a program needn't handle non-finite values.
Results may differ from a plain program's by a relative error of at most 0.00007.
Values sent between devices are 32-bit elements; how exact they have to be, the bound alone decides.
No kernel may reach another device: no remote copies, remote signals or barrier semaphores. Data moves between devices by JAX's collectives and lax.ppermute only.
A program may use at most 128 MiB of HBM per device.

v0:
```python
import jax
import jax.numpy as jnp
from jax import lax
from jax.sharding import PartitionSpec as P


def contract(ordered, integrals):
    return lax.dot_general(
        ordered,
        integrals,
        (((0,), (1,)), ((), ())),
        precision=lax.Precision.HIGHEST,
        preferred_element_type=jnp.float32,
    )


def local(integrals, amplitudes, source_order, target_order):
    length = target_order.shape[0]
    inverse = (
        jnp.zeros((length,), jnp.int32).at[source_order].set(jnp.arange(length, dtype=jnp.int32))
    )
    columns = jnp.take(inverse, target_order)
    gathered = lax.all_gather(amplitudes, "row", axis=1, tiled=True)
    summands = contract(jnp.take(gathered, columns, axis=1), integrals)
    return lax.psum_scatter(summands, "col", scatter_dimension=0, tiled=True)


def solution(mesh):
    in_specs = (P("row", "col"), P("col", "row"), P(), P())
    out_specs = P("col", "row")
    return jax.shard_map(local, mesh=mesh, in_specs=in_specs, out_specs=out_specs, check_vma=False)
```

profile of v0, /device:TPU:0, one launch (start us, length us, event | category | flops | bytes accessed | tf_op | source)
XLA Modules:
  0.0 300.1 jit_solution(13701118939031349474)
XLA Ops:
  6.5 0.0 all-gather.2.cloned.1.call-start
  6.5 2.6 copy.6
  9.1 0.0 all-gather.2.cloned.1.call-update
  9.2 0.0 reduce-scatter.2.cloned.1.call-start
  9.2 0.7 compare_select_fusion.1
  9.9 4.3 %scatter_custom_fusion = s32[1024]{0:T(1024)S(1)} fusion(s32[1024]{0:T(1024)S(1)} %compare_select_fusion.1, s32[1024]{0:T(1024)S(1)} %iota.3, s32[]{:T(128)} %constant.18.clone.1), kind=kCustom, calls=%fused_computation.13 | custom fusion | bytes 4100 | tf_op jit(solution)/shard_map/scatter | solution.py:20
  14.2 0.7 fusion.4
  14.9 4.5 %gather_fusion = s32[1024]{0:T(1024)S(1)} fusion(s32[1024]{0:T(1024)S(1)} %scatter_custom_fusion, s32[1024]{0:T(1024)S(1)} %fusion.4), kind=kCustom, calls=%fused_computation | custom fusion | bytes 12288 | tf_op jit(solution)/shard_map/jit(_take)/gather | solution.py:22
  19.5 0.7 compare_and_fusion
  20.2 0.7 broadcast_clamp_fusion
  20.8 98.6 %all-gather.2.cloned.1.call-done = f32[2048,1024]{0,1:T(8,128)} async-done(((f32[2048,128]{0,1:T(8,128)}), f32[2048,1024]{0,1:T(8,128)}) %all-gather.2.cloned.1.call-update) | async-done | bytes 8388624 | tf_op jit(solution)/shard_map/all_gather | solution.py:23
  119.5 12.4 %gather_fusion.1 = f32[1024,2048]{1,0:T(8,128)} fusion(f32[2048,1024]{0,1:T(8,128)} %all-gather.2.cloned.1.call-done, s32[1024]{0:T(1024)S(1)} %broadcast_clamp_fusion), kind=kCustom, calls=%fused_computation.1 | custom fusion | bytes 16781312 | tf_op jit(solution)/shard_map/jit(_take)/gather | solution.py:24
  131.9 69.1 %fusion = f32[1024,2048]{1,0:T(8,128)} fusion(f32[2048,2048]{1,0:T(8,128)} %param.4, f32[1024,2048]{1,0:T(8,128)} %gather_fusion.1, pred[1024]{0:T(1024)(128)(4,1)S(1)} %compare_and_fusion), kind=kOutput, calls=%fused_computation.3 | convolution fusion | flops 51541704704 | bytes 33555456 | tf_op jit(solution)/shard_map/dot_general | solution.py:8
  201.0 0.0 reduce-scatter.2.cloned.1.call-update
  201.0 92.2 %reduce-scatter.2.cloned.1.call-done = f32[64,2048]{1,0:T(8,128)} async-done(((f32[1024,2048]{1,0:T(8,128)}), f32[64,2048]{1,0:T(8,128)}) %reduce-scatter.2.cloned.1.call-update) | async-done | bytes 524304 | tf_op jit(solution)/shard_map/reduce_scatter | solution.py:25
  (1 shorter events, 0.0 us)
Async XLA Ops:
  6.5 112.9 %all-gather.2.cloned.1.call-start = ((), (), s32[]{:S(2)}) async-start(), calls=%async_computation.1 | async-start | bytes 9437184 | tf_op jit(solution)/shard_map/all_gather | solution.py:23
  9.2 284.1 %reduce-scatter.2.cloned.1.call-start = ((), (), s32[]{:S(2)}) async-start(), calls=%async_computation.2 | async-start | bytes 8912896 | tf_op jit(solution)/shard_map/reduce_scatter | solution.py:25
Sparse Core Ops, SparseCore 0:
  9.7 109.7 all-gather.1
  201.2 92.0 reduce-scatter.1
where the time goes:
time: 304 us; the launch traced here: 300 us
  waiting for transfers between devices  191 us (63%)
  matrix products  69.1 us (23%)
  local copies, waits for them, and re-layouts  23.8 us (8%)
  between operations  13.4 us (4%)
    all_gather x1, waiting for transfers between devices, local(): gathered = lax.all_gather(amplitudes, 'row', axis=1, tiled=True)  98.6 us
    reduce_scatter x1, waiting for transfers between devices, local(): return lax.psum_scatter(summands, 'col', scatter_dimension=0, tiled=True)  92.2 us
    dot_general x1, matrix products, contract(): lax.dot_general(ordered, integrals, (((0,), (1,)), ((), ())), precision=l...  69.1 us
    gather x1, local copies, waits for them, and re-layouts, local(): summands = contract(jnp.take(gathered, columns, axis=1), integrals)  12.4 us
  transfers between devices with their start and end apart: 2, of which 2 were waited for; matrix products, arithmetic and copies ran while one was open for 4% of the time, Pallas kernels for 0%

commit v1 on v0

v1 whole, which is shorter than its diff:
```python
import functools

import jax
import jax.numpy as jnp
from jax import lax
from jax.experimental import pallas as pl
from jax.experimental.pallas import tpu as pltpu
from jax.sharding import PartitionSpec as P

AXES = ("row", "col")
NT = (((1,), (1,)), ((), ()))
X_ROWS = 32
MIB = 1 << 20


def device_index(x, y, z, core):
    return ((y // 2) * 4 + z) * 16 + (x * 2 + y % 2) * 2 + core


def shift(array, dx=0, dy=0, dz=0, flip_y=False, flip_core=False):
    pairs = []
    for x in range(4):
        for y in range(4):
            for z in range(4):
                for core in range(2):
                    to_y = y ^ 1 if flip_y else (y + dy) % 4
                    to = device_index((x + dx) % 4, to_y, (z + dz) % 4, core ^ int(flip_core))
                    pairs.append((device_index(x, y, z, core), to))
    return lax.ppermute(array, AXES, pairs)


def place():
    row, col = lax.axis_index("row"), lax.axis_index("col")
    return col // 4, (col // 2) % 2, col % 2, row // 4, row % 4


def rolled(array, start):
    sizes = array.shape
    return lax.dynamic_slice(jnp.concatenate([array, array]), (start,) + (0,) * (array.ndim - 1), sizes)


def flipped(array, bit, axis):
    return jnp.where(bit == 0, array, jnp.flip(array, axis))


def select_kernel(n, choose_ref, *refs):
    pieces, last_a, last_b, outs = refs[:7], refs[7], refs[8], refs[9:]
    last = jnp.where(pl.program_id(0) == 0, last_a[...], last_b[...])
    block = jnp.concatenate([p[...] for p in pieces] + [last], axis=1)
    high = block.astype(jnp.bfloat16)
    low = (block - high.astype(jnp.float32)).astype(jnp.bfloat16)
    for part, (x_ref, y_ref) in ((high, outs[:2]), (low, outs[2:])):
        rows = lax.dot_general(choose_ref[...], part, NT, preferred_element_type=jnp.float32)
        rows = rows.astype(jnp.bfloat16)
        x_ref[...] = rows[:n]
        y_ref[...] = rows[n:]


def select(choose, pieces, last_a, last_b, n):
    k = pieces[0].shape[0]
    half = k // 2
    q = choose.shape[0]
    piece = pl.BlockSpec((half, 128), lambda i: (i, 0))
    whole = pl.BlockSpec((half, 128), lambda i: (0, 0))
    shapes = [(n, k), (q - n, k)] * 2
    return pl.pallas_call(
        functools.partial(select_kernel, n),
        grid=(2,),
        in_specs=[pl.BlockSpec(choose.shape, lambda i: (0, 0))] + [piece] * 7 + [whole] * 2,
        out_specs=[pl.BlockSpec((s[0], half), lambda i: (0, i)) for s in shapes],
        out_shape=[jax.ShapeDtypeStruct(s, jnp.bfloat16) for s in shapes],
        compiler_params=pltpu.CompilerParams(vmem_limit_bytes=48 * MIB),
        cost_estimate=pl.CostEstimate(flops=4 * q * 1024 * k, bytes_accessed=8 * q * k, transcendentals=0),
        name="select",
    )(choose, *pieces, last_a, last_b)


def contract_kernel(v_ref, ha_ref, la_ref, hb_ref, lb_ref, keep_ref, send_ref):
    v = v_ref[...]
    high = v.astype(jnp.bfloat16)
    low = (v - high.astype(jnp.float32)).astype(jnp.bfloat16)
    k = ha_ref.shape[1]
    dot = functools.partial(lax.dot_general, dimension_numbers=NT, preferred_element_type=jnp.float32)
    total = None
    for h_ref, l_ref, at in ((ha_ref, la_ref, 0), (hb_ref, lb_ref, k)):
        hv, lv = high[:, at : at + k], low[:, at : at + k]
        term = dot(h_ref[...], hv) + dot(h_ref[...], lv) + dot(l_ref[...], hv)
        total = term if total is None else total + term
    half = keep_ref.shape[0]
    keep_ref[...] = total[:half]
    send_ref[...] = total[half:]


def contract(v, ha, la, hb, lb, tile=256):
    n, k = ha.shape
    ab, cd = v.shape
    whole = pl.BlockSpec((n, k), lambda i: (0, 0))
    return pl.pallas_call(
        contract_kernel,
        grid=(ab // tile,),
        in_specs=[pl.BlockSpec((tile, cd), lambda i: (i, 0))] + [whole] * 4,
        out_specs=[pl.BlockSpec((n // 2, tile), lambda i: (0, i))] * 2,
        out_shape=[jax.ShapeDtypeStruct((n // 2, ab), jnp.float32)] * 2,
        compiler_params=pltpu.CompilerParams(vmem_limit_bytes=48 * MIB),
        cost_estimate=pl.CostEstimate(
            flops=6 * n * ab * cd, bytes_accessed=4 * (ab * cd + n * ab + n * cd), transcendentals=0
        ),
        name="contract",
    )(v, ha, la, hb, lb)


def gather(a):
    half = a.shape[0] // 2
    first, second = a[:half], a[half:]
    y_first = shift(first, dy=2)
    second_m = shift(second, dz=1)
    second_p = shift(second, dz=-1)
    first_m = shift(first, dz=1)
    first_p = shift(first, dz=-1)
    y_second = shift(second, dy=2)
    second_2 = shift(second_p, dz=-1)
    first_2 = shift(first_m, dz=1)
    y_second_m = shift(second_m, dy=2)
    y_second_p = shift(second_p, dy=2)
    y_first_m = shift(y_first, dz=1)
    y_first_p = shift(y_first, dz=-1)
    y_first_2a = shift(y_first_m[: half // 2], dz=1)
    y_first_2b = shift(y_first_p[half // 2 :], dz=-1)
    y_second_2 = shift(second_2, dy=2)
    firsts = [first, first_p, first_2, first_m, y_first, y_first_p, y_first_m]
    seconds = [second, second_p, second_2, second_m, y_second, y_second_p, y_second_m]
    return (firsts, y_first_2a, y_first_2b), (seconds, y_second_2[: half // 2], y_second_2[half // 2 :])


def sum_x(blocks):
    half = blocks[2].shape[0] // 2
    up, down = shift(blocks[2][:half], dx=1), shift(blocks[2][half:], dx=-1)
    one = jnp.concatenate([blocks[1][:half] + up, blocks[1][half:]])
    three = jnp.concatenate([blocks[3][:half], blocks[3][half:] + down])
    return blocks[0] + shift(one, dx=1) + shift(three, dx=-1)


def local(integrals, amplitudes, source_order, target_order):
    x, y_lo, core, y_hi, z = place()
    wanted = flipped(flipped(rolled(target_order.reshape(4, 2, 2, 64), x), y_lo, 1), core, 2)
    wanted_x = wanted[..., :X_ROWS].transpose(2, 0, 1, 3).reshape(-1)
    wanted_y = wanted[..., X_ROWS:].transpose(2, 1, 0, 3).reshape(-1)
    wanted = jnp.concatenate([wanted_x, wanted_y])
    held = flipped(rolled(source_order.reshape(2, 4, 128).transpose(1, 0, 2), z), y_hi, 1)
    held = held.transpose(1, 0, 2)
    order = jnp.concatenate([held[0].reshape(-1), held[1, 0], held[1, 1], held[1, 3], held[1, 2]])
    choose = (wanted[:, None] == order[None, :]).astype(jnp.bfloat16)

    first, second = gather(amplitudes)
    n = 16 * X_ROWS
    hxa, hya, lxa, lya = select(choose, *first, n)
    hxb, hyb, lxb, lyb = select(choose, *second, n)

    keep_y, send_y = contract(integrals, hya, lya, hyb, lyb)
    got_y = shift(send_y, flip_core=True)
    keep_x, send_x = contract(integrals, hxa, lxa, hxb, lxb)
    got_x = shift(send_x, flip_core=True)

    half = keep_y.shape[0] // 2
    y_one = keep_y[half:] + got_y[half:]
    y_own = keep_y[:half] + got_y[:half]
    y_sum = y_own + shift(y_one, flip_y=True)
    part = half // 4
    out_y = sum_x([y_sum[part * d : part * (d + 1)] for d in range(4)])

    part = keep_x.shape[0] // 4
    x_sum = sum_x([keep_x[part * d : part * (d + 1)] + got_x[part * d : part * (d + 1)] for d in range(4)])
    out_x = x_sum[: part // 2] + shift(x_sum[part // 2 :], flip_y=True)
    return jnp.concatenate([out_x, out_y])


def solution(mesh):
    in_specs = (P("row", "col"), P("col", "row"), P(), P())
    return jax.shard_map(local, mesh=mesh, in_specs=in_specs, out_specs=P("col", "row"), check_vma=False)
```

time: 304 us -> 186 us (0.61); the launches traced: 300 us -> 185 us
  waiting for transfers between devices: 191 us -> 82.5 us
  matrix products: 69.1 us -> 0 us
  Pallas kernels: 0 us -> 50.3 us
  starting transfers between devices: 0.04 us -> 45.4 us
  local copies, waits for them, and re-layouts: 23.8 us -> 3.08 us
  between operations: 13.4 us -> 0.28 us
    all_gather x1 -> x0, waiting for transfers between devices: 98.6 us -> none  [local(): gathered = lax.all_gather(amplitudes, 'row', axis=1, tiled=True)]
    reduce_scatter x1 -> x0, waiting for transfers between devices: 92.2 us -> none  [local(): return lax.psum_scatter(summands, 'col', scatter_dimension=0, tiled=True)]
    ppermute x0 -> x27, waiting for transfers between devices: none -> 82.5 us  [shift(): return lax.ppermute(array, AXES, pairs)]
    dot_general x1 -> x0, matrix products: 69.1 us -> none  [contract(): lax.dot_general(ordered, integrals, (((0,), (1,)), ((), ())), precision=l...]
    pallas_call x0 -> x4, Pallas kernels: none -> 50.3 us  [the longest x2 34.7 us: contract(): pl.pallas_call(contract_kernel, grid=(ab // tile,), in_specs=[pl.BlockSpe...]
    ppermute x0 -> x27, starting transfers between devices: none -> 45.4 us  [shift(): return lax.ppermute(array, AXES, pairs)]
    gather x2 -> x0, local copies, waits for them, and re-layouts: 16.9 us -> none  [the longest x1 12.4 us: local(): summands = contract(jnp.take(gathered, columns, axis=1), integrals)]
    scatter x1 -> x0, local copies, waits for them, and re-layouts: 4.31 us -> none  [local(): jnp.zeros((length,), jnp.int32).at[source_order]]
  transfers between devices with their start and end apart: 2 -> 27, of which waited for: 2 -> 15; matrix products, arithmetic and copies ran while one was open for 4% -> 2% of each run, Pallas kernels for 0% -> 14%
where the time goes in v1:
time: 186 us; the launch traced here: 185 us
  waiting for transfers between devices  82.5 us (44%)
  Pallas kernels  50.3 us (27%)
  starting transfers between devices  45.4 us (24%)
  other arithmetic  3.62 us (2%)
  local copies, waits for them, and re-layouts  3.08 us (2%)
    ppermute x27, waiting for transfers between devices, shift(): return lax.ppermute(array, AXES, pairs)  82.5 us
    ppermute x27, starting transfers between devices, shift(): return lax.ppermute(array, AXES, pairs)  45.4 us
    pallas_call x2, Pallas kernels, contract(): pl.pallas_call(contract_kernel, grid=(ab // tile,), in_specs=[pl.BlockSpe...  34.7 us
    pallas_call x2, Pallas kernels, select(): pl.pallas_call(functools.partial(select_kernel, n), grid=(2,), in_specs=[...  15.6 us
  transfers between devices with their start and end apart: 27, of which 15 were waited for; matrix products, arithmetic and copies ran while one was open for 2% of the time, Pallas kernels for 14%

profile of v1, /device:TPU:0, one launch (start us, length us, event | category | flops | bytes accessed | tf_op | source)
XLA Modules:
  0.0 185.1 jit_solution(13931269857050622169)
XLA Ops:
  0.0 1.3 fusion.7
  1.3 2.1 %collective-permute-start.10 = (f32[1024,128]{1,0:T(8,128)S(1)}, f32[1024,128]{1,0:T(8,128)S(1)}, u32[]{:S(2)}, u32[]{:S(2)}) collective-permute-start(f32[1024,128]{1,0:T(8,128)S(1)} %get-tuple-element.36.refs_0_), channel_id=1, source_target_pairs={{0,16},{1,17},{16,32},{17,33},{32,48},{33,49},{48,0},{49,1},{2,18}... | collective-permute-start | bytes 1572872 | tf_op jit(solution)/shard_map/ppermute | solution.py:29
  3.4 2.2 %collective-permute-start.8 = (f32[1024,128]{1,0:T(8,128)S(1)}, f32[1024,128]{1,0:T(8,128)S(1)}, u32[]{:S(2)}, u32[]{:S(2)}) collective-permute-start(f32[1024,128]{1,0:T(8,128)S(1)} %get-tuple-element.36.refs_0_), channel_id=1, source_target_pairs={{0,48},{1,49},{16,0},{17,1},{32,16},{33,17},{48,32},{49,33},{2,50}... | collective-permute-start | bytes 1572872 | tf_op jit(solution)/shard_map/ppermute | solution.py:29
  5.6 3.2 %collective-permute-start.3 = (f32[1024,128]{1,0:T(8,128)S(1)}, f32[1024,128]{1,0:T(8,128)S(1)}, u32[]{:S(2)}, u32[]{:S(2)}) collective-permute-start(f32[1024,128]{1,0:T(8,128)S(1)} %get-tuple-element.37.refs_0_), channel_id=1, source_target_pairs={{0,64},{1,65},{16,80},{17,81},{32,96},{33,97},{48,112},{49,113},{2... | collective-permute-start | bytes 1572872 | tf_op jit(solution)/shard_map/ppermute | solution.py:29
  9.1 11.4 %collective-permute-done.3.refs_4_ = f32[1024,128]{1,0:T(8,128)S(1)} collective-permute-done((f32[1024,128]{1,0:T(8,128)S(1)}, f32[1024,128]{1,0:T(8,128)S(1)}, u32[]{:S(2)}, u32[]{:S(2)}) %collective-permute-start.3) | collective-permute-done | bytes 524320 | tf_op jit(solution)/shard_map/ppermute | solution.py:29
  20.7 3.3 %collective-permute-start.4 = (f32[1024,128]{1,0:T(8,128)S(1)}, f32[1024,128]{1,0:T(8,128)S(1)}, u32[]{:S(2)}, u32[]{:S(2)}) collective-permute-start(f32[1024,128]{1,0:T(8,128)S(1)} %collective-permute-done.3.refs_4_), channel_id=1, source_target_pairs={{0,48},{1,49},{16,0},{17,1},{32,16},{33,17},{48,32},{49,33},{2,50}... | collective-permute-start | bytes 1572872 | tf_op jit(solution)/shard_map/ppermute | solution.py:29
  24.0 0.5 collective-permute-start.9
  24.4 5.2 %collective-permute-done.1.refs_3_ = f32[1024,128]{1,0:T(8,128)} collective-permute-done((f32[1024,128]{1,0:T(8,128)S(1)}, f32[1024,128]{1,0:T(8,128)}, u32[]{:S(2)}, u32[]{:S(2)}) %collective-permute-start.1) | collective-permute-done | bytes 524320 | tf_op jit(solution)/shard_map/ppermute | solution.py:29
  29.6 2.1 %collective-permute-start = (f32[1024,128]{1,0:T(8,128)S(1)}, f32[1024,128]{1,0:T(8,128)S(1)}, u32[]{:S(2)}, u32[]{:S(2)}) collective-permute-start(f32[1024,128]{1,0:T(8,128)S(1)} %get-tuple-element.37.refs_0_), channel_id=1, source_target_pairs={{0,48},{1,49},{16,0},{17,1},{32,16},{33,17},{48,32},{49,33},{2,50}... | collective-permute-start | bytes 1572872 | tf_op jit(solution)/shard_map/ppermute | solution.py:29
  31.6 8.2 %collective-permute-done.5.refs_6_ = f32[1024,128]{1,0:T(8,128)S(1)} collective-permute-done((f32[1024,128]{1,0:T(8,128)S(1)}, f32[1024,128]{1,0:T(8,128)S(1)}, u32[]{:S(2)}, u32[]{:S(2)}) %collective-permute-start.5) | collective-permute-done | bytes 524320 | tf_op jit(solution)/shard_map/ppermute | solution.py:29
  40.0 1.6 collective-permute-start.6
  41.6 1.8 collective-permute-start.7
  43.4 4.2 %collective-permute-done.9.refs_2_ = f32[1024,128]{1,0:T(8,128)S(1)} collective-permute-done((f32[1024,128]{1,0:T(8,128)S(1)}, f32[1024,128]{1,0:T(8,128)S(1)}, u32[]{:S(2)}, u32[]{:S(2)}) %collective-permute-start.9) | collective-permute-done | bytes 524320 | tf_op jit(solution)/shard_map/ppermute | solution.py:29
  47.6 3.2 %collective-permute-start.14 = (f32[1024,128]{1,0:T(8,128)S(1)}, f32[1024,128]{1,0:T(8,128)S(1)}, u32[]{:S(2)}, u32[]{:S(2)}) collective-permute-start(f32[1024,128]{1,0:T(8,128)S(1)} %collective-permute-done.9.refs_2_), channel_id=1, source_target_pairs={{0,64},{1,65},{16,80},{17,81},{32,96},{33,97},{48,112},{49,113},{2... | collective-permute-start | bytes 1572872 | tf_op jit(solution)/shard_map/ppermute | solution.py:29
  50.8 1.7 compare_convert_fusion.choose_ref
  52.5 6.3 %collective-permute-done.refs_1_ = f32[1024,128]{1,0:T(8,128)S(1)} collective-permute-done((f32[1024,128]{1,0:T(8,128)S(1)}, f32[1024,128]{1,0:T(8,128)S(1)}, u32[]{:S(2)}, u32[]{:S(2)}) %collective-permute-start) | collective-permute-done | bytes 524320 | tf_op jit(solution)/shard_map/ppermute | solution.py:29
  58.8 3.2 %collective-permute-start.11 = (f32[1024,128]{1,0:T(8,128)S(1)}, f32[1024,128]{1,0:T(8,128)S(1)}, u32[]{:S(2)}, u32[]{:S(2)}) collective-permute-start(f32[1024,128]{1,0:T(8,128)S(1)} %get-tuple-element.36.refs_0_), channel_id=1, source_target_pairs={{0,64},{1,65},{16,80},{17,81},{32,96},{33,97},{48,112},{49,113},{2... | collective-permute-start | bytes 1572872 | tf_op jit(solution)/shard_map/ppermute | solution.py:29
  62.0 0.3 collective-permute-start.12
  62.3 3.2 %collective-permute-start.13 = (f32[1024,128]{1,0:T(8,128)S(1)}, f32[1024,128]{1,0:T(8,128)S(1)}, u32[]{:S(2)}, u32[]{:S(2)}) collective-permute-start(f32[1024,128]{1,0:T(8,128)S(1)} %collective-permute-done.10.refs_3_), channel_id=1, source_target_pairs={{0,64},{1,65},{16,80},{17,81},{32,96},{33,97},{48,112},{49,113},{2... | collective-permute-start | bytes 1572872 | tf_op jit(solution)/shard_map/ppermute | solution.py:29
  65.5 7.8 %select.20 = (bf16[512,1024]{1,0:T(8,128)(2,1)S(1)}, bf16[512,1024]{1,0:T(8,128)(2,1)}, bf16[512,1024]{1,0:T(8,128)(2,1)}, bf16[512,1024]{1,0:T(8,128)(2,1)}) custom-call(bf16[1024,1024]{1,0:T(8,128)(2,1)} %compare_convert_fusion.choose_ref, f32[1024,128]{1,0:T(8,128)S(1)} %get-tuple-element.37.refs_0_, f32[1024,128]{1,0:T(8,128)S(1)} %collective-permute-done.refs_1_, ...), custom_call_target="tpu_custom_call" | custom-call | flops 4294967296 | bytes 8388608 | tf_op jit(solution)/shard_map/select/pallas_call | solution.py:66
  73.3 1.8 collective-permute-done.11.refs_4_
  75.2 16.8 %collective-permute-done.13.refs_6_ = f32[1024,128]{1,0:T(8,128)S(1)} collective-permute-done((f32[1024,128]{1,0:T(8,128)S(1)}, f32[1024,128]{1,0:T(8,128)S(1)}, u32[]{:S(2)}, u32[]{:S(2)}) %collective-permute-start.13) | collective-permute-done | bytes 524320 | tf_op jit(solution)/shard_map/ppermute | solution.py:29
  92.0 7.8 %select.21 = (bf16[512,1024]{1,0:T(8,128)(2,1)S(1)}, bf16[512,1024]{1,0:T(8,128)(2,1)}, bf16[512,1024]{1,0:T(8,128)(2,1)}, bf16[512,1024]{1,0:T(8,128)(2,1)}) custom-call(bf16[1024,1024]{1,0:T(8,128)(2,1)} %compare_convert_fusion.choose_ref, f32[1024,128]{1,0:T(8,128)S(1)} %get-tuple-element.36.refs_0_, f32[1024,128]{1,0:T(8,128)S(1)} %collective-permute-done.8.refs_1_, ...), custom_call_target="tpu_custom_call" | custom-call | flops 4294967296 | bytes 8388608 | tf_op jit(solution)/shard_map/select/pallas_call | solution.py:66
  99.8 1.2 copy-done.5
  101.0 17.3 %contract.2 = (f32[256,2048]{1,0:T(8,128)}, f32[256,2048]{1,0:T(8,128)}) custom-call(f32[2048,2048]{1,0:T(8,128)} %v_ref.3, bf16[512,1024]{1,0:T(8,128)(2,1)S(1)} %get-tuple-element.17.ha_ref, bf16[512,1024]{1,0:T(8,128)(2,1)S(1)} %copy-done.2, bf16[512,1024]{1,0:T(8,128)(2,1)S(1)} %get-tuple-element.19.hb_ref, bf16[512,1024]{1,0:T(8,128)(2,1)S(1)} %copy-done.5), custom_call_target="tpu_custom_call" | custom-call | flops 12884901888 | bytes 25165824 | tf_op jit(solution)/shard_map/contract/pallas_call | solution.py:98
  118.4 17.4 %contract.3 = (f32[256,2048]{1,0:T(8,128)}, f32[256,2048]{1,0:T(8,128)}) custom-call(f32[2048,2048]{1,0:T(8,128)} %v_ref.3, bf16[512,1024]{1,0:T(8,128)(2,1)S(1)} %copy-done, bf16[512,1024]{1,0:T(8,128)(2,1)S(1)} %copy-done.1, bf16[512,1024]{1,0:T(8,128)(2,1)S(1)} %copy-done.3, bf16[512,1024]{1,0:T(8,128)(2,1)S(1)} %copy-done.4), custom_call_target="tpu_custom_call" | custom-call | flops 12884901888 | bytes 25165824 | tf_op jit(solution)/shard_map/contract/pallas_call | solution.py:98
  135.8 0.5 collective-permute-start.21
  136.3 0.2 slice_add_fusion.4
  136.5 2.8 %collective-permute-start.18 = (f32[32,2048]{1,0:T(8,128)S(1)}, f32[32,2048]{1,0:T(8,128)S(1)}, u32[]{:S(2)}, u32[]{:S(2)}) collective-permute-start(f32[32,2048]{1,0:T(8,128)S(1)} %get-tuple-element.41), channel_id=1, source_target_pairs={{0,12},{1,13},{16,28},{17,29},{32,44},{33,45},{48,60},{49,61},{2,1... | collective-permute-start | bytes 786440 | tf_op jit(solution)/shard_map/ppermute | solution.py:29
  139.3 0.9 collective-permute-done.21
  140.4 1.7 collective-permute-start.22
  142.0 1.5 collective-permute-start.16
  143.5 1.5 collective-permute-done.18
  145.2 3.8 %collective-permute-start.19 = (f32[64,2048]{1,0:T(8,128)S(1)}, f32[64,2048]{1,0:T(8,128)S(1)}, u32[]{:S(2)}, u32[]{:S(2)}) collective-permute-start(f32[64,2048]{1,0:T(8,128)S(1)} %pad_maximum_fusion.1), channel_id=1, source_target_pairs={{0,12},{1,13},{16,28},{17,29},{32,44},{33,45},{48,60},{49,61},{2,1... | collective-permute-start | bytes 1572872 | tf_op jit(solution)/shard_map/ppermute | solution.py:29
  148.9 2.6 %collective-permute-done.16 = f32[32,2048]{1,0:T(8,128)S(1)} collective-permute-done((f32[32,2048]{1,0:T(8,128)S(1)}, f32[32,2048]{1,0:T(8,128)S(1)}, u32[]{:S(2)}, u32[]{:S(2)}) %collective-permute-start.16) | collective-permute-done | bytes 262176 | tf_op jit(solution)/shard_map/ppermute | solution.py:29
  151.6 0.3 collective-permute-start.17
  152.0 13.9 %collective-permute-done.22 = f32[128,2048]{1,0:T(8,128)S(1)} collective-permute-done((f32[128,2048]{1,0:T(8,128)S(1)}, f32[128,2048]{1,0:T(8,128)S(1)}, u32[]{:S(2)}, u32[]{:S(2)}) %collective-permute-start.22) | collective-permute-done | bytes 1048608 | tf_op jit(solution)/shard_map/ppermute | solution.py:29
  165.9 0.2 fusion
  166.1 1.6 collective-permute-start.23
  167.9 1.7 collective-permute-start.20
  169.5 2.9 %collective-permute-done.23 = f32[16,2048]{1,0:T(8,128)S(1)} collective-permute-done((f32[16,2048]{1,0:T(8,128)S(1)}, f32[16,2048]{1,0:T(8,128)S(1)}, u32[]{:S(2)}, u32[]{:S(2)}) %collective-permute-start.23) | collective-permute-done | bytes 131104 | tf_op jit(solution)/shard_map/ppermute | solution.py:29
  172.4 1.6 collective-permute-start.25
  174.1 0.5 collective-permute-start.24
  174.6 2.9 %collective-permute-done.25 = f32[16,2048]{1,0:T(8,128)S(1)} collective-permute-done((f32[16,2048]{1,0:T(8,128)S(1)}, f32[16,2048]{1,0:T(8,128)S(1)}, u32[]{:S(2)}, u32[]{:S(2)}) %collective-permute-start.25) | collective-permute-done | bytes 131104 | tf_op jit(solution)/shard_map/ppermute | solution.py:29
  177.5 2.8 %collective-permute-start.26 = (f32[32,2048]{1,0:T(8,128)S(1)}, f32[32,2048]{1,0:T(8,128)S(1)}, u32[]{:S(2)}, u32[]{:S(2)}) collective-permute-start(f32[32,2048]{1,0:T(8,128)S(1)} %pad_maximum_fusion.4), channel_id=1, source_target_pairs={{0,12},{1,13},{16,28},{17,29},{32,44},{33,45},{48,60},{49,61},{2,1... | collective-permute-start | bytes 786440 | tf_op jit(solution)/shard_map/ppermute | solution.py:29
  180.4 1.3 collective-permute-done.24
  181.7 2.5 %collective-permute-done.26 = f32[32,2048]{1,0:T(8,128)S(1)} collective-permute-done((f32[32,2048]{1,0:T(8,128)S(1)}, f32[32,2048]{1,0:T(8,128)S(1)}, u32[]{:S(2)}, u32[]{:S(2)}) %collective-permute-start.26) | collective-permute-done | bytes 262176 | tf_op jit(solution)/shard_map/ppermute | solution.py:29
  184.3 0.8 pad_maximum_fusion.2
  (72 shorter events, 1.3 us)
Async XLA Ops:
  0.0 8.8 %copy-start.8 = (s32[1024]{0:T(1024)S(1)}, s32[1024]{0:T(1024)}, u32[]{:S(2)}) copy-start(s32[1024]{0:T(1024)} %param.7) | copy-start | bytes 12292
  0.0 8.9 %copy-start.9 = (s32[1024]{0:T(1024)S(1)}, s32[1024]{0:T(1024)}, u32[]{:S(2)}) copy-start(s32[1024]{0:T(1024)} %param.6) | copy-start | bytes 12292
  1.3 40.3 %collective-permute-start.10 = (f32[1024,128]{1,0:T(8,128)S(1)}, f32[1024,128]{1,0:T(8,128)S(1)}, u32[]{:S(2)}, u32[]{:S(2)}) collective-permute-start(f32[1024,128]{1,0:T(8,128)S(1)} %get-tuple-element.36.refs_0_), channel_id=1, source_target_pairs={{0,16},{1,17},{16,32},{17,33},{32,48},{33,49},{48,0},{49,1},{2,18}... | collective-permute-start | bytes 1572872 | tf_op jit(solution)/shard_map/ppermute | solution.py:29
  3.4 20.6 %collective-permute-start.8 = (f32[1024,128]{1,0:T(8,128)S(1)}, f32[1024,128]{1,0:T(8,128)S(1)}, u32[]{:S(2)}, u32[]{:S(2)}) collective-permute-start(f32[1024,128]{1,0:T(8,128)S(1)} %get-tuple-element.36.refs_0_), channel_id=1, source_target_pairs={{0,48},{1,49},{16,0},{17,1},{32,16},{33,17},{48,32},{49,33},{2,50}... | collective-permute-start | bytes 1572872 | tf_op jit(solution)/shard_map/ppermute | solution.py:29
  5.6 14.9 %collective-permute-start.3 = (f32[1024,128]{1,0:T(8,128)S(1)}, f32[1024,128]{1,0:T(8,128)S(1)}, u32[]{:S(2)}, u32[]{:S(2)}) collective-permute-start(f32[1024,128]{1,0:T(8,128)S(1)} %get-tuple-element.37.refs_0_), channel_id=1, source_target_pairs={{0,64},{1,65},{16,80},{17,81},{32,96},{33,97},{48,112},{49,113},{2... | collective-permute-start | bytes 1572872 | tf_op jit(solution)/shard_map/ppermute | solution.py:29
  8.8 20.8 %collective-permute-start.1 = (f32[1024,128]{1,0:T(8,128)S(1)}, f32[1024,128]{1,0:T(8,128)}, u32[]{:S(2)}, u32[]{:S(2)}) collective-permute-start(f32[1024,128]{1,0:T(8,128)S(1)} %get-tuple-element.37.refs_0_), channel_id=1, source_target_pairs={{0,16},{1,17},{16,32},{17,33},{32,48},{33,49},{48,0},{49,1},{2,18}... | collective-permute-start | bytes 1572872 | tf_op jit(solution)/shard_map/ppermute | solution.py:29
  20.5 19.4 %collective-permute-start.5 = (f32[1024,128]{1,0:T(8,128)S(1)}, f32[1024,128]{1,0:T(8,128)S(1)}, u32[]{:S(2)}, u32[]{:S(2)}) collective-permute-start(f32[1024,128]{1,0:T(8,128)S(1)} %collective-permute-done.3.refs_4_), channel_id=1, source_target_pairs={{0,16},{1,17},{16,32},{17,33},{32,48},{33,49},{48,0},{49,1},{2,18}... | collective-permute-start | bytes 1572872 | tf_op jit(solution)/shard_map/ppermute | solution.py:29
  20.7 19.3 %collective-permute-start.4 = (f32[1024,128]{1,0:T(8,128)S(1)}, f32[1024,128]{1,0:T(8,128)S(1)}, u32[]{:S(2)}, u32[]{:S(2)}) collective-permute-start(f32[1024,128]{1,0:T(8,128)S(1)} %collective-permute-done.3.refs_4_), channel_id=1, source_target_pairs={{0,48},{1,49},{16,0},{17,1},{32,16},{33,17},{48,32},{49,33},{2,50}... | collective-permute-start | bytes 1572872 | tf_op jit(solution)/shard_map/ppermute | solution.py:29
  24.0 23.6 %collective-permute-start.9 = (f32[1024,128]{1,0:T(8,128)S(1)}, f32[1024,128]{1,0:T(8,128)S(1)}, u32[]{:S(2)}, u32[]{:S(2)}) collective-permute-start(f32[1024,128]{1,0:T(8,128)S(1)} %collective-permute-done.8.refs_1_), channel_id=1, source_target_pairs={{0,48},{1,49},{16,0},{17,1},{32,16},{33,17},{48,32},{49,33},{2,50}... | collective-permute-start | bytes 1572872 | tf_op jit(solution)/shard_map/ppermute | solution.py:29
  29.6 29.2 %collective-permute-start = (f32[1024,128]{1,0:T(8,128)S(1)}, f32[1024,128]{1,0:T(8,128)S(1)}, u32[]{:S(2)}, u32[]{:S(2)}) collective-permute-start(f32[1024,128]{1,0:T(8,128)S(1)} %get-tuple-element.37.refs_0_), channel_id=1, source_target_pairs={{0,48},{1,49},{16,0},{17,1},{32,16},{33,17},{48,32},{49,33},{2,50}... | collective-permute-start | bytes 1572872 | tf_op jit(solution)/shard_map/ppermute | solution.py:29
  39.9 22.1 %collective-permute-start.2 = (f32[1024,128]{1,0:T(8,128)}, f32[1024,128]{1,0:T(8,128)S(1)}, u32[]{:S(2)}, u32[]{:S(2)}) collective-permute-start(f32[1024,128]{1,0:T(8,128)} %collective-permute-done.1.refs_3_), channel_id=1, source_target_pairs={{0,16},{1,17},{16,32},{17,33},{32,48},{33,49},{48,0},{49,1},{2,18}... | collective-permute-start | bytes 1572872 | tf_op jit(solution)/shard_map/ppermute | solution.py:29
  40.0 22.4 %collective-permute-start.6 = (f32[512,128]{1,0:T(8,128)S(1)}, f32[512,128]{1,0:T(8,128)S(1)}, u32[]{:S(2)}, u32[]{:S(2)}) collective-permute-start(f32[512,128]{1,0:T(8,128)S(1)} %slice.176), channel_id=1, source_target_pairs={{0,16},{1,17},{16,32},{17,33},{32,48},{33,49},{48,0},{49,1},{2,18}... | collective-permute-start | bytes 786440 | tf_op jit(solution)/shard_map/ppermute | solution.py:29
  41.6 24.0 %collective-permute-start.7 = (f32[512,128]{1,0:T(8,128)S(1)}, f32[512,128]{1,0:T(8,128)S(1)}, u32[]{:S(2)}, u32[]{:S(2)}) collective-permute-start(f32[512,128]{1,0:T(8,128)S(1)} %slice.177), channel_id=1, source_target_pairs={{0,48},{1,49},{16,0},{17,1},{32,16},{33,17},{48,32},{49,33},{2,50}... | collective-permute-start | bytes 786440 | tf_op jit(solution)/shard_map/ppermute | solution.py:29
  47.6 25.7 %collective-permute-start.14 = (f32[1024,128]{1,0:T(8,128)S(1)}, f32[1024,128]{1,0:T(8,128)S(1)}, u32[]{:S(2)}, u32[]{:S(2)}) collective-permute-start(f32[1024,128]{1,0:T(8,128)S(1)} %collective-permute-done.9.refs_2_), channel_id=1, source_target_pairs={{0,64},{1,65},{16,80},{17,81},{32,96},{33,97},{48,112},{49,113},{2... | collective-permute-start | bytes 1572872 | tf_op jit(solution)/shard_map/ppermute | solution.py:29
  58.8 16.4 %collective-permute-start.11 = (f32[1024,128]{1,0:T(8,128)S(1)}, f32[1024,128]{1,0:T(8,128)S(1)}, u32[]{:S(2)}, u32[]{:S(2)}) collective-permute-start(f32[1024,128]{1,0:T(8,128)S(1)} %get-tuple-element.36.refs_0_), channel_id=1, source_target_pairs={{0,64},{1,65},{16,80},{17,81},{32,96},{33,97},{48,112},{49,113},{2... | collective-permute-start | bytes 1572872 | tf_op jit(solution)/shard_map/ppermute | solution.py:29
  62.0 30.0 %collective-permute-start.12 = (f32[1024,128]{1,0:T(8,128)S(1)}, f32[1024,128]{1,0:T(8,128)S(1)}, u32[]{:S(2)}, u32[]{:S(2)}) collective-permute-start(f32[1024,128]{1,0:T(8,128)S(1)} %collective-permute-done.8.refs_1_), channel_id=1, source_target_pairs={{0,64},{1,65},{16,80},{17,81},{32,96},{33,97},{48,112},{49,113},{2... | collective-permute-start | bytes 1572872 | tf_op jit(solution)/shard_map/ppermute | solution.py:29
  62.3 29.6 %collective-permute-start.13 = (f32[1024,128]{1,0:T(8,128)S(1)}, f32[1024,128]{1,0:T(8,128)S(1)}, u32[]{:S(2)}, u32[]{:S(2)}) collective-permute-start(f32[1024,128]{1,0:T(8,128)S(1)} %collective-permute-done.10.refs_3_), channel_id=1, source_target_pairs={{0,64},{1,65},{16,80},{17,81},{32,96},{33,97},{48,112},{49,113},{2... | collective-permute-start | bytes 1572872 | tf_op jit(solution)/shard_map/ppermute | solution.py:29
  92.0 7.8 %copy-start.2 = (bf16[512,1024]{1,0:T(8,128)(2,1)S(1)}, bf16[512,1024]{1,0:T(8,128)(2,1)}, u32[]{:S(2)}) copy-start(bf16[512,1024]{1,0:T(8,128)(2,1)} %get-tuple-element.18.la_ref) | copy-start | bytes 3145732
  99.8 1.2 copy-start.5
  101.0 17.3 %copy-start = (bf16[512,1024]{1,0:T(8,128)(2,1)S(1)}, bf16[512,1024]{1,0:T(8,128)(2,1)}, u32[]{:S(2)}) copy-start(bf16[512,1024]{1,0:T(8,128)(2,1)} %get-tuple-element.23.ha_ref) | copy-start | bytes 3145732
  101.0 17.3 %copy-start.1 = (bf16[512,1024]{1,0:T(8,128)(2,1)S(1)}, bf16[512,1024]{1,0:T(8,128)(2,1)}, u32[]{:S(2)}) copy-start(bf16[512,1024]{1,0:T(8,128)(2,1)} %get-tuple-element.24.la_ref) | copy-start | bytes 3145732
  101.0 17.4 %copy-start.3 = (bf16[512,1024]{1,0:T(8,128)(2,1)S(1)}, bf16[512,1024]{1,0:T(8,128)(2,1)}, u32[]{:S(2)}) copy-start(bf16[512,1024]{1,0:T(8,128)(2,1)} %get-tuple-element.25.hb_ref) | copy-start | bytes 3145732
  101.0 17.4 %copy-start.4 = (bf16[512,1024]{1,0:T(8,128)(2,1)S(1)}, bf16[512,1024]{1,0:T(8,128)(2,1)}, u32[]{:S(2)}) copy-start(bf16[512,1024]{1,0:T(8,128)(2,1)} %get-tuple-element.26.lb_ref) | copy-start | bytes 3145732
  118.3 17.9 %collective-permute-start.15 = (f32[256,2048]{1,0:T(8,128)}, f32[256,2048]{1,0:T(8,128)S(1)}, u32[]{:S(2)}, u32[]{:S(2)}) collective-permute-start(f32[256,2048]{1,0:T(8,128)} %get-tuple-element.22), channel_id=1, source_target_pairs={{0,1},{1,0},{16,17},{17,16},{32,33},{33,32},{48,49},{49,48},{2,3},... | collective-permute-start | bytes 6291464 | tf_op jit(solution)/shard_map/ppermute | solution.py:29
  118.4 17.9 %copy-start.6 = (f32[256,2048]{1,0:T(8,128)S(1)}, f32[256,2048]{1,0:T(8,128)}, u32[]{:S(2)}) copy-start(f32[256,2048]{1,0:T(8,128)} %get-tuple-element.21) | copy-start | bytes 6291460
  135.8 4.5 %collective-permute-start.21 = (f32[256,2048]{1,0:T(8,128)}, f32[256,2048]{1,0:T(8,128)S(1)}, u32[]{:S(2)}, u32[]{:S(2)}) collective-permute-start(f32[256,2048]{1,0:T(8,128)} %get-tuple-element.28), channel_id=1, source_target_pairs={{0,1},{1,0},{16,17},{17,16},{32,33},{33,32},{48,49},{49,48},{2,3},... | collective-permute-start | bytes 6291464 | tf_op jit(solution)/shard_map/ppermute | solution.py:29
  136.3 4.0 %copy-start.7 = (f32[256,2048]{1,0:T(8,128)S(1)}, f32[256,2048]{1,0:T(8,128)}, u32[]{:S(2)}) copy-start(f32[256,2048]{1,0:T(8,128)} %get-tuple-element.27) | copy-start | bytes 6291460
  136.5 8.6 %collective-permute-start.18 = (f32[32,2048]{1,0:T(8,128)S(1)}, f32[32,2048]{1,0:T(8,128)S(1)}, u32[]{:S(2)}, u32[]{:S(2)}) collective-permute-start(f32[32,2048]{1,0:T(8,128)S(1)} %get-tuple-element.41), channel_id=1, source_target_pairs={{0,12},{1,13},{16,28},{17,29},{32,44},{33,45},{48,60},{49,61},{2,1... | collective-permute-start | bytes 786440 | tf_op jit(solution)/shard_map/ppermute | solution.py:29
  140.4 25.5 %collective-permute-start.22 = (f32[128,2048]{1,0:T(8,128)S(1)}, f32[128,2048]{1,0:T(8,128)S(1)}, u32[]{:S(2)}, u32[]{:S(2)}) collective-permute-start(f32[128,2048]{1,0:T(8,128)S(1)} %slice_add_fusion), channel_id=1, source_target_pairs={{0,2},{1,3},{16,18},{17,19},{32,34},{33,35},{48,50},{49,51},{2,0},... | collective-permute-start | bytes 3145736 | tf_op jit(solution)/shard_map/ppermute | solution.py:29
  142.0 9.5 %collective-permute-start.16 = (f32[32,2048]{1,0:T(8,128)S(1)}, f32[32,2048]{1,0:T(8,128)S(1)}, u32[]{:S(2)}, u32[]{:S(2)}) collective-permute-start(f32[32,2048]{1,0:T(8,128)S(1)} %get-tuple-element.40), channel_id=1, source_target_pairs={{0,4},{1,5},{16,20},{17,21},{32,36},{33,37},{48,52},{49,53},{2,6},... | collective-permute-start | bytes 786440 | tf_op jit(solution)/shard_map/ppermute | solution.py:29
  145.2 22.5 %collective-permute-start.19 = (f32[64,2048]{1,0:T(8,128)S(1)}, f32[64,2048]{1,0:T(8,128)S(1)}, u32[]{:S(2)}, u32[]{:S(2)}) collective-permute-start(f32[64,2048]{1,0:T(8,128)S(1)} %pad_maximum_fusion.1), channel_id=1, source_target_pairs={{0,12},{1,13},{16,28},{17,29},{32,44},{33,45},{48,60},{49,61},{2,1... | collective-permute-start | bytes 1572872 | tf_op jit(solution)/shard_map/ppermute | solution.py:29
  151.6 16.1 %collective-permute-start.17 = (f32[64,2048]{1,0:T(8,128)S(1)}, f32[64,2048]{1,0:T(8,128)S(1)}, u32[]{:S(2)}, u32[]{:S(2)}) collective-permute-start(f32[64,2048]{1,0:T(8,128)S(1)} %pad_maximum_fusion), channel_id=1, source_target_pairs={{0,4},{1,5},{16,20},{17,21},{32,36},{33,37},{48,52},{49,53},{2,6},... | collective-permute-start | bytes 1572872 | tf_op jit(solution)/shard_map/ppermute | solution.py:29
  166.1 6.2 %collective-permute-start.23 = (f32[16,2048]{1,0:T(8,128)S(1)}, f32[16,2048]{1,0:T(8,128)S(1)}, u32[]{:S(2)}, u32[]{:S(2)}) collective-permute-start(f32[16,2048]{1,0:T(8,128)S(1)} %slice.196), channel_id=1, source_target_pairs={{0,4},{1,5},{16,20},{17,21},{32,36},{33,37},{48,52},{49,53},{2,6},... | collective-permute-start | bytes 393224 | tf_op jit(solution)/shard_map/ppermute | solution.py:29
  167.9 12.5 %collective-permute-start.20 = (f32[32,2048]{1,0:T(8,128)S(1)}, f32[32,2048]{1,0:T(8,128)S(1)}, u32[]{:S(2)}, u32[]{:S(2)}) collective-permute-start(f32[32,2048]{1,0:T(8,128)S(1)} %slice.191), channel_id=1, source_target_pairs={{0,2},{1,3},{16,18},{17,19},{32,34},{33,35},{48,50},{49,51},{2,0},... | collective-permute-start | bytes 786440 | tf_op jit(solution)/shard_map/ppermute | solution.py:29
  172.4 5.0 %collective-permute-start.25 = (f32[16,2048]{1,0:T(8,128)S(1)}, f32[16,2048]{1,0:T(8,128)S(1)}, u32[]{:S(2)}, u32[]{:S(2)}) collective-permute-start(f32[16,2048]{1,0:T(8,128)S(1)} %get-tuple-element.33), channel_id=1, source_target_pairs={{0,12},{1,13},{16,28},{17,29},{32,44},{33,45},{48,60},{49,61},{2,1... | collective-permute-start | bytes 393224 | tf_op jit(solution)/shard_map/ppermute | solution.py:29
  174.1 7.7 %collective-permute-start.24 = (f32[32,2048]{1,0:T(8,128)S(1)}, f32[32,2048]{1,0:T(8,128)S(1)}, u32[]{:S(2)}, u32[]{:S(2)}) collective-permute-start(f32[32,2048]{1,0:T(8,128)S(1)} %pad_maximum_fusion.3), channel_id=1, source_target_pairs={{0,4},{1,5},{16,20},{17,21},{32,36},{33,37},{48,52},{49,53},{2,6},... | collective-permute-start | bytes 786440 | tf_op jit(solution)/shard_map/ppermute | solution.py:29
  177.5 6.7 %collective-permute-start.26 = (f32[32,2048]{1,0:T(8,128)S(1)}, f32[32,2048]{1,0:T(8,128)S(1)}, u32[]{:S(2)}, u32[]{:S(2)}) collective-permute-start(f32[32,2048]{1,0:T(8,128)S(1)} %pad_maximum_fusion.4), channel_id=1, source_target_pairs={{0,12},{1,13},{16,28},{17,29},{32,44},{33,45},{48,60},{49,61},{2,1... | collective-permute-start | bytes 786440 | tf_op jit(solution)/shard_map/ppermute | solution.py:29

commit v2 on v0

v2 whole, which is shorter than its diff:
```python
import functools

import jax
import jax.numpy as jnp
from jax import lax
from jax.experimental import pallas as pl
from jax.experimental.pallas import tpu as pltpu
from jax.sharding import PartitionSpec as P

AXES = ("row", "col")
NT = (((1,), (1,)), ((), ()))
X_ROWS = 40
MIB = 1 << 20
WHOLE = pl.BlockSpec(memory_space=pltpu.VMEM)


def device_index(x, y, z, core):
    return ((y // 2) * 4 + z) * 16 + (x * 2 + y % 2) * 2 + core


def shift(array, dx=0, dy=0, dz=0, flip_y=False, flip_core=False):
    pairs = []
    for x in range(4):
        for y in range(4):
            for z in range(4):
                for core in range(2):
                    to_y = y ^ 1 if flip_y else (y + dy) % 4
                    to = device_index((x + dx) % 4, to_y, (z + dz) % 4, core ^ int(flip_core))
                    pairs.append((device_index(x, y, z, core), to))
    return lax.ppermute(array, AXES, pairs)


def place():
    row, col = lax.axis_index("row"), lax.axis_index("col")
    return col // 4, (col // 2) % 2, col % 2, row // 4, row % 4


def rolled(array, start):
    sizes = array.shape
    return lax.dynamic_slice(jnp.concatenate([array, array]), (start,) + (0,) * (array.ndim - 1), sizes)


def flipped(array, bit, axis):
    return jnp.where(bit == 0, array, jnp.flip(array, axis))


def parts_of(array):
    high = array.astype(jnp.bfloat16)
    return high, (array - high.astype(jnp.float32)).astype(jnp.bfloat16)


def stack_columns(layout, blocks, both):
    width = both.shape[1] // 2
    for at, start, size, row, col in layout:
        high, low = parts_of(blocks[at][start : start + size, :])
        both[row : row + size, col : col + 128] = high
        both[row : row + size, width + col : width + col + 128] = low


def product(vh, vl, both):
    width = both.shape[1] // 2
    dot = functools.partial(jnp.dot, preferred_element_type=jnp.float32)
    if width == 128:
        pair = dot(vh, both[...])
        return pair[:, :width] + pair[:, width:] + dot(vl, both[:, :width])
    return dot(vh, both[:, :width]) + dot(vh, both[:, width:]) + dot(vl, both[:, :width])


def first_kernel(layout, tile, v_ref, a_ref, out_h, out_l, vh_ref, vl_ref, both):
    stack_columns(layout, [a_ref], both)

    @pl.loop(0, v_ref.shape[0] // tile)
    def _(i):
        rows = pl.ds(pl.multiple_of(i * tile, tile), tile)
        vh, vl = parts_of(v_ref[rows, :])
        vh_ref[rows, :], vl_ref[rows, :] = vh, vl
        out_h[rows, :], out_l[rows, :] = parts_of(product(vh, vl, both))


def contract_kernel(layout, n, tile, vh_ref, vl_ref, *refs):
    blocks, (out_h, out_l, _, _, both) = refs[:n], refs[n:]
    stack_columns(layout, blocks, both)

    @pl.loop(0, out_h.shape[0] // tile)
    def _(i):
        rows = pl.ds(pl.multiple_of(i * tile, tile), tile)
        out_h[rows, :], out_l[rows, :] = parts_of(product(vh_ref[rows, :], vl_ref[rows, :], both))


def contract(v, columns, tile=1024):
    arrays, layout = [], []
    for i, stack in enumerate(columns):
        row = 0
        for array, start, size in stack:
            at = next((j for j, other in enumerate(arrays) if other is array), len(arrays))
            if at == len(arrays):
                arrays.append(array)
            layout.append((at, start, size, row, 128 * i))
            row += size
    ab, cd = v[0].shape
    width = 128 * len(columns)
    if len(v) == 1:
        kernel = functools.partial(first_kernel, layout, tile // 2)
    else:
        kernel = functools.partial(contract_kernel, layout, len(arrays), tile)
    inputs = [pltpu.with_memory_space_constraint(x, pltpu.VMEM) for x in (*v, *arrays)]
    out_h, out_l, *v = pl.pallas_call(
        kernel,
        in_specs=[WHOLE] * len(inputs),
        out_specs=[WHOLE] * 4,
        out_shape=[pltpu.VMEM((ab, width), jnp.bfloat16)] * 2 + [pltpu.VMEM((ab, cd), jnp.bfloat16)] * 2,
        input_output_aliases={} if len(v) == 1 else {0: 2, 1: 3},
        scratch_shapes=[pltpu.VMEM((cd, 2 * width), jnp.bfloat16)],
        compiler_params=pltpu.CompilerParams(vmem_limit_bytes=16 * MIB),
        cost_estimate=pl.CostEstimate(flops=6 * width * ab * cd, bytes_accessed=0, transcendentals=0),
        name="contract",
    )(*inputs)
    return [out_h, out_l], v


def order_kernel(n_products, n_got, tile, choose_ref, *refs):
    products, refs = refs[:n_products], refs[n_products:]
    got, outs = refs[:n_got], refs[n_got:]

    @pl.loop(0, products[0].shape[0] // tile)
    def _(i):
        some = pl.ds(pl.multiple_of(i * tile, tile), tile)
        total, at = None, 0
        for high, low in zip(products[::2], products[1::2], strict=True):
            chosen = choose_ref[:, at : at + high.shape[1]]
            at += high.shape[1]
            for part in (high, low):
                term = lax.dot_general(chosen, part[some, :], NT, preferred_element_type=jnp.float32)
                total = term if total is None else total + term
        for ref in got:
            total = total + ref[:, some]
        row = 0
        for ref in outs:
            ref[:, some] = total[row : row + ref.shape[0]]
            row += ref.shape[0]


def order(choose, products, got=(), n_outs=1, tile=1024):
    n, p = choose.shape
    ab = products[0].shape[0]
    inputs = [pltpu.with_memory_space_constraint(a, pltpu.VMEM) for a in (choose, *products, *got)]
    return pl.pallas_call(
        functools.partial(order_kernel, len(products), len(got), tile),
        in_specs=[WHOLE] * len(inputs),
        out_specs=[WHOLE] * n_outs,
        out_shape=[pltpu.VMEM((n // n_outs, ab), jnp.float32)] * n_outs,
        compiler_params=pltpu.CompilerParams(vmem_limit_bytes=16 * MIB),
        cost_estimate=pl.CostEstimate(flops=4 * n * ab * p, bytes_accessed=0, transcendentals=0),
        name="order",
    )(*inputs)


def gather(a):
    n, mid = a.shape[0], a.shape[0] // 2
    zp, zm = shift(a, dz=-1), shift(a, dz=1)
    y0 = shift(a, dy=2)
    y_rest = shift(jnp.concatenate([zm[mid:], zp[mid:]]), dy=2)
    up = shift(jnp.concatenate([zm[:mid], y0[:mid]]), dz=1)
    down = shift(jnp.concatenate([zp[mid:], y0[:mid]]), dz=-1)
    y_z2a, y_z2b = shift(up[mid:], dz=1), shift(y_rest[mid:], dz=-1)
    return (
        ([(a, 0, n)],),
        ([(zm, 0, n)], [(zp, 0, n)]),
        ([(y0, 0, n)],),
        ([(up, 0, mid), (down, 0, mid)], [(up, mid, mid), (y_rest, 0, mid)]),
        ([(down, mid, mid), (y_rest, mid, mid)], [(y_z2a, 0, mid), (y_z2b, 0, mid)]),
    )


def sum_x(blocks):
    return blocks[0] + shift(blocks[2], dx=2) + shift(blocks[1], dx=1) + shift(blocks[3], dx=-1)


def local(integrals, amplitudes, source_order, target_order):
    x, y_lo, core, y_hi, z = place()
    wanted = flipped(flipped(rolled(target_order.reshape(4, 2, 2, 64), x), y_lo, 1), core, 2)
    wanted_x = wanted[..., :X_ROWS].transpose(2, 0, 1, 3).reshape(-1)
    wanted_y = wanted[..., X_ROWS:].transpose(2, 1, 0, 3).reshape(-1)
    held = flipped(rolled(source_order.reshape(2, 4, 128).transpose(1, 0, 2), z), y_hi, 1)
    order_in = ((0, 0), (3, 0), (1, 0), (0, 1), (2, 0), (3, 1), (1, 1), (2, 1))
    held = jnp.concatenate([held[at] for at in order_in])
    choose_x, choose_y = ((w[:, None] == held[None, :]).astype(jnp.bfloat16) for w in (wanted_x, wanted_y))

    v, chosen = lax.optimization_barrier((integrals, (choose_x, choose_y)))
    (keep_x, send_x), (keep_y, send_y) = (jnp.split(c, 2) for c in chosen)
    v, products = [v], []
    for columns in gather(amplitudes):
        parts, v = contract(v, columns)
        products += parts

    (term_y,) = order(send_y, products)
    got_y = shift(term_y, flip_core=True)
    (term_x,) = order(send_x, products)
    got_x = shift(term_x, flip_core=True)
    y_own, y_one = order(keep_y, products, [got_y], 2)
    y_sum = y_own + shift(y_one, flip_y=True)
    x_sum = sum_x(order(keep_x, products, [got_x], 4))

    part = y_sum.shape[0] // 4
    out_y = sum_x([y_sum[part * d : part * (d + 1)] for d in range(4)])
    part = x_sum.shape[0] // 2
    out_x = x_sum[:part] + shift(x_sum[part:], flip_y=True)
    return jnp.concatenate([out_x, out_y])


def solution(mesh):
    in_specs = (P("row", "col"), P("col", "row"), P(), P())
    return jax.shard_map(local, mesh=mesh, in_specs=in_specs, out_specs=P("col", "row"), check_vma=False)
```

time: 304 us -> 142 us (0.47); the launches traced: 300 us -> 141 us
  waiting for transfers between devices: 191 us -> 54.4 us
  matrix products: 69.1 us -> 0 us
  Pallas kernels: 0 us -> 45.8 us
  starting transfers between devices: 0.04 us -> 29.8 us
  local copies, waits for them, and re-layouts: 23.8 us -> 8.52 us
  between operations: 13.4 us -> 0.32 us
    all_gather x1 -> x0, waiting for transfers between devices: 98.6 us -> none  [local(): gathered = lax.all_gather(amplitudes, 'row', axis=1, tiled=True)]
    reduce_scatter x1 -> x0, waiting for transfers between devices: 92.2 us -> none  [local(): return lax.psum_scatter(summands, 'col', scatter_dimension=0, tiled=True)]
    dot_general x1 -> x0, matrix products: 69.1 us -> none  [contract(): lax.dot_general(ordered, integrals, (((0,), (1,)), ((), ())), precision=l...]
    ppermute x0 -> x18, waiting for transfers between devices: none -> 54.4 us  [shift(): return lax.ppermute(array, AXES, pairs)]
    pallas_call x0 -> x9, Pallas kernels: none -> 45.8 us  [the longest x5 32.1 us: contract(): pl.pallas_call(kernel, in_specs=[WHOLE] * len(inputs), out_specs=[WHOLE]...]
    ppermute x0 -> x18, starting transfers between devices: none -> 29.8 us  [shift(): return lax.ppermute(array, AXES, pairs)]
    gather x2 -> x0, local copies, waits for them, and re-layouts: 16.9 us -> none  [the longest x1 12.4 us: local(): summands = contract(jnp.take(gathered, columns, axis=1), integrals)]
    unnamed x1 -> x11, local copies, waits for them, and re-layouts: 2.61 us -> 7.03 us
  transfers between devices with their start and end apart: 2 -> 18, of which waited for: 2 -> 12; matrix products, arithmetic and copies ran while one was open for 4% -> 2% of each run, Pallas kernels for 0% -> 25%
where the time goes in v2:
time: 142 us; the launch traced here: 141 us
  waiting for transfers between devices  54.4 us (38%)
  Pallas kernels  45.8 us (32%)
  starting transfers between devices  29.8 us (21%)
  local copies, waits for them, and re-layouts  8.52 us (6%)
  other arithmetic  2.63 us (2%)
    ppermute x18, waiting for transfers between devices, shift(): return lax.ppermute(array, AXES, pairs)  54.4 us
    pallas_call x5, Pallas kernels, contract(): pl.pallas_call(kernel, in_specs=[WHOLE] * len(inputs), out_specs=[WHOLE]...  32.1 us
    ppermute x18, starting transfers between devices, shift(): return lax.ppermute(array, AXES, pairs)  29.8 us
    pallas_call x4, Pallas kernels, order(): pl.pallas_call(functools.partial(order_kernel, len(products), len(got), t...  13.7 us
    unnamed x11, local copies, waits for them, and re-layouts  7.03 us
  transfers between devices with their start and end apart: 18, of which 12 were waited for; matrix products, arithmetic and copies ran while one was open for 2% of the time, Pallas kernels for 25%

profile of v2, /device:TPU:0, one launch (start us, length us, event | category | flops | bytes accessed | tf_op | source)
XLA Modules:
  0.0 141.5 jit_solution(15558098160942786935)
XLA Ops:
  0.0 2.0 %collective-permute-start = (f32[2048,128]{1,0:T(8,128)}, f32[2048,128]{1,0:T(8,128)S(1)}, u32[]{:S(2)}, u32[]{:S(2)}) collective-permute-start(f32[2048,128]{1,0:T(8,128)} %a_ref.1), channel_id=1, source_target_pairs={{0,16},{1,17},{16,32},{17,33},{32,48},{33,49},{48,0},{49,1},{2,18}... | collective-permute-start | bytes 3145736 | tf_op jit(solution)/shard_map/ppermute | solution.py:30
  2.0 3.2 %collective-permute-start.2 = (f32[2048,128]{1,0:T(8,128)}, f32[2048,128]{1,0:T(8,128)S(1)}, u32[]{:S(2)}, u32[]{:S(2)}) collective-permute-start(f32[2048,128]{1,0:T(8,128)} %a_ref.1), channel_id=1, source_target_pairs={{0,64},{1,65},{16,80},{17,81},{32,96},{33,97},{48,112},{49,113},{2... | collective-permute-start | bytes 3145736 | tf_op jit(solution)/shard_map/ppermute | solution.py:30
  5.2 2.1 %collective-permute-start.1 = (f32[2048,128]{1,0:T(8,128)}, f32[2048,128]{1,0:T(8,128)S(1)}, u32[]{:S(2)}, u32[]{:S(2)}) collective-permute-start(f32[2048,128]{1,0:T(8,128)} %a_ref.1), channel_id=1, source_target_pairs={{0,48},{1,49},{16,0},{17,1},{32,16},{33,17},{48,32},{49,33},{2,50}... | collective-permute-start | bytes 3145736 | tf_op jit(solution)/shard_map/ppermute | solution.py:30
  7.3 0.8 reshape.9
  8.2 0.8 fusion.3
  9.1 0.1 eq.45
  9.2 0.1 eq.50
  9.4 0.2 compare_convert_fusion.1
  9.6 0.3 compare_convert_fusion
  9.9 5.8 %copy-done = f32[2048,2048]{1,0:T(8,128)S(1)} copy-done((f32[2048,2048]{1,0:T(8,128)S(1)}, f32[2048,2048]{1,0:T(8,128)}, u32[]{:S(2)}) %copy-start) | copy-done | bytes 16777240
  15.6 1.2 copy-done.1
  16.8 5.4 %contract.5 = (bf16[2048,128]{1,0:T(8,128)(2,1)S(1)}, bf16[2048,128]{1,0:T(8,128)(2,1)S(1)}, bf16[2048,2048]{1,0:T(8,128)(2,1)S(1)}, bf16[2048,2048]{1,0:T(8,128)(2,1)S(1)}) custom-call(f32[2048,2048]{1,0:T(8,128)S(1)} %copy-done, f32[2048,128]{1,0:T(8,128)S(1)} %copy-done.1), custom_call_target="tpu_custom_call" | custom-call | flops 3221225472 | tf_op jit(solution)/shard_map/contract/pallas_call | solution.py:107
  22.3 6.1 %collective-permute-done.2.refs_0_ = f32[2048,128]{1,0:T(8,128)S(1)} collective-permute-done((f32[2048,128]{1,0:T(8,128)}, f32[2048,128]{1,0:T(8,128)S(1)}, u32[]{:S(2)}, u32[]{:S(2)}) %collective-permute-start.2) | collective-permute-done | bytes 1048608 | tf_op jit(solution)/shard_map/ppermute | solution.py:30
  28.5 1.5 %collective-permute-done.1.refs_1_ = f32[2048,128]{1,0:T(8,128)S(1)} collective-permute-done((f32[2048,128]{1,0:T(8,128)}, f32[2048,128]{1,0:T(8,128)S(1)}, u32[]{:S(2)}, u32[]{:S(2)}) %collective-permute-start.1) | collective-permute-done | bytes 1048608 | tf_op jit(solution)/shard_map/ppermute | solution.py:30
  30.0 0.2 pad_maximum_fusion.2
  30.2 1.8 %collective-permute-start.5 = (f32[2048,128]{1,0:T(8,128)S(1)}, f32[2048,128]{1,0:T(8,128)S(1)}, u32[]{:S(2)}, u32[]{:S(2)}) collective-permute-start(f32[2048,128]{1,0:T(8,128)S(1)} %get-tuple-element.68), channel_id=1, source_target_pairs={{0,64},{1,65},{16,80},{17,81},{32,96},{33,97},{48,112},{49,113},{2... | collective-permute-start | bytes 3145736 | tf_op jit(solution)/shard_map/ppermute | solution.py:30
  32.0 2.4 %collective-permute-start.4 = (f32[2048,128]{1,0:T(8,128)S(1)}, f32[2048,128]{1,0:T(8,128)S(1)}, u32[]{:S(2)}, u32[]{:S(2)}) collective-permute-start(f32[2048,128]{1,0:T(8,128)S(1)} %get-tuple-element.69), channel_id=1, source_target_pairs={{0,48},{1,49},{16,0},{17,1},{32,16},{33,17},{48,32},{49,33},{2,50}... | collective-permute-start | bytes 3145736 | tf_op jit(solution)/shard_map/ppermute | solution.py:30
  34.4 0.1 fusion.4
  34.5 7.2 %contract.6 = (bf16[2048,256]{1,0:T(8,128)(2,1)S(1)}, bf16[2048,256]{1,0:T(8,128)(2,1)S(1)}, bf16[2048,2048]{1,0:T(8,128)(2,1)S(1)}, bf16[2048,2048]{1,0:T(8,128)(2,1)S(1)}) custom-call(bf16[2048,2048]{1,0:T(8,128)(2,1)S(1)} %get-tuple-element.36.vh_ref, ...), custom_call_target="tpu_custom_call", output_to_operand_aliasing={{2}: (0, {}), {3}: (1, {})} | custom-call | flops 6442450944 | tf_op jit(solution)/shard_map/contract/pallas_call | solution.py:107
  41.7 4.9 %contract.7 = (bf16[2048,128]{1,0:T(8,128)(2,1)S(1)}, bf16[2048,128]{1,0:T(8,128)(2,1)S(1)}, bf16[2048,2048]{1,0:T(8,128)(2,1)S(1)}, bf16[2048,2048]{1,0:T(8,128)(2,1)S(1)}) custom-call(bf16[2048,2048]{1,0:T(8,128)(2,1)S(1)} %get-tuple-element.40.vh_ref, ...), custom_call_target="tpu_custom_call", output_to_operand_aliasing={{2}: (0, {}), {3}: (1, {})} | custom-call | flops 3221225472 | tf_op jit(solution)/shard_map/contract/pallas_call | solution.py:107
  46.6 8.8 %collective-permute-done.5.refs_2_.refs_1_ = f32[2048,128]{1,0:T(8,128)S(1)} collective-permute-done((f32[2048,128]{1,0:T(8,128)S(1)}, f32[2048,128]{1,0:T(8,128)S(1)}, u32[]{:S(2)}, u32[]{:S(2)}) %collective-permute-start.5) | collective-permute-done | bytes 1048608 | tf_op jit(solution)/shard_map/ppermute | solution.py:30
  55.4 3.6 %collective-permute-start.7 = (f32[1024,128]{1,0:T(8,128)S(1)}, f32[1024,128]{1,0:T(8,128)S(1)}, u32[]{:S(2)}, u32[]{:S(2)}) collective-permute-start(f32[1024,128]{1,0:T(8,128)S(1)} %slice.105), channel_id=1, source_target_pairs={{0,48},{1,49},{16,0},{17,1},{32,16},{33,17},{48,32},{49,33},{2,50}... | collective-permute-start | bytes 1572872 | tf_op jit(solution)/shard_map/ppermute | solution.py:30
  59.1 0.3 collective-permute-start.6
  59.4 7.2 %contract.8 = (bf16[2048,256]{1,0:T(8,128)(2,1)S(1)}, bf16[2048,256]{1,0:T(8,128)(2,1)S(1)}, bf16[2048,2048]{1,0:T(8,128)(2,1)S(1)}, bf16[2048,2048]{1,0:T(8,128)(2,1)S(1)}) custom-call(bf16[2048,2048]{1,0:T(8,128)(2,1)S(1)} %get-tuple-element.44.vh_ref, ...), custom_call_target="tpu_custom_call", output_to_operand_aliasing={{2}: (0, {}), {3}: (1, {})} | custom-call | flops 6442450944 | tf_op jit(solution)/shard_map/contract/pallas_call | solution.py:107
  66.7 1.4 %collective-permute-done.7.refs_3_ = f32[1024,128]{1,0:T(8,128)S(1)} collective-permute-done((f32[1024,128]{1,0:T(8,128)S(1)}, f32[1024,128]{1,0:T(8,128)S(1)}, u32[]{:S(2)}, u32[]{:S(2)}) %collective-permute-start.7) | collective-permute-done | bytes 524320 | tf_op jit(solution)/shard_map/ppermute | solution.py:30
  68.1 3.8 %collective-permute-done.6.refs_2_ = f32[1024,128]{1,0:T(8,128)S(1)} collective-permute-done((f32[1024,128]{1,0:T(8,128)S(1)}, f32[1024,128]{1,0:T(8,128)S(1)}, u32[]{:S(2)}, u32[]{:S(2)}) %collective-permute-start.6) | collective-permute-done | bytes 524320 | tf_op jit(solution)/shard_map/ppermute | solution.py:30
  71.9 7.3 %contract.9 = (bf16[2048,256]{1,0:T(8,128)(2,1)S(1)}, bf16[2048,256]{1,0:T(8,128)(2,1)S(1)}, bf16[2048,2048]{1,0:T(8,128)(2,1)S(1)}, bf16[2048,2048]{1,0:T(8,128)(2,1)S(1)}) custom-call(bf16[2048,2048]{1,0:T(8,128)(2,1)S(1)} %get-tuple-element.48.vh_ref, ...), custom_call_target="tpu_custom_call", output_to_operand_aliasing={{2}: (0, {}), {3}: (1, {})} | custom-call | flops 6442450944 | tf_op jit(solution)/shard_map/contract/pallas_call | solution.py:107
  79.2 3.7 %order.4 = f32[320,2048]{1,0:T(8,128)S(1)} custom-call(bf16[320,1024]{1,0:T(8,128)(2,1)S(1)} %get-tuple-element.59.choose_ref, bf16[2048,128]{1,0:T(8,128)(2,1)S(1)} %get-tuple-element.34.refs_0_, bf16[2048,128]{1,0:T(8,128)(2,1)S(1)} %get-tuple-element.35.refs_1_, bf16[2048,256]{1,0:T(8,128)(2,1)S(1)} %get-tuple-element.38.refs_2_, ...), custom_call_target="tpu_custom_call" | custom-call | flops 2684354560 | tf_op jit(solution)/shard_map/order/pallas_call | solution.py:147
  83.0 3.1 %order.6 = f32[192,2048]{1,0:T(8,128)S(1)} custom-call(bf16[192,1024]{1,0:T(8,128)(2,1)S(1)} %get-tuple-element.66.choose_ref, bf16[2048,128]{1,0:T(8,128)(2,1)S(1)} %get-tuple-element.34.refs_0_, bf16[2048,128]{1,0:T(8,128)(2,1)S(1)} %get-tuple-element.35.refs_1_, bf16[2048,256]{1,0:T(8,128)(2,1)S(1)} %get-tuple-element.38.refs_2_, ...), custom_call_target="tpu_custom_call" | custom-call | flops 1610612736 | tf_op jit(solution)/shard_map/order/pallas_call | solution.py:147
  86.2 0.6 collective-permute-start.13
  86.7 3.4 %collective-permute-done.13.refs_10_ = f32[192,2048]{1,0:T(8,128)S(1)} collective-permute-done((f32[192,2048]{1,0:T(8,128)S(1)}, f32[192,2048]{1,0:T(8,128)S(1)}, u32[]{:S(2)}, u32[]{:S(2)}) %collective-permute-start.13) | collective-permute-done | bytes 1572896 | tf_op jit(solution)/shard_map/ppermute | solution.py:30
  90.1 3.1 %order.7 = (f32[96,2048]{1,0:T(8,128)S(1)}, f32[96,2048]{1,0:T(8,128)S(1)}) custom-call(bf16[192,1024]{1,0:T(8,128)(2,1)S(1)} %get-tuple-element.67.choose_ref, bf16[2048,128]{1,0:T(8,128)(2,1)S(1)} %get-tuple-element.34.refs_0_, bf16[2048,128]{1,0:T(8,128)(2,1)S(1)} %get-tuple-element.35.refs_1_, bf16[2048,256]{1,0:T(8,128)(2,1)S(1)} %get-tuple-element.38.refs_2_, ...), custom_call_target="tpu_custom_call" | custom-call | flops 1610612736 | tf_op jit(solution)/shard_map/order/pallas_call | solution.py:147
  93.3 0.6 collective-permute-start.14
  93.9 3.7 %order.5 = (f32[80,2048]{1,0:T(8,128)S(1)}, f32[80,2048]{1,0:T(8,128)S(1)}, f32[80,2048]{1,0:T(8,128)S(1)}, f32[80,2048]{1,0:T(8,128)S(1)}) custom-call(bf16[320,1024]{1,0:T(8,128)(2,1)S(1)} %get-tuple-element.60.choose_ref, bf16[2048,128]{1,0:T(8,128)(2,1)S(1)} %get-tuple-element.34.refs_0_, bf16[2048,128]{1,0:T(8,128)(2,1)S(1)} %get-tuple-element.35.refs_1_, ...), custom_call_target="tpu_custom_call" | custom-call | flops 2684354560 | tf_op jit(solution)/shard_map/order/pallas_call | solution.py:147
  97.6 3.1 %collective-permute-start.9 = (f32[80,2048]{1,0:T(8,128)S(1)}, f32[80,2048]{1,0:T(8,128)S(1)}, u32[]{:S(2)}, u32[]{:S(2)}) collective-permute-start(f32[80,2048]{1,0:T(8,128)S(1)} %get-tuple-element.53), channel_id=1, source_target_pairs={{0,8},{1,9},{16,24},{17,25},{32,40},{33,41},{48,56},{49,57},{2,10}... | collective-permute-start | bytes 1966088 | tf_op jit(solution)/shard_map/ppermute | solution.py:30
  100.7 0.6 collective-permute-start.10
  101.3 2.6 %collective-permute-start.11 = (f32[80,2048]{1,0:T(8,128)S(1)}, f32[80,2048]{1,0:T(8,128)S(1)}, u32[]{:S(2)}, u32[]{:S(2)}) collective-permute-start(f32[80,2048]{1,0:T(8,128)S(1)} %get-tuple-element.55), channel_id=1, source_target_pairs={{0,12},{1,13},{16,28},{17,29},{32,44},{33,45},{48,60},{49,61},{2,1... | collective-permute-start | bytes 1966088 | tf_op jit(solution)/shard_map/ppermute | solution.py:30
  104.0 9.0 %collective-permute-done.14 = f32[96,2048]{1,0:T(8,128)S(1)} collective-permute-done((f32[96,2048]{1,0:T(8,128)S(1)}, f32[96,2048]{1,0:T(8,128)S(1)}, u32[]{:S(2)}, u32[]{:S(2)}) %collective-permute-start.14) | collective-permute-done | bytes 786464 | tf_op jit(solution)/shard_map/ppermute | solution.py:30
  113.1 3.1 %collective-permute-start.15 = (f32[24,2048]{1,0:T(8,128)S(1)}, f32[24,2048]{1,0:T(8,128)S(1)}, u32[]{:S(2)}, u32[]{:S(2)}) collective-permute-start(f32[24,2048]{1,0:T(8,128)S(1)} %get-tuple-element.63), channel_id=1, source_target_pairs={{0,8},{1,9},{16,24},{17,25},{32,40},{33,41},{48,56},{49,57},{2,10}... | collective-permute-start | bytes 589832 | tf_op jit(solution)/shard_map/ppermute | solution.py:30
  116.2 1.1 collective-permute-start.17
  117.3 1.1 collective-permute-start.16
  118.4 12.6 %collective-permute-done.10 = f32[80,2048]{1,0:T(8,128)S(1)} collective-permute-done((f32[80,2048]{1,0:T(8,128)S(1)}, f32[80,2048]{1,0:T(8,128)S(1)}, u32[]{:S(2)}, u32[]{:S(2)}) %collective-permute-start.10) | collective-permute-done | bytes 655392 | tf_op jit(solution)/shard_map/ppermute | solution.py:30
  131.0 0.1 add_add_fusion
  131.2 1.5 %collective-permute-start.12 = (f32[40,2048]{1,0:T(8,128)S(1)}, f32[40,2048]{1,0:T(8,128)S(1)}, u32[]{:S(2)}, u32[]{:S(2)}) collective-permute-start(f32[40,2048]{1,0:T(8,128)S(1)} %slice.107), channel_id=1, source_target_pairs={{0,2},{1,3},{16,18},{17,19},{32,34},{33,35},{48,50},{49,51},{2,0},... | collective-permute-start | bytes 983048 | tf_op jit(solution)/shard_map/ppermute | solution.py:30
  132.7 2.5 %collective-permute-done.15 = f32[24,2048]{1,0:T(8,128)S(1)} collective-permute-done((f32[24,2048]{1,0:T(8,128)S(1)}, f32[24,2048]{1,0:T(8,128)S(1)}, u32[]{:S(2)}, u32[]{:S(2)}) %collective-permute-start.15) | collective-permute-done | bytes 196640 | tf_op jit(solution)/shard_map/ppermute | solution.py:30
  135.2 3.2 %collective-permute-done.17 = f32[24,2048]{1,0:T(8,128)S(1)} collective-permute-done((f32[24,2048]{1,0:T(8,128)S(1)}, f32[24,2048]{1,0:T(8,128)S(1)}, u32[]{:S(2)}, u32[]{:S(2)}) %collective-permute-start.17) | collective-permute-done | bytes 196640 | tf_op jit(solution)/shard_map/ppermute | solution.py:30
  138.4 2.2 %collective-permute-done.12 = f32[40,2048]{1,0:T(8,128)S(1)} collective-permute-done((f32[40,2048]{1,0:T(8,128)S(1)}, f32[40,2048]{1,0:T(8,128)S(1)}, u32[]{:S(2)}, u32[]{:S(2)}) %collective-permute-start.12) | collective-permute-done | bytes 327712 | tf_op jit(solution)/shard_map/ppermute | solution.py:30
  140.7 0.8 pad_maximum_fusion.3
  (40 shorter events, 0.9 us)
Async XLA Ops:
  0.0 28.4 %collective-permute-start = (f32[2048,128]{1,0:T(8,128)}, f32[2048,128]{1,0:T(8,128)S(1)}, u32[]{:S(2)}, u32[]{:S(2)}) collective-permute-start(f32[2048,128]{1,0:T(8,128)} %a_ref.1), channel_id=1, source_target_pairs={{0,16},{1,17},{16,32},{17,33},{32,48},{33,49},{48,0},{49,1},{2,18}... | collective-permute-start | bytes 3145736 | tf_op jit(solution)/shard_map/ppermute | solution.py:30
  2.0 26.4 %collective-permute-start.2 = (f32[2048,128]{1,0:T(8,128)}, f32[2048,128]{1,0:T(8,128)S(1)}, u32[]{:S(2)}, u32[]{:S(2)}) collective-permute-start(f32[2048,128]{1,0:T(8,128)} %a_ref.1), channel_id=1, source_target_pairs={{0,64},{1,65},{16,80},{17,81},{32,96},{33,97},{48,112},{49,113},{2... | collective-permute-start | bytes 3145736 | tf_op jit(solution)/shard_map/ppermute | solution.py:30
  5.2 24.8 %collective-permute-start.1 = (f32[2048,128]{1,0:T(8,128)}, f32[2048,128]{1,0:T(8,128)S(1)}, u32[]{:S(2)}, u32[]{:S(2)}) collective-permute-start(f32[2048,128]{1,0:T(8,128)} %a_ref.1), channel_id=1, source_target_pairs={{0,48},{1,49},{16,0},{17,1},{32,16},{33,17},{48,32},{49,33},{2,50}... | collective-permute-start | bytes 3145736 | tf_op jit(solution)/shard_map/ppermute | solution.py:30
  9.8 5.8 %copy-start = (f32[2048,2048]{1,0:T(8,128)S(1)}, f32[2048,2048]{1,0:T(8,128)}, u32[]{:S(2)}) copy-start(f32[2048,2048]{1,0:T(8,128)} %v_ref) | copy-start | bytes 50331652
  15.6 1.2 copy-start.1
  30.2 25.2 %collective-permute-start.5 = (f32[2048,128]{1,0:T(8,128)S(1)}, f32[2048,128]{1,0:T(8,128)S(1)}, u32[]{:S(2)}, u32[]{:S(2)}) collective-permute-start(f32[2048,128]{1,0:T(8,128)S(1)} %get-tuple-element.68), channel_id=1, source_target_pairs={{0,64},{1,65},{16,80},{17,81},{32,96},{33,97},{48,112},{49,113},{2... | collective-permute-start | bytes 3145736 | tf_op jit(solution)/shard_map/ppermute | solution.py:30
  32.0 27.4 %collective-permute-start.4 = (f32[2048,128]{1,0:T(8,128)S(1)}, f32[2048,128]{1,0:T(8,128)S(1)}, u32[]{:S(2)}, u32[]{:S(2)}) collective-permute-start(f32[2048,128]{1,0:T(8,128)S(1)} %get-tuple-element.69), channel_id=1, source_target_pairs={{0,48},{1,49},{16,0},{17,1},{32,16},{33,17},{48,32},{49,33},{2,50}... | collective-permute-start | bytes 3145736 | tf_op jit(solution)/shard_map/ppermute | solution.py:30
  34.4 24.7 %collective-permute-start.3 = (f32[2048,128]{1,0:T(8,128)S(1)}, f32[2048,128]{1,0:T(8,128)S(1)}, u32[]{:S(2)}, u32[]{:S(2)}) collective-permute-start(f32[2048,128]{1,0:T(8,128)S(1)} %get-tuple-element.70), channel_id=1, source_target_pairs={{0,16},{1,17},{16,32},{17,33},{32,48},{33,49},{48,0},{49,1},{2,18}... | collective-permute-start | bytes 3145736 | tf_op jit(solution)/shard_map/ppermute | solution.py:30
  55.4 12.6 %collective-permute-start.7 = (f32[1024,128]{1,0:T(8,128)S(1)}, f32[1024,128]{1,0:T(8,128)S(1)}, u32[]{:S(2)}, u32[]{:S(2)}) collective-permute-start(f32[1024,128]{1,0:T(8,128)S(1)} %slice.105), channel_id=1, source_target_pairs={{0,48},{1,49},{16,0},{17,1},{32,16},{33,17},{48,32},{49,33},{2,50}... | collective-permute-start | bytes 1572872 | tf_op jit(solution)/shard_map/ppermute | solution.py:30
  59.1 12.8 %collective-permute-start.6 = (f32[1024,128]{1,0:T(8,128)S(1)}, f32[1024,128]{1,0:T(8,128)S(1)}, u32[]{:S(2)}, u32[]{:S(2)}) collective-permute-start(f32[1024,128]{1,0:T(8,128)S(1)} %slice.104), channel_id=1, source_target_pairs={{0,16},{1,17},{16,32},{17,33},{32,48},{33,49},{48,0},{49,1},{2,18}... | collective-permute-start | bytes 1572872 | tf_op jit(solution)/shard_map/ppermute | solution.py:30
  82.9 11.0 %collective-permute-start.8 = (f32[320,2048]{1,0:T(8,128)S(1)}, f32[320,2048]{1,0:T(8,128)S(1)}, u32[]{:S(2)}, u32[]{:S(2)}) collective-permute-start(f32[320,2048]{1,0:T(8,128)S(1)} %order.4), channel_id=1, source_target_pairs={{0,1},{1,0},{16,17},{17,16},{32,33},{33,32},{48,49},{49,48},{2,3},... | collective-permute-start | bytes 7864328 | tf_op jit(solution)/shard_map/ppermute | solution.py:30
  86.2 3.9 %collective-permute-start.13 = (f32[192,2048]{1,0:T(8,128)S(1)}, f32[192,2048]{1,0:T(8,128)S(1)}, u32[]{:S(2)}, u32[]{:S(2)}) collective-permute-start(f32[192,2048]{1,0:T(8,128)S(1)} %order.6), channel_id=1, source_target_pairs={{0,1},{1,0},{16,17},{17,16},{32,33},{33,32},{48,49},{49,48},{2,3},... | collective-permute-start | bytes 4718600 | tf_op jit(solution)/shard_map/ppermute | solution.py:30
  93.3 19.7 %collective-permute-start.14 = (f32[96,2048]{1,0:T(8,128)S(1)}, f32[96,2048]{1,0:T(8,128)S(1)}, u32[]{:S(2)}, u32[]{:S(2)}) collective-permute-start(f32[96,2048]{1,0:T(8,128)S(1)} %get-tuple-element.58), channel_id=1, source_target_pairs={{0,2},{1,3},{16,18},{17,19},{32,34},{33,35},{48,50},{49,51},{2,0},... | collective-permute-start | bytes 2359304 | tf_op jit(solution)/shard_map/ppermute | solution.py:30
  97.6 19.7 %collective-permute-start.9 = (f32[80,2048]{1,0:T(8,128)S(1)}, f32[80,2048]{1,0:T(8,128)S(1)}, u32[]{:S(2)}, u32[]{:S(2)}) collective-permute-start(f32[80,2048]{1,0:T(8,128)S(1)} %get-tuple-element.53), channel_id=1, source_target_pairs={{0,8},{1,9},{16,24},{17,25},{32,40},{33,41},{48,56},{49,57},{2,10}... | collective-permute-start | bytes 1966088 | tf_op jit(solution)/shard_map/ppermute | solution.py:30
  100.7 30.2 %collective-permute-start.10 = (f32[80,2048]{1,0:T(8,128)S(1)}, f32[80,2048]{1,0:T(8,128)S(1)}, u32[]{:S(2)}, u32[]{:S(2)}) collective-permute-start(f32[80,2048]{1,0:T(8,128)S(1)} %get-tuple-element.54), channel_id=1, source_target_pairs={{0,4},{1,5},{16,20},{17,21},{32,36},{33,37},{48,52},{49,53},{2,6},... | collective-permute-start | bytes 1966088 | tf_op jit(solution)/shard_map/ppermute | solution.py:30
  101.3 29.7 %collective-permute-start.11 = (f32[80,2048]{1,0:T(8,128)S(1)}, f32[80,2048]{1,0:T(8,128)S(1)}, u32[]{:S(2)}, u32[]{:S(2)}) collective-permute-start(f32[80,2048]{1,0:T(8,128)S(1)} %get-tuple-element.55), channel_id=1, source_target_pairs={{0,12},{1,13},{16,28},{17,29},{32,44},{33,45},{48,60},{49,61},{2,1... | collective-permute-start | bytes 1966088 | tf_op jit(solution)/shard_map/ppermute | solution.py:30
  113.1 22.1 %collective-permute-start.15 = (f32[24,2048]{1,0:T(8,128)S(1)}, f32[24,2048]{1,0:T(8,128)S(1)}, u32[]{:S(2)}, u32[]{:S(2)}) collective-permute-start(f32[24,2048]{1,0:T(8,128)S(1)} %get-tuple-element.63), channel_id=1, source_target_pairs={{0,8},{1,9},{16,24},{17,25},{32,40},{33,41},{48,56},{49,57},{2,10}... | collective-permute-start | bytes 589832 | tf_op jit(solution)/shard_map/ppermute | solution.py:30
  116.2 22.2 %collective-permute-start.17 = (f32[24,2048]{1,0:T(8,128)S(1)}, f32[24,2048]{1,0:T(8,128)S(1)}, u32[]{:S(2)}, u32[]{:S(2)}) collective-permute-start(f32[24,2048]{1,0:T(8,128)S(1)} %get-tuple-element.64), channel_id=1, source_target_pairs={{0,12},{1,13},{16,28},{17,29},{32,44},{33,45},{48,60},{49,61},{2,1... | collective-permute-start | bytes 589832 | tf_op jit(solution)/shard_map/ppermute | solution.py:30
  117.3 21.1 %collective-permute-start.16 = (f32[24,2048]{1,0:T(8,128)S(1)}, f32[24,2048]{1,0:T(8,128)S(1)}, u32[]{:S(2)}, u32[]{:S(2)}) collective-permute-start(f32[24,2048]{1,0:T(8,128)S(1)} %get-tuple-element.65), channel_id=1, source_target_pairs={{0,4},{1,5},{16,20},{17,21},{32,36},{33,37},{48,52},{49,53},{2,6},... | collective-permute-start | bytes 589832 | tf_op jit(solution)/shard_map/ppermute | solution.py:30
  131.2 9.4 %collective-permute-start.12 = (f32[40,2048]{1,0:T(8,128)S(1)}, f32[40,2048]{1,0:T(8,128)S(1)}, u32[]{:S(2)}, u32[]{:S(2)}) collective-permute-start(f32[40,2048]{1,0:T(8,128)S(1)} %slice.107), channel_id=1, source_target_pairs={{0,2},{1,3},{16,18},{17,19},{32,34},{33,35},{48,50},{49,51},{2,0},... | collective-permute-start | bytes 983048 | tf_op jit(solution)/shard_map/ppermute | solution.py:30

commit v3 on v0

v3 whole, which is shorter than its diff:
```python
import functools

import jax
import jax.numpy as jnp
from jax import lax
from jax.experimental import pallas as pl
from jax.experimental.pallas import tpu as pltpu
from jax.sharding import PartitionSpec as P

AXES = ("row", "col")
MIB = 1 << 20
WHOLE = pl.BlockSpec(memory_space=pltpu.VMEM)
SCALARS = pl.BlockSpec(memory_space=pltpu.SMEM)
PAIRS, LANES, HALF = 1024, 128, 1024


def device_index(x, y, z, core):
    return ((y // 2) * 4 + z) * 16 + (x * 2 + y % 2) * 2 + core


def shift(array, dx=0, dy=0, dz=0, flip_y=False, flip_core=False):
    pairs = []
    for x in range(4):
        for y in range(4):
            for z in range(4):
                for core in range(2):
                    to_y = y ^ 1 if flip_y else (y + dy) % 4
                    to = device_index((x + dx) % 4, to_y, (z + dz) % 4, core ^ int(flip_core))
                    pairs.append((device_index(x, y, z, core), to))
    return lax.ppermute(array, AXES, pairs)


def place():
    row, col = lax.axis_index("row"), lax.axis_index("col")
    return col // 4, (col // 2) % 2, col % 2, row // 4, row % 4


def rolled(array, start):
    sizes = array.shape
    return lax.dynamic_slice(jnp.concatenate([array, array]), (start,) + (0,) * (array.ndim - 1), sizes)


def flipped(array, bit, axis):
    return jnp.where(bit == 0, array, jnp.flip(array, axis))


def parts_of(array):
    high = array.astype(jnp.bfloat16)
    return high, (array - high.astype(jnp.float32)).astype(jnp.bfloat16)


def stack_columns(layout, blocks, both):
    width = both.shape[1] // 2
    for at, start, size, row, col in layout:
        high, low = parts_of(blocks[at][start : start + size, :])
        both[row : row + size, col : col + 128] = high
        both[row : row + size, width + col : width + col + 128] = low


def product(vh, vl, both):
    width = both.shape[1] // 2
    dot = functools.partial(jnp.dot, preferred_element_type=jnp.float32)
    if width == 128:
        pair = dot(vh, both[...])
        return pair[:, :width] + pair[:, width:] + dot(vl, both[:, :width])
    return dot(vh, both[:, :width]) + dot(vh, both[:, width:]) + dot(vl, both[:, :width])


def store_rows(products, first, block):
    block = block.T
    for c in range(HALF // LANES):
        products[first : first + block.shape[0], c, :] = block[:, LANES * c : LANES * (c + 1)]


def first_kernel(layout, v_hbm, a_ref, vh_ref, vl_ref, *refs):
    halves, (both, total) = refs[:-2], refs[-2:]
    stack_columns(layout, [a_ref], both)
    ab, cd = vh_ref.shape
    tile = 256

    def body(v_ref):
        rows = pl.ds(pl.multiple_of(pl.program_id(0) * tile, tile), tile)
        vh, vl = parts_of(v_ref[...])
        vh_ref[rows, :], vl_ref[rows, :] = vh, vl
        total[rows, :] = product(vh, vl, both)

    block = pl.BlockSpec((tile, cd), lambda i: (i, 0), pipeline_mode=pl.Buffered(4))
    pltpu.emit_pipeline(body, grid=(ab // tile,), in_specs=[block], out_specs=[])(v_hbm)
    for i, products in enumerate(halves):
        store_rows(products, 0, total[HALF * i : HALF * (i + 1), :])


def contract_kernel(layout, n, which, first, vh_ref, vl_ref, *refs):
    blocks, halves, both = refs[:n], refs[-1 - len(which) : -1], refs[-1]
    stack_columns(layout, blocks, both)
    for i, products in zip(which, halves, strict=True):
        rows = pl.ds(HALF * i, HALF)
        store_rows(products, first, product(vh_ref[rows, :], vl_ref[rows, :], both))


def in_vmem(arrays):
    return [pltpu.with_memory_space_constraint(a, pltpu.VMEM) for a in arrays]


def contract(v, columns, which=(0, 1), into=()):
    layout, arrays = [], []
    for i, stack in enumerate(columns):
        row = 0
        for block in stack:
            layout.append((len(arrays), 0, block.shape[0], row, 128 * i))
            arrays.append(block)
            row += block.shape[0]
    ab, cd = v[0].shape
    width = 128 * len(columns)
    n_out = into[0].shape[0] if into else width
    scratch = [pltpu.VMEM((cd, 2 * width), jnp.bfloat16)]
    fresh = len(v) == 1
    if fresh:
        kernel = functools.partial(first_kernel, layout)
        inputs = [pltpu.with_memory_space_constraint(v[0], pltpu.HBM)]
        scratch += [pltpu.VMEM((ab, width), jnp.float32)]
    else:
        kernel = functools.partial(contract_kernel, layout, len(arrays), which, n_out - width)
        inputs = in_vmem(v)
    aliases = {} if fresh else {0: 0, 1: 1}
    aliases |= {2 + len(arrays) + i: 2 + i for i in range(len(into))}
    vh, vl, *products = pl.pallas_call(
        kernel,
        in_specs=[pl.BlockSpec(memory_space=pl.ANY) if fresh else WHOLE] * len(inputs)
        + [WHOLE] * (len(arrays) + len(into)),
        out_specs=[WHOLE] * (2 + len(which)),
        out_shape=[pltpu.VMEM((ab, cd), jnp.bfloat16)] * 2
        + [pltpu.VMEM((n_out, HALF // LANES, LANES), jnp.float32)] * len(which),
        input_output_aliases=aliases,
        scratch_shapes=scratch,
        compiler_params=pltpu.CompilerParams(vmem_limit_bytes=(18 if fresh else 14) * MIB),
        cost_estimate=pl.CostEstimate(flops=6 * width * HALF * len(which) * cd, bytes_accessed=0, transcendentals=0),
        name="contract",
    )(*inputs, *in_vmem(arrays), *in_vmem(into))
    return [vh, vl], products


def merge_kernel(*refs):
    out, row = refs[-1], 0
    for ref in refs[:-1]:
        out[row : row + ref.shape[0]] = ref[...]
        row += ref.shape[0]


def merge(products):
    return pl.pallas_call(
        merge_kernel,
        in_specs=[WHOLE] * len(products),
        out_specs=WHOLE,
        out_shape=pltpu.VMEM((PAIRS, *products[0].shape[1:]), jnp.float32),
        compiler_params=pltpu.CompilerParams(vmem_limit_bytes=4 * MIB),
        cost_estimate=pl.CostEstimate(flops=0, bytes_accessed=0, transcendentals=0),
        name="merge",
    )(*in_vmem(products))


def pack_kernel(layout, *refs):
    for at, out, row, start, size in layout:
        refs[out][row : row + size, :] = refs[at][start : start + size, :]


def pack(*stacks):
    arrays = [block[0] for stack in stacks for block in stack]
    arrays = [a for i, a in enumerate(arrays) if not any(a is b for b in arrays[:i])]
    layout, shapes = [], []
    for out, stack in enumerate(stacks):
        row = 0
        for array, start, size in stack:
            at = next(i for i, a in enumerate(arrays) if a is array)
            layout.append((at, len(arrays) + out, row, start, size))
            row += size
        shapes.append(pltpu.VMEM((row, arrays[0].shape[1]), jnp.float32))
    return pl.pallas_call(
        functools.partial(pack_kernel, layout),
        in_specs=[WHOLE] * len(arrays),
        out_specs=[WHOLE] * len(stacks),
        out_shape=shapes,
        compiler_params=pltpu.CompilerParams(vmem_limit_bytes=5 * MIB),
        cost_estimate=pl.CostEstimate(flops=0, bytes_accessed=0, transcendentals=0),
        name="pack",
    )(*[pltpu.with_memory_space_constraint(a, pltpu.VMEM) for a in arrays])


def find_kernel(held_ref, wanted_ref, at_ref, inverse):
    @pl.loop(0, PAIRS, unroll=16)
    def _(p):
        inverse[held_ref[p]] = p

    @pl.loop(0, at_ref.shape[0], unroll=16)
    def _(q):
        at_ref[q] = inverse[wanted_ref[q]]


def find(held, wanted):
    return pl.pallas_call(
        find_kernel,
        in_specs=[SCALARS] * 2,
        out_specs=SCALARS,
        out_shape=jax.ShapeDtypeStruct(wanted.shape, jnp.int32),
        scratch_shapes=[pltpu.SMEM((PAIRS,), jnp.int32)],
        compiler_params=pltpu.CompilerParams(vmem_limit_bytes=MIB),
        cost_estimate=pl.CostEstimate(flops=0, bytes_accessed=0, transcendentals=0),
        name="find",
    )(held, wanted)


def order_kernel(first, n_got, at_ref, products, *refs):
    got, outs = refs[:n_got], refs[n_got:]
    row = 0
    for ref in outs:

        @pl.loop(0, ref.shape[0], unroll=8)
        def _(q, ref=ref, row=row):
            block = products[at_ref[first + row + q]]
            for term in got:
                block = block + term[row + q]
            ref[q] = block

        row += ref.shape[0]


def order(at, products, first, sizes, got=()):
    inputs = in_vmem((products, *got))
    return pl.pallas_call(
        functools.partial(order_kernel, first, len(got)),
        in_specs=[SCALARS] + [WHOLE] * len(inputs),
        out_specs=[WHOLE] * len(sizes),
        out_shape=[pltpu.VMEM((n, *products.shape[1:]), jnp.float32) for n in sizes],
        compiler_params=pltpu.CompilerParams(vmem_limit_bytes=4 * MIB),
        cost_estimate=pl.CostEstimate(flops=0, bytes_accessed=0, transcendentals=0),
        name="order",
    )(at, *inputs)


def after(value, *others):
    return lax.optimization_barrier((value, others))[0]


def products_of(v, a, held, wanted):
    mid = a.shape[0] // 2
    zm, zp, y0 = shift(a, dz=1), shift(a, dz=-1), shift(a, dy=2)
    at = find(held, wanted)
    v, own = contract([after(v, at)], ([a],))

    zm_low, zm_high, zp_high, y0_low = pack(
        *(((block, row, mid),) for block, row in ((after(zm, own), 0), (zm, mid), (zp, mid), (y0, 0)))
    )
    y_zm_high, z2_low, z2_high = shift(zm_high, dy=2), shift(zm_low, dz=1), shift(zp_high, dz=-1)
    v, near = contract(v, ([zm], [zp]))

    y_zm_low, y_zp_low = shift(after(y0_low, near), dz=1), shift(after(y0_low, near), dz=-1)
    y_zp_high = shift(after(zp_high, near, y_zm_high), dy=2)
    v, far = contract(v, ([y0], [z2_low, z2_high]))

    y_z2_low, y_z2_high = shift(after(y_zm_low, far), dz=1), shift(after(y_zp_high, far), dz=-1)
    v, beyond = contract(v, ([y_zm_low, y_zm_high], [y_zp_low, y_zp_high]))
    low, high = (merge(list(parts)) for parts in zip(own, near, far, beyond, strict=True))
    v, (low,) = contract(v, ([y_z2_low, y_z2_high],), (0,), [low])
    return low, lambda *others: contract(after(v, *others), ([y_z2_low, y_z2_high],), (1,), [high])[1][0], at


def add_rows(block, more, row):
    return lax.dynamic_update_slice_in_dim(block, block[row : row + more.shape[0]] + more, row, 0)


def ring_x(own, up, far_up, far_down, down):
    n = far_up.shape[0]
    far_up, far_down = shift(far_up, dx=1), shift(far_down, dx=-1)
    return own, shift(add_rows(up, far_up, 0), dx=1), shift(add_rows(down, far_down, n), dx=-1)


def spread_x(blocks):
    return [blocks[0], shift(blocks[2], dx=2), shift(blocks[1], dx=1), shift(blocks[3], dx=-1)]


def local(integrals, amplitudes, source_order, target_order):
    x, y_lo, core, y_hi, z = place()
    wanted = flipped(flipped(rolled(target_order.reshape(4, 2, 2, 64), x), y_lo, 1), core, 2)
    wanted_x = wanted.transpose(2, 0, 1, 3).reshape(-1)
    wanted_y = wanted.transpose(2, 1, 0, 3).reshape(-1)
    held = flipped(rolled(source_order.reshape(2, 4, 128).transpose(1, 0, 2), z), y_hi, 1)
    order_in = ((0, 0), (3, 0), (1, 0), (0, 1), (2, 0), (3, 1), (1, 1), (2, 1))
    held = jnp.concatenate([held[at] for at in order_in])
    products, more, at = products_of(integrals, amplitudes, held, jnp.concatenate([wanted_x, wanted_y]))

    n = PAIRS // 2
    (term_y,) = order(at, products, PAIRS + n, [n])
    got_y = shift(term_y, flip_core=True)
    y_own, y_one = order(at, products, PAIRS, [n // 2] * 2, [got_y])
    y_sum = y_own + shift(y_one, flip_y=True)

    products = more(term_y)
    (term_x,) = order(at, products, n, [n])
    got_x = shift(term_x, flip_core=True)
    x_terms = ring_x(*order(at, after(products, y_one), 0, [n // 4] * 2 + [n // 8] * 2 + [n // 4], [got_x]))

    part = n // 8
    y_terms = spread_x([y_sum[part * d : part * (d + 1)] for d in range(4)])
    out_y, x_sum = sum(y_terms), sum(after(x_terms, y_terms[1]))
    out_x = x_sum[:part] + shift(x_sum[part:], flip_y=True)
    return jnp.concatenate([out_y.reshape(part, -1), out_x.reshape(part, -1)], axis=1)


def solution(mesh):
    in_specs = (P("row", "col"), P("col", "row"), P(), P())
    return jax.shard_map(local, mesh=mesh, in_specs=in_specs, out_specs=P("col", "row"), check_vma=False)
```

time: 304 us -> 128 us (0.42); the launches traced: 300 us -> 128 us
  waiting for transfers between devices: 191 us -> 38.3 us
  matrix products: 69.1 us -> 0 us
  Pallas kernels: 0 us -> 51 us
  starting transfers between devices: 0.04 us -> 33.8 us
  local copies, waits for them, and re-layouts: 23.8 us -> 2.4 us
  between operations: 13.4 us -> 0.33 us
    all_gather x1 -> x0, waiting for transfers between devices: 98.6 us -> none  [local(): gathered = lax.all_gather(amplitudes, 'row', axis=1, tiled=True)]
    reduce_scatter x1 -> x0, waiting for transfers between devices: 92.2 us -> none  [local(): return lax.psum_scatter(summands, 'col', scatter_dimension=0, tiled=True)]
    dot_general x1 -> x0, matrix products: 69.1 us -> none  [contract(): lax.dot_general(ordered, integrals, (((0,), (1,)), ((), ())), precision=l...]
    pallas_call x0 -> x14, Pallas kernels: none -> 51 us  [the longest x6 37.5 us: contract(): pl.pallas_call(kernel, in_specs=[pl.BlockSpec(memory_space=pl.ANY) if fre...]
    ppermute x0 -> x22, waiting for transfers between devices: none -> 38.3 us  [shift(): return lax.ppermute(array, AXES, pairs)]
    ppermute x0 -> x22, starting transfers between devices: none -> 33.8 us  [shift(): return lax.ppermute(array, AXES, pairs)]
    gather x2 -> x0, local copies, waits for them, and re-layouts: 16.9 us -> none  [the longest x1 12.4 us: local(): summands = contract(jnp.take(gathered, columns, axis=1), integrals)]
    scatter x1 -> x0, local copies, waits for them, and re-layouts: 4.31 us -> none  [local(): jnp.zeros((length,), jnp.int32).at[source_order]]
  transfers between devices with their start and end apart: 2 -> 22, of which waited for: 2 -> 11; matrix products, arithmetic and copies ran while one was open for 4% -> 2% of each run, Pallas kernels for 0% -> 36%
where the time goes in v3:
time: 128 us
  Pallas kernels  51 us (40%)
  waiting for transfers between devices  38.3 us (30%)
  starting transfers between devices  33.8 us (26%)
  local copies, waits for them, and re-layouts  2.4 us (2%)
  other arithmetic  2.03 us (2%)
    ppermute x22, waiting for transfers between devices, shift(): return lax.ppermute(array, AXES, pairs)  38.3 us
    pallas_call x6, Pallas kernels, contract(): pl.pallas_call(kernel, in_specs=[pl.BlockSpec(memory_space=pl.ANY) if fre...  37.5 us
    ppermute x22, starting transfers between devices, shift(): return lax.ppermute(array, AXES, pairs)  33.8 us
    pallas_call x4, Pallas kernels, order(): pl.pallas_call(functools.partial(order_kernel, first, len(got)), in_specs...  6.59 us
    pallas_call x1, Pallas kernels, find(): pl.pallas_call(find_kernel, in_specs=[SCALARS] * 2, out_specs=SCALARS, ou...  6.37 us
  transfers between devices with their start and end apart: 22, of which 11 were waited for; matrix products, arithmetic and copies ran while one was open for 2% of the time, Pallas kernels for 36%

profile of v3, /device:TPU:0, one launch (start us, length us, event | category | flops | bytes accessed | tf_op | source)
XLA Modules:
  0.0 127.8 jit_solution(14163002597694235825)
XLA Ops:
  0.0 2.0 %collective-permute-start = (f32[2048,128]{1,0:T(8,128)}, f32[2048,128]{1,0:T(8,128)S(1)}, u32[]{:S(2)}, u32[]{:S(2)}) collective-permute-start(f32[2048,128]{1,0:T(8,128)} %a_ref.1), channel_id=1, source_target_pairs={{0,16},{1,17},{16,32},{17,33},{32,48},{33,49},{48,0},{49,1},{2,18}... | collective-permute-start | bytes 3145736 | tf_op jit(solution)/shard_map/ppermute | solution.py:30
  2.0 2.1 %collective-permute-start.1 = (f32[2048,128]{1,0:T(8,128)}, f32[2048,128]{1,0:T(8,128)S(1)}, u32[]{:S(2)}, u32[]{:S(2)}) collective-permute-start(f32[2048,128]{1,0:T(8,128)} %a_ref.1), channel_id=1, source_target_pairs={{0,48},{1,49},{16,0},{17,1},{32,16},{33,17},{48,32},{49,33},{2,50}... | collective-permute-start | bytes 3145736 | tf_op jit(solution)/shard_map/ppermute | solution.py:30
  4.1 3.2 %collective-permute-start.2 = (f32[2048,128]{1,0:T(8,128)}, f32[2048,128]{1,0:T(8,128)S(1)}, u32[]{:S(2)}, u32[]{:S(2)}) collective-permute-start(f32[2048,128]{1,0:T(8,128)} %a_ref.1), channel_id=1, source_target_pairs={{0,64},{1,65},{16,80},{17,81},{32,96},{33,97},{48,112},{49,113},{2... | collective-permute-start | bytes 3145736 | tf_op jit(solution)/shard_map/ppermute | solution.py:30
  7.3 0.8 reshape.19
  8.3 0.1 reshape.21
  8.4 0.8 fusion.3
  9.3 6.4 %find.1.at_ref = s32[2048]{0:T(1024)S(1)} custom-call(s32[1024]{0:T(1024)S(1)} %constant_dynamic-update-slice_fusion.held_ref, s32[2048]{0:T(1024)S(1)} %pad_add_fusion.wanted_ref), custom_call_target="tpu_custom_call" | custom-call | tf_op jit(solution)/shard_map/find/pallas_call | solution.py:200
  15.6 1.2 copy-done
  16.9 8.2 %contract.6 = (bf16[2048,2048]{1,0:T(8,128)(2,1)S(1)}, bf16[2048,2048]{1,0:T(8,128)(2,1)S(1)}, f32[128,8,128]{2,1,0:T(8,128)S(1)}, f32[128,8,128]{2,1,0:T(8,128)S(1)}) custom-call(f32[2048,2048]{1,0:T(8,128)} %v_hbm, f32[2048,128]{1,0:T(8,128)S(1)} %copy-done), custom_call_target="tpu_custom_call" | custom-call | flops 3221225472 | tf_op jit(solution)/shard_map/contract/pallas_call | solution.py:127
  25.1 2.4 %collective-permute-done.refs_0_.refs_1_ = f32[2048,128]{1,0:T(8,128)S(1)} collective-permute-done((f32[2048,128]{1,0:T(8,128)}, f32[2048,128]{1,0:T(8,128)S(1)}, u32[]{:S(2)}, u32[]{:S(2)}) %collective-permute-start) | collective-permute-done | bytes 1048608 | tf_op jit(solution)/shard_map/ppermute | solution.py:30
  27.5 3.0 %collective-permute-done.2.refs_3_.refs_0_ = f32[2048,128]{1,0:T(8,128)S(1)} collective-permute-done((f32[2048,128]{1,0:T(8,128)}, f32[2048,128]{1,0:T(8,128)S(1)}, u32[]{:S(2)}, u32[]{:S(2)}) %collective-permute-start.2) | collective-permute-done | bytes 1048608 | tf_op jit(solution)/shard_map/ppermute | solution.py:30
  30.5 0.1 pack.1
  30.6 3.3 %collective-permute-start.6 = (f32[1024,128]{1,0:T(8,128)S(1)}, f32[1024,128]{1,0:T(8,128)S(1)}, u32[]{:S(2)}, u32[]{:S(2)}) collective-permute-start(f32[1024,128]{1,0:T(8,128)S(1)} %get-tuple-element.64), channel_id=1, source_target_pairs={{0,64},{1,65},{16,80},{17,81},{32,96},{33,97},{48,112},{49,113},{2... | collective-permute-start | bytes 1572872 | tf_op jit(solution)/shard_map/ppermute | solution.py:30
  33.9 3.2 %collective-permute-start.4 = (f32[1024,128]{1,0:T(8,128)S(1)}, f32[1024,128]{1,0:T(8,128)S(1)}, u32[]{:S(2)}, u32[]{:S(2)}) collective-permute-start(f32[1024,128]{1,0:T(8,128)S(1)} %get-tuple-element.65), channel_id=1, source_target_pairs={{0,48},{1,49},{16,0},{17,1},{32,16},{33,17},{48,32},{49,33},{2,50}... | collective-permute-start | bytes 1572872 | tf_op jit(solution)/shard_map/ppermute | solution.py:30
  37.1 7.9 %contract.7 = (bf16[2048,2048]{1,0:T(8,128)(2,1)S(1)}, bf16[2048,2048]{1,0:T(8,128)(2,1)S(1)}, f32[256,8,128]{2,1,0:T(8,128)S(1)}, f32[256,8,128]{2,1,0:T(8,128)S(1)}) custom-call(bf16[2048,2048]{1,0:T(8,128)(2,1)S(1)} %get-tuple-element.49.vh_ref, bf16[2048,2048]{1,0:T(8,128)(2,1)S(1)} %get-tuple-element.50.vl_ref, ...), custom_call_target="tpu_custom_call", output_to_operand_aliasing={{0}: (0, {}), {1}: (1, {})} | custom-call | flops 6442450944 | tf_op jit(solution)/shard_map/contract/pallas_call | solution.py:127
  45.1 3.2 %collective-permute-start.7 = (f32[1024,128]{1,0:T(8,128)S(1)}, f32[1024,128]{1,0:T(8,128)S(1)}, u32[]{:S(2)}, u32[]{:S(2)}) collective-permute-start(f32[1024,128]{1,0:T(8,128)S(1)} %get-tuple-element.63), channel_id=1, source_target_pairs={{0,48},{1,49},{16,0},{17,1},{32,16},{33,17},{48,32},{49,33},{2,50}... | collective-permute-start | bytes 1572872 | tf_op jit(solution)/shard_map/ppermute | solution.py:30
  48.3 0.4 collective-permute-start.8
  48.7 7.9 %contract.8 = (bf16[2048,2048]{1,0:T(8,128)(2,1)S(1)}, bf16[2048,2048]{1,0:T(8,128)(2,1)S(1)}, f32[256,8,128]{2,1,0:T(8,128)S(1)}, f32[256,8,128]{2,1,0:T(8,128)S(1)}) custom-call(bf16[2048,2048]{1,0:T(8,128)(2,1)S(1)} %get-tuple-element.51.vh_ref, bf16[2048,2048]{1,0:T(8,128)(2,1)S(1)} %get-tuple-element.52.vl_ref, ...), custom_call_target="tpu_custom_call", output_to_operand_aliasing={{0}: (0, {}), {1}: (1, {})} | custom-call | flops 6442450944 | tf_op jit(solution)/shard_map/contract/pallas_call | solution.py:127
  56.6 1.9 %collective-permute-done.5.refs_0_ = f32[1024,128]{1,0:T(8,128)S(1)} collective-permute-done((f32[1024,128]{1,0:T(8,128)S(1)}, f32[1024,128]{1,0:T(8,128)S(1)}, u32[]{:S(2)}, u32[]{:S(2)}) %collective-permute-start.5) | collective-permute-done | bytes 524320 | tf_op jit(solution)/shard_map/ppermute | solution.py:30
  58.5 2.4 %collective-permute-done.8.refs_3_ = f32[1024,128]{1,0:T(8,128)S(1)} collective-permute-done((f32[1024,128]{1,0:T(8,128)S(1)}, f32[1024,128]{1,0:T(8,128)S(1)}, u32[]{:S(2)}, u32[]{:S(2)}) %collective-permute-start.8) | collective-permute-done | bytes 524320 | tf_op jit(solution)/shard_map/ppermute | solution.py:30
  60.9 0.8 collective-permute-start.10
  61.8 7.9 %contract.9 = (bf16[2048,2048]{1,0:T(8,128)(2,1)S(1)}, bf16[2048,2048]{1,0:T(8,128)(2,1)S(1)}, f32[256,8,128]{2,1,0:T(8,128)S(1)}, f32[256,8,128]{2,1,0:T(8,128)S(1)}) custom-call(bf16[2048,2048]{1,0:T(8,128)(2,1)S(1)} %get-tuple-element.58.vh_ref, bf16[2048,2048]{1,0:T(8,128)(2,1)S(1)} %get-tuple-element.59.vl_ref, ...), custom_call_target="tpu_custom_call", output_to_operand_aliasing={{0}: (0, {}), {1}: (1, {})} | custom-call | flops 6442450944 | tf_op jit(solution)/shard_map/contract/pallas_call | solution.py:127
  69.7 0.2 merge.2.refs_2_
  69.9 1.1 collective-permute-done.9.refs_0_
  71.1 2.8 %contract.10 = (bf16[2048,2048]{1,0:T(8,128)(2,1)S(1)}, bf16[2048,2048]{1,0:T(8,128)(2,1)S(1)}, f32[1024,8,128]{2,1,0:T(8,128)S(1)}) custom-call(bf16[2048,2048]{1,0:T(8,128)(2,1)S(1)} %get-tuple-element.66.vh_ref, bf16[2048,2048]{1,0:T(8,128)(2,1)S(1)} %get-tuple-element.67.vl_ref, ...), custom_call_target="tpu_custom_call", output_to_operand_aliasing={{0}: (0, {}), {1}: (1, {}), {2}: (4, {})} | custom-call | flops 1610612736 | tf_op jit(solution)/shard_map/contract/pallas_call | solution.py:127
  73.8 1.6 %order.4 = f32[512,8,128]{2,1,0:T(8,128)S(1)} custom-call(s32[2048]{0:T(1024)S(1)} %find.1.at_ref, f32[1024,8,128]{2,1,0:T(8,128)S(1)} %get-tuple-element.73.products), custom_call_target="tpu_custom_call" | custom-call | tf_op jit(solution)/shard_map/order/pallas_call | solution.py:229
  75.4 0.1 collective-permute-start.11
  75.5 0.2 merge.3.refs_2_
  75.8 2.8 %contract.11 = (bf16[2048,2048]{1,0:T(8,128)(2,1)S(1)}, bf16[2048,2048]{1,0:T(8,128)(2,1)S(1)}, f32[1024,8,128]{2,1,0:T(8,128)S(1)}) custom-call(bf16[2048,2048]{1,0:T(8,128)(2,1)S(1)} %get-tuple-element.78.vh_ref, bf16[2048,2048]{1,0:T(8,128)(2,1)S(1)} %get-tuple-element.79.vl_ref, ...), custom_call_target="tpu_custom_call", output_to_operand_aliasing={{0}: (0, {}), {1}: (1, {}), {2}: (4, {})} | custom-call | flops 1610612736 | tf_op jit(solution)/shard_map/contract/pallas_call | solution.py:127
  78.5 1.6 %order.6 = f32[512,8,128]{2,1,0:T(8,128)S(1)} custom-call(s32[2048]{0:T(1024)S(1)} %find.1.at_ref, f32[1024,8,128]{2,1,0:T(8,128)S(1)} %get-tuple-element.82.products), custom_call_target="tpu_custom_call" | custom-call | tf_op jit(solution)/shard_map/order/pallas_call | solution.py:229
  80.2 0.6 collective-permute-start.16
  80.7 1.7 %order.5 = (f32[256,8,128]{2,1,0:T(8,128)S(1)}, f32[256,8,128]{2,1,0:T(8,128)S(1)}) custom-call(s32[2048]{0:T(1024)S(1)} %find.1.at_ref, f32[1024,8,128]{2,1,0:T(8,128)S(1)} %get-tuple-element.73.products, f32[512,8,128]{2,1,0:T(8,128)S(1)} %collective-permute-done.11.refs_0_), custom_call_target="tpu_custom_call" | custom-call | tf_op jit(solution)/shard_map/order/pallas_call | solution.py:229
  82.4 1.0 collective-permute-start.12
  83.5 1.1 collective-permute-done.16.refs_0_
  84.5 1.7 %order.7 = (f32[128,8,128]{2,1,0:T(8,128)S(1)}, f32[128,8,128]{2,1,0:T(8,128)S(1)}, f32[64,8,128]{2,1,0:T(8,128)S(1)}, f32[64,8,128]{2,1,0:T(8,128)S(1)}, f32[128,8,128]{2,1,0:T(8,128)S(1)}) custom-call(s32[2048]{0:T(1024)S(1)} %find.1.at_ref, f32[1024,8,128]{2,1,0:T(8,128)S(1)} %get-tuple-element.82.products, f32[512,8,128]{2,1,0:T(8,128)S(1)} %collective-permute-done.16.refs_0_), custom_call_target="tpu_custom_call" | custom-call | tf_op jit(solution)/shard_map/order/pallas_call | solution.py:229
  86.2 2.8 %collective-permute-start.19 = (f32[64,8,128]{2,1,0:T(8,128)S(1)}, f32[64,8,128]{2,1,0:T(8,128)S(1)}, u32[]{:S(2)}, u32[]{:S(2)}) collective-permute-start(f32[64,8,128]{2,1,0:T(8,128)S(1)} %get-tuple-element.87), channel_id=1, source_target_pairs={{0,12},{1,13},{16,28},{17,29},{32,44},{33,45},{48,60},{49,61},{2,1... | collective-permute-start | bytes 786440 | tf_op jit(solution)/shard_map/ppermute | solution.py:30
  89.0 6.1 %collective-permute-done.19 = f32[64,8,128]{2,1,0:T(8,128)S(1)} collective-permute-done((f32[64,8,128]{2,1,0:T(8,128)S(1)}, f32[64,8,128]{2,1,0:T(8,128)S(1)}, u32[]{:S(2)}, u32[]{:S(2)}) %collective-permute-start.19) | collective-permute-done | bytes 262176 | tf_op jit(solution)/shard_map/ppermute | solution.py:30
  95.2 3.8 %collective-permute-start.20 = (f32[128,8,128]{2,1,0:T(8,128)S(1)}, f32[128,8,128]{2,1,0:T(8,128)S(1)}, u32[]{:S(2)}, u32[]{:S(2)}) collective-permute-start(f32[128,8,128]{2,1,0:T(8,128)S(1)} %add_dynamic-update-slice_fusion), channel_id=1, source_target_pairs={{0,12},{1,13},{16,28},{17,29},{32,44},{33,45},{48,60},{49,61},{2,1... | collective-permute-start | bytes 1572872 | tf_op jit(solution)/shard_map/ppermute | solution.py:30
  99.1 8.8 %collective-permute-done.12 = f32[256,8,128]{2,1,0:T(8,128)S(1)} collective-permute-done((f32[256,8,128]{2,1,0:T(8,128)S(1)}, f32[256,8,128]{2,1,0:T(8,128)S(1)}, u32[]{:S(2)}, u32[]{:S(2)}) %collective-permute-start.12) | collective-permute-done | bytes 1048608 | tf_op jit(solution)/shard_map/ppermute | solution.py:30
  107.9 0.1 add.51
  108.0 3.1 %collective-permute-start.13 = (f32[64,8,128]{2,1,0:T(8,128)S(1)}, f32[64,8,128]{2,1,0:T(8,128)S(1)}, u32[]{:S(2)}, u32[]{:S(2)}) collective-permute-start(f32[64,8,128]{2,1,0:T(8,128)S(1)} %get-tuple-element.93), channel_id=1, source_target_pairs={{0,8},{1,9},{16,24},{17,25},{32,40},{33,41},{48,56},{49,57},{2,10}... | collective-permute-start | bytes 786440 | tf_op jit(solution)/shard_map/ppermute | solution.py:30
  111.1 0.6 collective-permute-start.14
  111.7 2.6 %collective-permute-start.15 = (f32[64,8,128]{2,1,0:T(8,128)S(1)}, f32[64,8,128]{2,1,0:T(8,128)S(1)}, u32[]{:S(2)}, u32[]{:S(2)}) collective-permute-start(f32[64,8,128]{2,1,0:T(8,128)S(1)} %get-tuple-element.92), channel_id=1, source_target_pairs={{0,12},{1,13},{16,28},{17,29},{32,44},{33,45},{48,60},{49,61},{2,1... | collective-permute-start | bytes 786440 | tf_op jit(solution)/shard_map/ppermute | solution.py:30
  114.4 5.9 %collective-permute-done.18 = f32[128,8,128]{2,1,0:T(8,128)S(1)} collective-permute-done((f32[128,8,128]{2,1,0:T(8,128)S(1)}, f32[128,8,128]{2,1,0:T(8,128)S(1)}, u32[]{:S(2)}, u32[]{:S(2)}) %collective-permute-start.18) | collective-permute-done | bytes 524320 | tf_op jit(solution)/shard_map/ppermute | solution.py:30
  120.4 0.8 collective-permute-start.21
  121.2 3.4 %collective-permute-done.14 = f32[64,8,128]{2,1,0:T(8,128)S(1)} collective-permute-done((f32[64,8,128]{2,1,0:T(8,128)S(1)}, f32[64,8,128]{2,1,0:T(8,128)S(1)}, u32[]{:S(2)}, u32[]{:S(2)}) %collective-permute-start.14) | collective-permute-done | bytes 262176 | tf_op jit(solution)/shard_map/ppermute | solution.py:30
  124.7 2.1 %collective-permute-done.21 = f32[64,8,128]{2,1,0:T(8,128)S(1)} collective-permute-done((f32[64,8,128]{2,1,0:T(8,128)S(1)}, f32[64,8,128]{2,1,0:T(8,128)S(1)}, u32[]{:S(2)}, u32[]{:S(2)}) %collective-permute-start.21) | collective-permute-done | bytes 262176 | tf_op jit(solution)/shard_map/ppermute | solution.py:30
  127.0 0.8 pad_maximum_fusion
  (44 shorter events, 0.9 us)
Async XLA Ops:
  0.0 27.5 %collective-permute-start = (f32[2048,128]{1,0:T(8,128)}, f32[2048,128]{1,0:T(8,128)S(1)}, u32[]{:S(2)}, u32[]{:S(2)}) collective-permute-start(f32[2048,128]{1,0:T(8,128)} %a_ref.1), channel_id=1, source_target_pairs={{0,16},{1,17},{16,32},{17,33},{32,48},{33,49},{48,0},{49,1},{2,18}... | collective-permute-start | bytes 3145736 | tf_op jit(solution)/shard_map/ppermute | solution.py:30
  2.0 25.5 %collective-permute-start.1 = (f32[2048,128]{1,0:T(8,128)}, f32[2048,128]{1,0:T(8,128)S(1)}, u32[]{:S(2)}, u32[]{:S(2)}) collective-permute-start(f32[2048,128]{1,0:T(8,128)} %a_ref.1), channel_id=1, source_target_pairs={{0,48},{1,49},{16,0},{17,1},{32,16},{33,17},{48,32},{49,33},{2,50}... | collective-permute-start | bytes 3145736 | tf_op jit(solution)/shard_map/ppermute | solution.py:30
  4.1 26.4 %collective-permute-start.2 = (f32[2048,128]{1,0:T(8,128)}, f32[2048,128]{1,0:T(8,128)S(1)}, u32[]{:S(2)}, u32[]{:S(2)}) collective-permute-start(f32[2048,128]{1,0:T(8,128)} %a_ref.1), channel_id=1, source_target_pairs={{0,64},{1,65},{16,80},{17,81},{32,96},{33,97},{48,112},{49,113},{2... | collective-permute-start | bytes 3145736 | tf_op jit(solution)/shard_map/ppermute | solution.py:30
  15.6 1.2 copy-start
  30.6 17.7 %collective-permute-start.6 = (f32[1024,128]{1,0:T(8,128)S(1)}, f32[1024,128]{1,0:T(8,128)S(1)}, u32[]{:S(2)}, u32[]{:S(2)}) collective-permute-start(f32[1024,128]{1,0:T(8,128)S(1)} %get-tuple-element.64), channel_id=1, source_target_pairs={{0,64},{1,65},{16,80},{17,81},{32,96},{33,97},{48,112},{49,113},{2... | collective-permute-start | bytes 1572872 | tf_op jit(solution)/shard_map/ppermute | solution.py:30
  33.9 14.8 %collective-permute-start.3 = (f32[1024,128]{1,0:T(8,128)S(1)}, f32[1024,128]{1,0:T(8,128)S(1)}, u32[]{:S(2)}, u32[]{:S(2)}) collective-permute-start(f32[1024,128]{1,0:T(8,128)S(1)} %get-tuple-element.56), channel_id=1, source_target_pairs={{0,16},{1,17},{16,32},{17,33},{32,48},{33,49},{48,0},{49,1},{2,18}... | collective-permute-start | bytes 1572872 | tf_op jit(solution)/shard_map/ppermute | solution.py:30
  33.9 14.8 %collective-permute-start.4 = (f32[1024,128]{1,0:T(8,128)S(1)}, f32[1024,128]{1,0:T(8,128)S(1)}, u32[]{:S(2)}, u32[]{:S(2)}) collective-permute-start(f32[1024,128]{1,0:T(8,128)S(1)} %get-tuple-element.65), channel_id=1, source_target_pairs={{0,48},{1,49},{16,0},{17,1},{32,16},{33,17},{48,32},{49,33},{2,50}... | collective-permute-start | bytes 1572872 | tf_op jit(solution)/shard_map/ppermute | solution.py:30
  45.0 13.5 %collective-permute-start.5 = (f32[1024,128]{1,0:T(8,128)S(1)}, f32[1024,128]{1,0:T(8,128)S(1)}, u32[]{:S(2)}, u32[]{:S(2)}) collective-permute-start(f32[1024,128]{1,0:T(8,128)S(1)} %get-tuple-element.63), channel_id=1, source_target_pairs={{0,16},{1,17},{16,32},{17,33},{32,48},{33,49},{48,0},{49,1},{2,18}... | collective-permute-start | bytes 1572872 | tf_op jit(solution)/shard_map/ppermute | solution.py:30
  45.1 16.7 %collective-permute-start.7 = (f32[1024,128]{1,0:T(8,128)S(1)}, f32[1024,128]{1,0:T(8,128)S(1)}, u32[]{:S(2)}, u32[]{:S(2)}) collective-permute-start(f32[1024,128]{1,0:T(8,128)S(1)} %get-tuple-element.63), channel_id=1, source_target_pairs={{0,48},{1,49},{16,0},{17,1},{32,16},{33,17},{48,32},{49,33},{2,50}... | collective-permute-start | bytes 1572872 | tf_op jit(solution)/shard_map/ppermute | solution.py:30
  48.3 12.6 %collective-permute-start.8 = (f32[1024,128]{1,0:T(8,128)S(1)}, f32[1024,128]{1,0:T(8,128)S(1)}, u32[]{:S(2)}, u32[]{:S(2)}) collective-permute-start(f32[1024,128]{1,0:T(8,128)S(1)} %get-tuple-element.65), channel_id=1, source_target_pairs={{0,64},{1,65},{16,80},{17,81},{32,96},{33,97},{48,112},{49,113},{2... | collective-permute-start | bytes 1572872 | tf_op jit(solution)/shard_map/ppermute | solution.py:30
  58.5 12.5 %collective-permute-start.9 = (f32[1024,128]{1,0:T(8,128)S(1)}, f32[1024,128]{1,0:T(8,128)S(1)}, u32[]{:S(2)}, u32[]{:S(2)}) collective-permute-start(f32[1024,128]{1,0:T(8,128)S(1)} %collective-permute-done.5.refs_0_), channel_id=1, source_target_pairs={{0,16},{1,17},{16,32},{17,33},{32,48},{33,49},{48,0},{49,1},{2,18}... | collective-permute-start | bytes 1572872 | tf_op jit(solution)/shard_map/ppermute | solution.py:30
  60.9 10.1 %collective-permute-start.10 = (f32[1024,128]{1,0:T(8,128)S(1)}, f32[1024,128]{1,0:T(8,128)S(1)}, u32[]{:S(2)}, u32[]{:S(2)}) collective-permute-start(f32[1024,128]{1,0:T(8,128)S(1)} %collective-permute-done.8.refs_3_), channel_id=1, source_target_pairs={{0,48},{1,49},{16,0},{17,1},{32,16},{33,17},{48,32},{49,33},{2,50}... | collective-permute-start | bytes 1572872 | tf_op jit(solution)/shard_map/ppermute | solution.py:30
  75.4 5.3 %collective-permute-start.11 = (f32[512,8,128]{2,1,0:T(8,128)S(1)}, f32[512,8,128]{2,1,0:T(8,128)S(1)}, u32[]{:S(2)}, u32[]{:S(2)}) collective-permute-start(f32[512,8,128]{2,1,0:T(8,128)S(1)} %order.4), channel_id=1, source_target_pairs={{0,1},{1,0},{16,17},{17,16},{32,33},{33,32},{48,49},{49,48},{2,3},... | collective-permute-start | bytes 6291464 | tf_op jit(solution)/shard_map/ppermute | solution.py:30
  80.2 4.4 %collective-permute-start.16 = (f32[512,8,128]{2,1,0:T(8,128)S(1)}, f32[512,8,128]{2,1,0:T(8,128)S(1)}, u32[]{:S(2)}, u32[]{:S(2)}) collective-permute-start(f32[512,8,128]{2,1,0:T(8,128)S(1)} %order.6), channel_id=1, source_target_pairs={{0,1},{1,0},{16,17},{17,16},{32,33},{33,32},{48,49},{49,48},{2,3},... | collective-permute-start | bytes 6291464 | tf_op jit(solution)/shard_map/ppermute | solution.py:30
  82.4 25.4 %collective-permute-start.12 = (f32[256,8,128]{2,1,0:T(8,128)S(1)}, f32[256,8,128]{2,1,0:T(8,128)S(1)}, u32[]{:S(2)}, u32[]{:S(2)}) collective-permute-start(f32[256,8,128]{2,1,0:T(8,128)S(1)} %get-tuple-element.75), channel_id=1, source_target_pairs={{0,2},{1,3},{16,18},{17,19},{32,34},{33,35},{48,50},{49,51},{2,0},... | collective-permute-start | bytes 3145736 | tf_op jit(solution)/shard_map/ppermute | solution.py:30
  86.2 8.9 %collective-permute-start.19 = (f32[64,8,128]{2,1,0:T(8,128)S(1)}, f32[64,8,128]{2,1,0:T(8,128)S(1)}, u32[]{:S(2)}, u32[]{:S(2)}) collective-permute-start(f32[64,8,128]{2,1,0:T(8,128)S(1)} %get-tuple-element.87), channel_id=1, source_target_pairs={{0,12},{1,13},{16,28},{17,29},{32,44},{33,45},{48,60},{49,61},{2,1... | collective-permute-start | bytes 786440 | tf_op jit(solution)/shard_map/ppermute | solution.py:30
  89.0 9.9 %collective-permute-start.17 = (f32[64,8,128]{2,1,0:T(8,128)S(1)}, f32[64,8,128]{2,1,0:T(8,128)S(1)}, u32[]{:S(2)}, u32[]{:S(2)}) collective-permute-start(f32[64,8,128]{2,1,0:T(8,128)S(1)} %get-tuple-element.85), channel_id=1, source_target_pairs={{0,4},{1,5},{16,20},{17,21},{32,36},{33,37},{48,52},{49,53},{2,6},... | collective-permute-start | bytes 786440 | tf_op jit(solution)/shard_map/ppermute | solution.py:30
  95.2 19.2 %collective-permute-start.20 = (f32[128,8,128]{2,1,0:T(8,128)S(1)}, f32[128,8,128]{2,1,0:T(8,128)S(1)}, u32[]{:S(2)}, u32[]{:S(2)}) collective-permute-start(f32[128,8,128]{2,1,0:T(8,128)S(1)} %add_dynamic-update-slice_fusion), channel_id=1, source_target_pairs={{0,12},{1,13},{16,28},{17,29},{32,44},{33,45},{48,60},{49,61},{2,1... | collective-permute-start | bytes 1572872 | tf_op jit(solution)/shard_map/ppermute | solution.py:30
  99.0 21.3 %collective-permute-start.18 = (f32[128,8,128]{2,1,0:T(8,128)S(1)}, f32[128,8,128]{2,1,0:T(8,128)S(1)}, u32[]{:S(2)}, u32[]{:S(2)}) collective-permute-start(f32[128,8,128]{2,1,0:T(8,128)S(1)} %add_dynamic-update-slice_fusion.1), channel_id=1, source_target_pairs={{0,4},{1,5},{16,20},{17,21},{32,36},{33,37},{48,52},{49,53},{2,6},... | collective-permute-start | bytes 1572872 | tf_op jit(solution)/shard_map/ppermute | solution.py:30
  108.0 12.3 %collective-permute-start.13 = (f32[64,8,128]{2,1,0:T(8,128)S(1)}, f32[64,8,128]{2,1,0:T(8,128)S(1)}, u32[]{:S(2)}, u32[]{:S(2)}) collective-permute-start(f32[64,8,128]{2,1,0:T(8,128)S(1)} %get-tuple-element.93), channel_id=1, source_target_pairs={{0,8},{1,9},{16,24},{17,25},{32,40},{33,41},{48,56},{49,57},{2,10}... | collective-permute-start | bytes 786440 | tf_op jit(solution)/shard_map/ppermute | solution.py:30
  111.1 13.5 %collective-permute-start.14 = (f32[64,8,128]{2,1,0:T(8,128)S(1)}, f32[64,8,128]{2,1,0:T(8,128)S(1)}, u32[]{:S(2)}, u32[]{:S(2)}) collective-permute-start(f32[64,8,128]{2,1,0:T(8,128)S(1)} %get-tuple-element.91), channel_id=1, source_target_pairs={{0,4},{1,5},{16,20},{17,21},{32,36},{33,37},{48,52},{49,53},{2,6},... | collective-permute-start | bytes 786440 | tf_op jit(solution)/shard_map/ppermute | solution.py:30
  111.7 12.9 %collective-permute-start.15 = (f32[64,8,128]{2,1,0:T(8,128)S(1)}, f32[64,8,128]{2,1,0:T(8,128)S(1)}, u32[]{:S(2)}, u32[]{:S(2)}) collective-permute-start(f32[64,8,128]{2,1,0:T(8,128)S(1)} %get-tuple-element.92), channel_id=1, source_target_pairs={{0,12},{1,13},{16,28},{17,29},{32,44},{33,45},{48,60},{49,61},{2,1... | collective-permute-start | bytes 786440 | tf_op jit(solution)/shard_map/ppermute | solution.py:30
  120.4 6.5 %collective-permute-start.21 = (f32[64,8,128]{2,1,0:T(8,128)S(1)}, f32[64,8,128]{2,1,0:T(8,128)S(1)}, u32[]{:S(2)}, u32[]{:S(2)}) collective-permute-start(f32[64,8,128]{2,1,0:T(8,128)S(1)} %slice.77), channel_id=1, source_target_pairs={{0,2},{1,3},{16,18},{17,19},{32,34},{33,35},{48,50},{49,51},{2,0},... | collective-permute-start | bytes 786440 | tf_op jit(solution)/shard_map/ppermute | solution.py:30

commit v4 on v3

--- a/solution.py
+++ b/solution.py
@@ -214,7 +214,7 @@
     row = 0
     for ref in outs:
 
-        @pl.loop(0, ref.shape[0], unroll=8)
+        @pl.loop(0, ref.shape[0], unroll=32)
         def _(q, ref=ref, row=row):
             block = products[at_ref[first + row + q]]
             for term in got:
@@ -270,7 +270,7 @@
 
 def ring_x(own, up, far_up, far_down, down):
     n = far_up.shape[0]
-    far_up, far_down = shift(far_up, dx=1), shift(far_down, dx=-1)
+    far_up, far_down = lax.optimization_barrier((shift(far_up, dx=1), shift(far_down, dx=-1)))
     return own, shift(add_rows(up, far_up, 0), dx=1), shift(add_rows(down, far_down, n), dx=-1)
 
 
@@ -300,8 +300,10 @@
     x_terms = ring_x(*order(at, after(products, y_one), 0, [n // 4] * 2 + [n // 8] * 2 + [n // 4], [got_x]))
 
     part = n // 8
-    y_terms = spread_x([y_sum[part * d : part * (d + 1)] for d in range(4)])
-    out_y, x_sum = sum(y_terms), sum(after(x_terms, y_terms[1]))
+    half = part // 2
+    y_rows = (0, part), (part, 2 * part), (2 * part, 2 * part + half), (2 * part + half, 3 * part), (3 * part, 4 * part)
+    y_terms = ring_x(*[y_sum[i:j] for i, j in y_rows])
+    out_y, x_sum = sum(y_terms), sum(after(x_terms, y_sum))
     out_x = x_sum[:part] + shift(x_sum[part:], flip_y=True)
     return jnp.concatenate([out_y.reshape(part, -1), out_x.reshape(part, -1)], axis=1)
 

time: 128 us -> 125 us (0.977)
  waiting for transfers between devices: 38.3 us -> 35.4 us
    ppermute x22 -> x23, waiting for transfers between devices: 38.3 us -> 35.4 us  [shift(): return lax.ppermute(array, AXES, pairs)]
    ppermute x22 -> x23, starting transfers between devices: 33.8 us -> 33.7 us  [shift(): return lax.ppermute(array, AXES, pairs)]
  transfers between devices with their start and end apart: 22 -> 23, of which waited for: 11 -> 12; matrix products, arithmetic and copies ran while one was open for 2% -> 2% of each run, Pallas kernels for 36% -> 37%
where the time goes in v4:
time: 125 us; the launch traced here: 124 us
  Pallas kernels  50.1 us (40%)
  waiting for transfers between devices  35.4 us (28%)
  starting transfers between devices  33.7 us (27%)
  local copies, waits for them, and re-layouts  2.4 us (2%)
  other arithmetic  2.06 us (2%)
    pallas_call x6, Pallas kernels, contract(): pl.pallas_call(kernel, in_specs=[pl.BlockSpec(memory_space=pl.ANY) if fre...  37.5 us
    ppermute x23, waiting for transfers between devices, shift(): return lax.ppermute(array, AXES, pairs)  35.4 us
    ppermute x23, starting transfers between devices, shift(): return lax.ppermute(array, AXES, pairs)  33.7 us
    pallas_call x1, Pallas kernels, find(): pl.pallas_call(find_kernel, in_specs=[SCALARS] * 2, out_specs=SCALARS, ou...  6.37 us
    pallas_call x4, Pallas kernels, order(): pl.pallas_call(functools.partial(order_kernel, first, len(got)), in_specs...  5.61 us
  transfers between devices with their start and end apart: 23, of which 12 were waited for; matrix products, arithmetic and copies ran while one was open for 2% of the time, Pallas kernels for 37%

profile of v4, /device:TPU:0, one launch (start us, length us, event | category | flops | bytes accessed | tf_op | source)
XLA Modules:
  0.0 124.0 jit_solution(12028138255101874366)
XLA Ops:
  0.0 2.0 %collective-permute-start = (f32[2048,128]{1,0:T(8,128)}, f32[2048,128]{1,0:T(8,128)S(1)}, u32[]{:S(2)}, u32[]{:S(2)}) collective-permute-start(f32[2048,128]{1,0:T(8,128)} %a_ref.1), channel_id=1, source_target_pairs={{0,16},{1,17},{16,32},{17,33},{32,48},{33,49},{48,0},{49,1},{2,18}... | collective-permute-start | bytes 3145736 | tf_op jit(solution)/shard_map/ppermute | solution.py:30
  2.0 2.1 %collective-permute-start.1 = (f32[2048,128]{1,0:T(8,128)}, f32[2048,128]{1,0:T(8,128)S(1)}, u32[]{:S(2)}, u32[]{:S(2)}) collective-permute-start(f32[2048,128]{1,0:T(8,128)} %a_ref.1), channel_id=1, source_target_pairs={{0,48},{1,49},{16,0},{17,1},{32,16},{33,17},{48,32},{49,33},{2,50}... | collective-permute-start | bytes 3145736 | tf_op jit(solution)/shard_map/ppermute | solution.py:30
  4.1 3.2 %collective-permute-start.2 = (f32[2048,128]{1,0:T(8,128)}, f32[2048,128]{1,0:T(8,128)S(1)}, u32[]{:S(2)}, u32[]{:S(2)}) collective-permute-start(f32[2048,128]{1,0:T(8,128)} %a_ref.1), channel_id=1, source_target_pairs={{0,64},{1,65},{16,80},{17,81},{32,96},{33,97},{48,112},{49,113},{2... | collective-permute-start | bytes 3145736 | tf_op jit(solution)/shard_map/ppermute | solution.py:30
  7.3 0.8 reshape.19
  8.4 0.8 fusion.4
  9.3 6.4 %find.1.at_ref = s32[2048]{0:T(1024)S(1)} custom-call(s32[1024]{0:T(1024)S(1)} %constant_dynamic-update-slice_fusion.held_ref, s32[2048]{0:T(1024)S(1)} %pad_add_fusion.wanted_ref), custom_call_target="tpu_custom_call" | custom-call | tf_op jit(solution)/shard_map/find/pallas_call | solution.py:200
  15.6 1.2 copy-done
  16.9 8.2 %contract.6 = (bf16[2048,2048]{1,0:T(8,128)(2,1)S(1)}, bf16[2048,2048]{1,0:T(8,128)(2,1)S(1)}, f32[128,8,128]{2,1,0:T(8,128)S(1)}, f32[128,8,128]{2,1,0:T(8,128)S(1)}) custom-call(f32[2048,2048]{1,0:T(8,128)} %v_hbm, f32[2048,128]{1,0:T(8,128)S(1)} %copy-done), custom_call_target="tpu_custom_call" | custom-call | flops 3221225472 | tf_op jit(solution)/shard_map/contract/pallas_call | solution.py:127
  25.1 2.4 %collective-permute-done.refs_0_.refs_1_ = f32[2048,128]{1,0:T(8,128)S(1)} collective-permute-done((f32[2048,128]{1,0:T(8,128)}, f32[2048,128]{1,0:T(8,128)S(1)}, u32[]{:S(2)}, u32[]{:S(2)}) %collective-permute-start) | collective-permute-done | bytes 1048608 | tf_op jit(solution)/shard_map/ppermute | solution.py:30
  27.5 3.0 %collective-permute-done.2.refs_3_.refs_0_ = f32[2048,128]{1,0:T(8,128)S(1)} collective-permute-done((f32[2048,128]{1,0:T(8,128)}, f32[2048,128]{1,0:T(8,128)S(1)}, u32[]{:S(2)}, u32[]{:S(2)}) %collective-permute-start.2) | collective-permute-done | bytes 1048608 | tf_op jit(solution)/shard_map/ppermute | solution.py:30
  30.5 0.1 pack.1
  30.6 3.3 %collective-permute-start.6 = (f32[1024,128]{1,0:T(8,128)S(1)}, f32[1024,128]{1,0:T(8,128)S(1)}, u32[]{:S(2)}, u32[]{:S(2)}) collective-permute-start(f32[1024,128]{1,0:T(8,128)S(1)} %get-tuple-element.68), channel_id=1, source_target_pairs={{0,64},{1,65},{16,80},{17,81},{32,96},{33,97},{48,112},{49,113},{2... | collective-permute-start | bytes 1572872 | tf_op jit(solution)/shard_map/ppermute | solution.py:30
  33.9 3.2 %collective-permute-start.4 = (f32[1024,128]{1,0:T(8,128)S(1)}, f32[1024,128]{1,0:T(8,128)S(1)}, u32[]{:S(2)}, u32[]{:S(2)}) collective-permute-start(f32[1024,128]{1,0:T(8,128)S(1)} %get-tuple-element.69), channel_id=1, source_target_pairs={{0,48},{1,49},{16,0},{17,1},{32,16},{33,17},{48,32},{49,33},{2,50}... | collective-permute-start | bytes 1572872 | tf_op jit(solution)/shard_map/ppermute | solution.py:30
  37.1 7.9 %contract.7 = (bf16[2048,2048]{1,0:T(8,128)(2,1)S(1)}, bf16[2048,2048]{1,0:T(8,128)(2,1)S(1)}, f32[256,8,128]{2,1,0:T(8,128)S(1)}, f32[256,8,128]{2,1,0:T(8,128)S(1)}) custom-call(bf16[2048,2048]{1,0:T(8,128)(2,1)S(1)} %get-tuple-element.53.vh_ref, bf16[2048,2048]{1,0:T(8,128)(2,1)S(1)} %get-tuple-element.54.vl_ref, ...), custom_call_target="tpu_custom_call", output_to_operand_aliasing={{0}: (0, {}), {1}: (1, {})} | custom-call | flops 6442450944 | tf_op jit(solution)/shard_map/contract/pallas_call | solution.py:127
  45.1 3.2 %collective-permute-start.7 = (f32[1024,128]{1,0:T(8,128)S(1)}, f32[1024,128]{1,0:T(8,128)S(1)}, u32[]{:S(2)}, u32[]{:S(2)}) collective-permute-start(f32[1024,128]{1,0:T(8,128)S(1)} %get-tuple-element.67), channel_id=1, source_target_pairs={{0,48},{1,49},{16,0},{17,1},{32,16},{33,17},{48,32},{49,33},{2,50}... | collective-permute-start | bytes 1572872 | tf_op jit(solution)/shard_map/ppermute | solution.py:30
  48.3 0.4 collective-permute-start.8
  48.7 7.9 %contract.8 = (bf16[2048,2048]{1,0:T(8,128)(2,1)S(1)}, bf16[2048,2048]{1,0:T(8,128)(2,1)S(1)}, f32[256,8,128]{2,1,0:T(8,128)S(1)}, f32[256,8,128]{2,1,0:T(8,128)S(1)}) custom-call(bf16[2048,2048]{1,0:T(8,128)(2,1)S(1)} %get-tuple-element.55.vh_ref, bf16[2048,2048]{1,0:T(8,128)(2,1)S(1)} %get-tuple-element.56.vl_ref, ...), custom_call_target="tpu_custom_call", output_to_operand_aliasing={{0}: (0, {}), {1}: (1, {})} | custom-call | flops 6442450944 | tf_op jit(solution)/shard_map/contract/pallas_call | solution.py:127
  56.6 1.9 %collective-permute-done.5.refs_0_ = f32[1024,128]{1,0:T(8,128)S(1)} collective-permute-done((f32[1024,128]{1,0:T(8,128)S(1)}, f32[1024,128]{1,0:T(8,128)S(1)}, u32[]{:S(2)}, u32[]{:S(2)}) %collective-permute-start.5) | collective-permute-done | bytes 524320 | tf_op jit(solution)/shard_map/ppermute | solution.py:30
  58.5 2.4 %collective-permute-done.8.refs_3_ = f32[1024,128]{1,0:T(8,128)S(1)} collective-permute-done((f32[1024,128]{1,0:T(8,128)S(1)}, f32[1024,128]{1,0:T(8,128)S(1)}, u32[]{:S(2)}, u32[]{:S(2)}) %collective-permute-start.8) | collective-permute-done | bytes 524320 | tf_op jit(solution)/shard_map/ppermute | solution.py:30
  60.9 0.8 collective-permute-start.10
  61.8 7.9 %contract.9 = (bf16[2048,2048]{1,0:T(8,128)(2,1)S(1)}, bf16[2048,2048]{1,0:T(8,128)(2,1)S(1)}, f32[256,8,128]{2,1,0:T(8,128)S(1)}, f32[256,8,128]{2,1,0:T(8,128)S(1)}) custom-call(bf16[2048,2048]{1,0:T(8,128)(2,1)S(1)} %get-tuple-element.62.vh_ref, bf16[2048,2048]{1,0:T(8,128)(2,1)S(1)} %get-tuple-element.63.vl_ref, ...), custom_call_target="tpu_custom_call", output_to_operand_aliasing={{0}: (0, {}), {1}: (1, {})} | custom-call | flops 6442450944 | tf_op jit(solution)/shard_map/contract/pallas_call | solution.py:127
  69.7 0.2 merge.2.refs_2_
  69.9 0.2 merge.3.refs_2_
  70.2 0.8 collective-permute-done.9.refs_0_
  71.1 2.8 %contract.10 = (bf16[2048,2048]{1,0:T(8,128)(2,1)S(1)}, bf16[2048,2048]{1,0:T(8,128)(2,1)S(1)}, f32[1024,8,128]{2,1,0:T(8,128)S(1)}) custom-call(bf16[2048,2048]{1,0:T(8,128)(2,1)S(1)} %get-tuple-element.70.vh_ref, bf16[2048,2048]{1,0:T(8,128)(2,1)S(1)} %get-tuple-element.71.vl_ref, ...), custom_call_target="tpu_custom_call", output_to_operand_aliasing={{0}: (0, {}), {1}: (1, {}), {2}: (4, {})} | custom-call | flops 1610612736 | tf_op jit(solution)/shard_map/contract/pallas_call | solution.py:127
  73.8 1.4 %order.4 = f32[512,8,128]{2,1,0:T(8,128)S(1)} custom-call(s32[2048]{0:T(1024)S(1)} %find.1.at_ref, f32[1024,8,128]{2,1,0:T(8,128)S(1)} %get-tuple-element.77.products), custom_call_target="tpu_custom_call" | custom-call | tf_op jit(solution)/shard_map/order/pallas_call | solution.py:229
  75.3 2.8 %contract.11 = (bf16[2048,2048]{1,0:T(8,128)(2,1)S(1)}, bf16[2048,2048]{1,0:T(8,128)(2,1)S(1)}, f32[1024,8,128]{2,1,0:T(8,128)S(1)}) custom-call(bf16[2048,2048]{1,0:T(8,128)(2,1)S(1)} %get-tuple-element.84.vh_ref, bf16[2048,2048]{1,0:T(8,128)(2,1)S(1)} %get-tuple-element.85.vl_ref, ...), custom_call_target="tpu_custom_call", output_to_operand_aliasing={{0}: (0, {}), {1}: (1, {}), {2}: (4, {})} | custom-call | flops 1610612736 | tf_op jit(solution)/shard_map/contract/pallas_call | solution.py:127
  78.1 1.4 %order.6 = f32[512,8,128]{2,1,0:T(8,128)S(1)} custom-call(s32[2048]{0:T(1024)S(1)} %find.1.at_ref, f32[1024,8,128]{2,1,0:T(8,128)S(1)} %get-tuple-element.88.products), custom_call_target="tpu_custom_call" | custom-call | tf_op jit(solution)/shard_map/order/pallas_call | solution.py:229
  79.5 0.8 collective-permute-start.17
  80.3 1.4 %order.5 = (f32[256,8,128]{2,1,0:T(8,128)S(1)}, f32[256,8,128]{2,1,0:T(8,128)S(1)}) custom-call(s32[2048]{0:T(1024)S(1)} %find.1.at_ref, f32[1024,8,128]{2,1,0:T(8,128)S(1)} %get-tuple-element.77.products, f32[512,8,128]{2,1,0:T(8,128)S(1)} %collective-permute-done.11.refs_0_), custom_call_target="tpu_custom_call" | custom-call | tf_op jit(solution)/shard_map/order/pallas_call | solution.py:229
  81.8 0.8 collective-permute-start.12
  82.5 1.6 %collective-permute-done.17.refs_0_ = f32[512,8,128]{2,1,0:T(8,128)S(1)} collective-permute-done((f32[512,8,128]{2,1,0:T(8,128)S(1)}, f32[512,8,128]{2,1,0:T(8,128)S(1)}, u32[]{:S(2)}, u32[]{:S(2)}) %collective-permute-start.17) | collective-permute-done | bytes 2097184 | tf_op jit(solution)/shard_map/ppermute | solution.py:30
  84.1 1.4 %order.7 = (f32[128,8,128]{2,1,0:T(8,128)S(1)}, f32[128,8,128]{2,1,0:T(8,128)S(1)}, f32[64,8,128]{2,1,0:T(8,128)S(1)}, f32[64,8,128]{2,1,0:T(8,128)S(1)}, f32[128,8,128]{2,1,0:T(8,128)S(1)}) custom-call(s32[2048]{0:T(1024)S(1)} %find.1.at_ref, f32[1024,8,128]{2,1,0:T(8,128)S(1)} %get-tuple-element.88.products, f32[512,8,128]{2,1,0:T(8,128)S(1)} %collective-permute-done.17.refs_0_), custom_call_target="tpu_custom_call" | custom-call | tf_op jit(solution)/shard_map/order/pallas_call | solution.py:229
  85.5 1.6 %collective-permute-start.18 = (f32[64,8,128]{2,1,0:T(8,128)S(1)}, f32[64,8,128]{2,1,0:T(8,128)S(1)}, u32[]{:S(2)}, u32[]{:S(2)}) collective-permute-start(f32[64,8,128]{2,1,0:T(8,128)S(1)} %get-tuple-element.91), channel_id=1, source_target_pairs={{0,4},{1,5},{16,20},{17,21},{32,36},{33,37},{48,52},{49,53},{2,6},... | collective-permute-start | bytes 786440 | tf_op jit(solution)/shard_map/ppermute | solution.py:30
  87.1 1.8 %collective-permute-start.19 = (f32[64,8,128]{2,1,0:T(8,128)S(1)}, f32[64,8,128]{2,1,0:T(8,128)S(1)}, u32[]{:S(2)}, u32[]{:S(2)}) collective-permute-start(f32[64,8,128]{2,1,0:T(8,128)S(1)} %get-tuple-element.92), channel_id=1, source_target_pairs={{0,12},{1,13},{16,28},{17,29},{32,44},{33,45},{48,60},{49,61},{2,1... | collective-permute-start | bytes 786440 | tf_op jit(solution)/shard_map/ppermute | solution.py:30
  88.8 6.5 %collective-permute-done.18 = f32[64,8,128]{2,1,0:T(8,128)S(1)} collective-permute-done((f32[64,8,128]{2,1,0:T(8,128)S(1)}, f32[64,8,128]{2,1,0:T(8,128)S(1)}, u32[]{:S(2)}, u32[]{:S(2)}) %collective-permute-start.18) | collective-permute-done | bytes 262176 | tf_op jit(solution)/shard_map/ppermute | solution.py:30
  95.4 3.0 %collective-permute-start.21 = (f32[128,8,128]{2,1,0:T(8,128)S(1)}, f32[128,8,128]{2,1,0:T(8,128)S(1)}, u32[]{:S(2)}, u32[]{:S(2)}) collective-permute-start(f32[128,8,128]{2,1,0:T(8,128)S(1)} %add_dynamic-update-slice_fusion), channel_id=1, source_target_pairs={{0,12},{1,13},{16,28},{17,29},{32,44},{33,45},{48,60},{49,61},{2,1... | collective-permute-start | bytes 1572872 | tf_op jit(solution)/shard_map/ppermute | solution.py:30
  98.6 8.3 %collective-permute-done.12 = f32[256,8,128]{2,1,0:T(8,128)S(1)} collective-permute-done((f32[256,8,128]{2,1,0:T(8,128)S(1)}, f32[256,8,128]{2,1,0:T(8,128)S(1)}, u32[]{:S(2)}, u32[]{:S(2)}) %collective-permute-start.12) | collective-permute-done | bytes 1048608 | tf_op jit(solution)/shard_map/ppermute | solution.py:30
  106.9 0.1 add.54
  107.1 1.6 %collective-permute-start.13 = (f32[32,8,128]{2,1,0:T(8,128)S(1)}, f32[32,8,128]{2,1,0:T(8,128)S(1)}, u32[]{:S(2)}, u32[]{:S(2)}) collective-permute-start(f32[32,8,128]{2,1,0:T(8,128)S(1)} %get-tuple-element.104), channel_id=1, source_target_pairs={{0,4},{1,5},{16,20},{17,21},{32,36},{33,37},{48,52},{49,53},{2,6},... | collective-permute-start | bytes 393224 | tf_op jit(solution)/shard_map/ppermute | solution.py:30
  108.6 1.8 %collective-permute-start.14 = (f32[32,8,128]{2,1,0:T(8,128)S(1)}, f32[32,8,128]{2,1,0:T(8,128)S(1)}, u32[]{:S(2)}, u32[]{:S(2)}) collective-permute-start(f32[32,8,128]{2,1,0:T(8,128)S(1)} %get-tuple-element.103), channel_id=1, source_target_pairs={{0,12},{1,13},{16,28},{17,29},{32,44},{33,45},{48,60},{49,61},{2,1... | collective-permute-start | bytes 393224 | tf_op jit(solution)/shard_map/ppermute | solution.py:30
  110.4 3.6 %collective-permute-done.20 = f32[128,8,128]{2,1,0:T(8,128)S(1)} collective-permute-done((f32[128,8,128]{2,1,0:T(8,128)S(1)}, f32[128,8,128]{2,1,0:T(8,128)S(1)}, u32[]{:S(2)}, u32[]{:S(2)}) %collective-permute-start.20) | collective-permute-done | bytes 524320 | tf_op jit(solution)/shard_map/ppermute | solution.py:30
  114.1 0.8 collective-permute-start.22
  114.9 0.5 collective-permute-done.13
  115.5 3.2 %collective-permute-start.16 = (f32[64,8,128]{2,1,0:T(8,128)S(1)}, f32[64,8,128]{2,1,0:T(8,128)S(1)}, u32[]{:S(2)}, u32[]{:S(2)}) collective-permute-start(f32[64,8,128]{2,1,0:T(8,128)S(1)} %get-tuple-element.100), channel_id=1, source_target_pairs={{0,12},{1,13},{16,28},{17,29},{32,44},{33,45},{48,60},{49,61},{2,1... | collective-permute-start | bytes 786440 | tf_op jit(solution)/shard_map/ppermute | solution.py:30
  118.7 1.8 %collective-permute-done.22 = f32[64,8,128]{2,1,0:T(8,128)S(1)} collective-permute-done((f32[64,8,128]{2,1,0:T(8,128)S(1)}, f32[64,8,128]{2,1,0:T(8,128)S(1)}, u32[]{:S(2)}, u32[]{:S(2)}) %collective-permute-start.22) | collective-permute-done | bytes 262176 | tf_op jit(solution)/shard_map/ppermute | solution.py:30
  120.6 2.4 %collective-permute-done.15 = f32[64,8,128]{2,1,0:T(8,128)S(1)} collective-permute-done((f32[64,8,128]{2,1,0:T(8,128)S(1)}, f32[64,8,128]{2,1,0:T(8,128)S(1)}, u32[]{:S(2)}, u32[]{:S(2)}) %collective-permute-start.15) | collective-permute-done | bytes 262176 | tf_op jit(solution)/shard_map/ppermute | solution.py:30
  123.2 0.8 pad_maximum_fusion
  (48 shorter events, 1.2 us)
Async XLA Ops:
  0.0 27.5 %collective-permute-start = (f32[2048,128]{1,0:T(8,128)}, f32[2048,128]{1,0:T(8,128)S(1)}, u32[]{:S(2)}, u32[]{:S(2)}) collective-permute-start(f32[2048,128]{1,0:T(8,128)} %a_ref.1), channel_id=1, source_target_pairs={{0,16},{1,17},{16,32},{17,33},{32,48},{33,49},{48,0},{49,1},{2,18}... | collective-permute-start | bytes 3145736 | tf_op jit(solution)/shard_map/ppermute | solution.py:30
  2.0 25.5 %collective-permute-start.1 = (f32[2048,128]{1,0:T(8,128)}, f32[2048,128]{1,0:T(8,128)S(1)}, u32[]{:S(2)}, u32[]{:S(2)}) collective-permute-start(f32[2048,128]{1,0:T(8,128)} %a_ref.1), channel_id=1, source_target_pairs={{0,48},{1,49},{16,0},{17,1},{32,16},{33,17},{48,32},{49,33},{2,50}... | collective-permute-start | bytes 3145736 | tf_op jit(solution)/shard_map/ppermute | solution.py:30
  4.1 26.4 %collective-permute-start.2 = (f32[2048,128]{1,0:T(8,128)}, f32[2048,128]{1,0:T(8,128)S(1)}, u32[]{:S(2)}, u32[]{:S(2)}) collective-permute-start(f32[2048,128]{1,0:T(8,128)} %a_ref.1), channel_id=1, source_target_pairs={{0,64},{1,65},{16,80},{17,81},{32,96},{33,97},{48,112},{49,113},{2... | collective-permute-start | bytes 3145736 | tf_op jit(solution)/shard_map/ppermute | solution.py:30
  15.6 1.2 copy-start
  30.6 17.7 %collective-permute-start.6 = (f32[1024,128]{1,0:T(8,128)S(1)}, f32[1024,128]{1,0:T(8,128)S(1)}, u32[]{:S(2)}, u32[]{:S(2)}) collective-permute-start(f32[1024,128]{1,0:T(8,128)S(1)} %get-tuple-element.68), channel_id=1, source_target_pairs={{0,64},{1,65},{16,80},{17,81},{32,96},{33,97},{48,112},{49,113},{2... | collective-permute-start | bytes 1572872 | tf_op jit(solution)/shard_map/ppermute | solution.py:30
  33.9 14.8 %collective-permute-start.3 = (f32[1024,128]{1,0:T(8,128)S(1)}, f32[1024,128]{1,0:T(8,128)S(1)}, u32[]{:S(2)}, u32[]{:S(2)}) collective-permute-start(f32[1024,128]{1,0:T(8,128)S(1)} %get-tuple-element.60), channel_id=1, source_target_pairs={{0,16},{1,17},{16,32},{17,33},{32,48},{33,49},{48,0},{49,1},{2,18}... | collective-permute-start | bytes 1572872 | tf_op jit(solution)/shard_map/ppermute | solution.py:30
  33.9 14.8 %collective-permute-start.4 = (f32[1024,128]{1,0:T(8,128)S(1)}, f32[1024,128]{1,0:T(8,128)S(1)}, u32[]{:S(2)}, u32[]{:S(2)}) collective-permute-start(f32[1024,128]{1,0:T(8,128)S(1)} %get-tuple-element.69), channel_id=1, source_target_pairs={{0,48},{1,49},{16,0},{17,1},{32,16},{33,17},{48,32},{49,33},{2,50}... | collective-permute-start | bytes 1572872 | tf_op jit(solution)/shard_map/ppermute | solution.py:30
  45.0 13.5 %collective-permute-start.5 = (f32[1024,128]{1,0:T(8,128)S(1)}, f32[1024,128]{1,0:T(8,128)S(1)}, u32[]{:S(2)}, u32[]{:S(2)}) collective-permute-start(f32[1024,128]{1,0:T(8,128)S(1)} %get-tuple-element.67), channel_id=1, source_target_pairs={{0,16},{1,17},{16,32},{17,33},{32,48},{33,49},{48,0},{49,1},{2,18}... | collective-permute-start | bytes 1572872 | tf_op jit(solution)/shard_map/ppermute | solution.py:30
  45.1 16.7 %collective-permute-start.7 = (f32[1024,128]{1,0:T(8,128)S(1)}, f32[1024,128]{1,0:T(8,128)S(1)}, u32[]{:S(2)}, u32[]{:S(2)}) collective-permute-start(f32[1024,128]{1,0:T(8,128)S(1)} %get-tuple-element.67), channel_id=1, source_target_pairs={{0,48},{1,49},{16,0},{17,1},{32,16},{33,17},{48,32},{49,33},{2,50}... | collective-permute-start | bytes 1572872 | tf_op jit(solution)/shard_map/ppermute | solution.py:30
  48.3 12.6 %collective-permute-start.8 = (f32[1024,128]{1,0:T(8,128)S(1)}, f32[1024,128]{1,0:T(8,128)S(1)}, u32[]{:S(2)}, u32[]{:S(2)}) collective-permute-start(f32[1024,128]{1,0:T(8,128)S(1)} %get-tuple-element.69), channel_id=1, source_target_pairs={{0,64},{1,65},{16,80},{17,81},{32,96},{33,97},{48,112},{49,113},{2... | collective-permute-start | bytes 1572872 | tf_op jit(solution)/shard_map/ppermute | solution.py:30
  58.5 12.5 %collective-permute-start.9 = (f32[1024,128]{1,0:T(8,128)S(1)}, f32[1024,128]{1,0:T(8,128)S(1)}, u32[]{:S(2)}, u32[]{:S(2)}) collective-permute-start(f32[1024,128]{1,0:T(8,128)S(1)} %collective-permute-done.5.refs_0_), channel_id=1, source_target_pairs={{0,16},{1,17},{16,32},{17,33},{32,48},{33,49},{48,0},{49,1},{2,18}... | collective-permute-start | bytes 1572872 | tf_op jit(solution)/shard_map/ppermute | solution.py:30
  60.9 10.1 %collective-permute-start.10 = (f32[1024,128]{1,0:T(8,128)S(1)}, f32[1024,128]{1,0:T(8,128)S(1)}, u32[]{:S(2)}, u32[]{:S(2)}) collective-permute-start(f32[1024,128]{1,0:T(8,128)S(1)} %collective-permute-done.8.refs_3_), channel_id=1, source_target_pairs={{0,48},{1,49},{16,0},{17,1},{32,16},{33,17},{48,32},{49,33},{2,50}... | collective-permute-start | bytes 1572872 | tf_op jit(solution)/shard_map/ppermute | solution.py:30
  75.2 5.1 %collective-permute-start.11 = (f32[512,8,128]{2,1,0:T(8,128)S(1)}, f32[512,8,128]{2,1,0:T(8,128)S(1)}, u32[]{:S(2)}, u32[]{:S(2)}) collective-permute-start(f32[512,8,128]{2,1,0:T(8,128)S(1)} %order.4), channel_id=1, source_target_pairs={{0,1},{1,0},{16,17},{17,16},{32,33},{33,32},{48,49},{49,48},{2,3},... | collective-permute-start | bytes 6291464 | tf_op jit(solution)/shard_map/ppermute | solution.py:30
  79.5 4.6 %collective-permute-start.17 = (f32[512,8,128]{2,1,0:T(8,128)S(1)}, f32[512,8,128]{2,1,0:T(8,128)S(1)}, u32[]{:S(2)}, u32[]{:S(2)}) collective-permute-start(f32[512,8,128]{2,1,0:T(8,128)S(1)} %order.6), channel_id=1, source_target_pairs={{0,1},{1,0},{16,17},{17,16},{32,33},{33,32},{48,49},{49,48},{2,3},... | collective-permute-start | bytes 6291464 | tf_op jit(solution)/shard_map/ppermute | solution.py:30
  81.8 25.2 %collective-permute-start.12 = (f32[256,8,128]{2,1,0:T(8,128)S(1)}, f32[256,8,128]{2,1,0:T(8,128)S(1)}, u32[]{:S(2)}, u32[]{:S(2)}) collective-permute-start(f32[256,8,128]{2,1,0:T(8,128)S(1)} %get-tuple-element.79), channel_id=1, source_target_pairs={{0,2},{1,3},{16,18},{17,19},{32,34},{33,35},{48,50},{49,51},{2,0},... | collective-permute-start | bytes 3145736 | tf_op jit(solution)/shard_map/ppermute | solution.py:30
  85.5 9.9 %collective-permute-start.18 = (f32[64,8,128]{2,1,0:T(8,128)S(1)}, f32[64,8,128]{2,1,0:T(8,128)S(1)}, u32[]{:S(2)}, u32[]{:S(2)}) collective-permute-start(f32[64,8,128]{2,1,0:T(8,128)S(1)} %get-tuple-element.91), channel_id=1, source_target_pairs={{0,4},{1,5},{16,20},{17,21},{32,36},{33,37},{48,52},{49,53},{2,6},... | collective-permute-start | bytes 786440 | tf_op jit(solution)/shard_map/ppermute | solution.py:30
  87.1 8.3 %collective-permute-start.19 = (f32[64,8,128]{2,1,0:T(8,128)S(1)}, f32[64,8,128]{2,1,0:T(8,128)S(1)}, u32[]{:S(2)}, u32[]{:S(2)}) collective-permute-start(f32[64,8,128]{2,1,0:T(8,128)S(1)} %get-tuple-element.92), channel_id=1, source_target_pairs={{0,12},{1,13},{16,28},{17,29},{32,44},{33,45},{48,60},{49,61},{2,1... | collective-permute-start | bytes 786440 | tf_op jit(solution)/shard_map/ppermute | solution.py:30
  95.4 14.9 %collective-permute-start.21 = (f32[128,8,128]{2,1,0:T(8,128)S(1)}, f32[128,8,128]{2,1,0:T(8,128)S(1)}, u32[]{:S(2)}, u32[]{:S(2)}) collective-permute-start(f32[128,8,128]{2,1,0:T(8,128)S(1)} %add_dynamic-update-slice_fusion), channel_id=1, source_target_pairs={{0,12},{1,13},{16,28},{17,29},{32,44},{33,45},{48,60},{49,61},{2,1... | collective-permute-start | bytes 1572872 | tf_op jit(solution)/shard_map/ppermute | solution.py:30
  98.5 15.5 %collective-permute-start.20 = (f32[128,8,128]{2,1,0:T(8,128)S(1)}, f32[128,8,128]{2,1,0:T(8,128)S(1)}, u32[]{:S(2)}, u32[]{:S(2)}) collective-permute-start(f32[128,8,128]{2,1,0:T(8,128)S(1)} %add_dynamic-update-slice_fusion.1), channel_id=1, source_target_pairs={{0,4},{1,5},{16,20},{17,21},{32,36},{33,37},{48,52},{49,53},{2,6},... | collective-permute-start | bytes 1572872 | tf_op jit(solution)/shard_map/ppermute | solution.py:30
  107.1 8.3 %collective-permute-start.13 = (f32[32,8,128]{2,1,0:T(8,128)S(1)}, f32[32,8,128]{2,1,0:T(8,128)S(1)}, u32[]{:S(2)}, u32[]{:S(2)}) collective-permute-start(f32[32,8,128]{2,1,0:T(8,128)S(1)} %get-tuple-element.104), channel_id=1, source_target_pairs={{0,4},{1,5},{16,20},{17,21},{32,36},{33,37},{48,52},{49,53},{2,6},... | collective-permute-start | bytes 393224 | tf_op jit(solution)/shard_map/ppermute | solution.py:30
  108.6 6.8 %collective-permute-start.14 = (f32[32,8,128]{2,1,0:T(8,128)S(1)}, f32[32,8,128]{2,1,0:T(8,128)S(1)}, u32[]{:S(2)}, u32[]{:S(2)}) collective-permute-start(f32[32,8,128]{2,1,0:T(8,128)S(1)} %get-tuple-element.103), channel_id=1, source_target_pairs={{0,12},{1,13},{16,28},{17,29},{32,44},{33,45},{48,60},{49,61},{2,1... | collective-permute-start | bytes 393224 | tf_op jit(solution)/shard_map/ppermute | solution.py:30
  114.1 6.5 %collective-permute-start.22 = (f32[64,8,128]{2,1,0:T(8,128)S(1)}, f32[64,8,128]{2,1,0:T(8,128)S(1)}, u32[]{:S(2)}, u32[]{:S(2)}) collective-permute-start(f32[64,8,128]{2,1,0:T(8,128)S(1)} %slice.94), channel_id=1, source_target_pairs={{0,2},{1,3},{16,18},{17,19},{32,34},{33,35},{48,50},{49,51},{2,0},... | collective-permute-start | bytes 786440 | tf_op jit(solution)/shard_map/ppermute | solution.py:30
  115.4 7.7 %collective-permute-start.15 = (f32[64,8,128]{2,1,0:T(8,128)S(1)}, f32[64,8,128]{2,1,0:T(8,128)S(1)}, u32[]{:S(2)}, u32[]{:S(2)}) collective-permute-start(f32[64,8,128]{2,1,0:T(8,128)S(1)} %get-tuple-element.99), channel_id=1, source_target_pairs={{0,4},{1,5},{16,20},{17,21},{32,36},{33,37},{48,52},{49,53},{2,6},... | collective-permute-start | bytes 786440 | tf_op jit(solution)/shard_map/ppermute | solution.py:30
  115.5 7.6 %collective-permute-start.16 = (f32[64,8,128]{2,1,0:T(8,128)S(1)}, f32[64,8,128]{2,1,0:T(8,128)S(1)}, u32[]{:S(2)}, u32[]{:S(2)}) collective-permute-start(f32[64,8,128]{2,1,0:T(8,128)S(1)} %get-tuple-element.100), channel_id=1, source_target_pairs={{0,12},{1,13},{16,28},{17,29},{32,44},{33,45},{48,60},{49,61},{2,1... | collective-permute-start | bytes 786440 | tf_op jit(solution)/shard_map/ppermute | solution.py:30

commit v5 on v4

--- a/solution.py
+++ b/solution.py
@@ -247,12 +247,11 @@
     at = find(held, wanted)
     v, own = contract([after(v, at)], ([a],))
 
-    zm_low, zm_high, zp_high, y0_low = pack(
-        *(((block, row, mid),) for block, row in ((after(zm, own), 0), (zm, mid), (zp, mid), (y0, 0)))
-    )
+    zm_low, zm_high, zp_high = pack(*(((block, row, mid),) for block, row in ((after(zm, own), 0), (zm, mid), (zp, mid))))
     y_zm_high, z2_low, z2_high = shift(zm_high, dy=2), shift(zm_low, dz=1), shift(zp_high, dz=-1)
     v, near = contract(v, ([zm], [zp]))
 
+    (y0_low,) = pack(((after(y0, near), 0, mid),))
     y_zm_low, y_zp_low = shift(after(y0_low, near), dz=1), shift(after(y0_low, near), dz=-1)
     y_zp_high = shift(after(zp_high, near, y_zm_high), dy=2)
     v, far = contract(v, ([y0], [z2_low, z2_high]))

time: 125 us -> 123 us (0.984)
  waiting for transfers between devices: 35.4 us -> 33.8 us
    ppermute x23, waiting for transfers between devices: 35.4 us -> 33.8 us  [shift(): return lax.ppermute(array, AXES, pairs)]
  transfers between devices with their start and end apart: 23 -> 23, of which waited for: 12 -> 12; matrix products, arithmetic and copies ran while one was open for 2% -> 2% of each run, Pallas kernels for 37% -> 38%
where the time goes in v5:
time: 123 us; the launch traced here: 122 us
  Pallas kernels  50.1 us (41%)
  waiting for transfers between devices  33.8 us (27%)
  starting transfers between devices  33.7 us (27%)
  local copies, waits for them, and re-layouts  2.4 us (2%)
  other arithmetic  2.07 us (2%)
    pallas_call x6, Pallas kernels, contract(): pl.pallas_call(kernel, in_specs=[pl.BlockSpec(memory_space=pl.ANY) if fre...  37.5 us
    ppermute x23, waiting for transfers between devices, shift(): return lax.ppermute(array, AXES, pairs)  33.8 us
    ppermute x23, starting transfers between devices, shift(): return lax.ppermute(array, AXES, pairs)  33.7 us
    pallas_call x1, Pallas kernels, find(): pl.pallas_call(find_kernel, in_specs=[SCALARS] * 2, out_specs=SCALARS, ou...  6.36 us
    pallas_call x4, Pallas kernels, order(): pl.pallas_call(functools.partial(order_kernel, first, len(got)), in_specs...  5.61 us
  transfers between devices with their start and end apart: 23, of which 12 were waited for; matrix products, arithmetic and copies ran while one was open for 2% of the time, Pallas kernels for 38%

profile of v5, /device:TPU:0, one launch (start us, length us, event | category | flops | bytes accessed | tf_op | source)
XLA Modules:
  0.0 122.4 jit_solution(10442626723640729601)
XLA Ops:
  0.0 2.0 %collective-permute-start = (f32[2048,128]{1,0:T(8,128)}, f32[2048,128]{1,0:T(8,128)S(1)}, u32[]{:S(2)}, u32[]{:S(2)}) collective-permute-start(f32[2048,128]{1,0:T(8,128)} %a_ref.1), channel_id=1, source_target_pairs={{0,16},{1,17},{16,32},{17,33},{32,48},{33,49},{48,0},{49,1},{2,18}... | collective-permute-start | bytes 3145736 | tf_op jit(solution)/shard_map/ppermute | solution.py:30
  2.0 2.1 %collective-permute-start.1 = (f32[2048,128]{1,0:T(8,128)}, f32[2048,128]{1,0:T(8,128)S(1)}, u32[]{:S(2)}, u32[]{:S(2)}) collective-permute-start(f32[2048,128]{1,0:T(8,128)} %a_ref.1), channel_id=1, source_target_pairs={{0,48},{1,49},{16,0},{17,1},{32,16},{33,17},{48,32},{49,33},{2,50}... | collective-permute-start | bytes 3145736 | tf_op jit(solution)/shard_map/ppermute | solution.py:30
  4.1 3.2 %collective-permute-start.2 = (f32[2048,128]{1,0:T(8,128)}, f32[2048,128]{1,0:T(8,128)S(1)}, u32[]{:S(2)}, u32[]{:S(2)}) collective-permute-start(f32[2048,128]{1,0:T(8,128)} %a_ref.1), channel_id=1, source_target_pairs={{0,64},{1,65},{16,80},{17,81},{32,96},{33,97},{48,112},{49,113},{2... | collective-permute-start | bytes 3145736 | tf_op jit(solution)/shard_map/ppermute | solution.py:30
  7.3 0.8 reshape.19
  8.2 0.8 fusion.4
  9.3 6.4 %find.1.at_ref = s32[2048]{0:T(1024)S(1)} custom-call(s32[1024]{0:T(1024)S(1)} %constant_dynamic-update-slice_fusion.held_ref, s32[2048]{0:T(1024)S(1)} %pad_add_fusion.wanted_ref), custom_call_target="tpu_custom_call" | custom-call | tf_op jit(solution)/shard_map/find/pallas_call | solution.py:200
  15.7 1.2 copy-done
  16.9 8.2 %contract.6 = (bf16[2048,2048]{1,0:T(8,128)(2,1)S(1)}, bf16[2048,2048]{1,0:T(8,128)(2,1)S(1)}, f32[128,8,128]{2,1,0:T(8,128)S(1)}, f32[128,8,128]{2,1,0:T(8,128)S(1)}) custom-call(f32[2048,2048]{1,0:T(8,128)} %v_hbm, f32[2048,128]{1,0:T(8,128)S(1)} %copy-done), custom_call_target="tpu_custom_call" | custom-call | flops 3221225472 | tf_op jit(solution)/shard_map/contract/pallas_call | solution.py:127
  25.1 2.4 %collective-permute-done.refs_0_.refs_1_ = f32[2048,128]{1,0:T(8,128)S(1)} collective-permute-done((f32[2048,128]{1,0:T(8,128)}, f32[2048,128]{1,0:T(8,128)S(1)}, u32[]{:S(2)}, u32[]{:S(2)}) %collective-permute-start) | collective-permute-done | bytes 1048608 | tf_op jit(solution)/shard_map/ppermute | solution.py:30
  27.6 3.3 %collective-permute-start.6 = (f32[1024,128]{1,0:T(8,128)S(1)}, f32[1024,128]{1,0:T(8,128)S(1)}, u32[]{:S(2)}, u32[]{:S(2)}) collective-permute-start(f32[1024,128]{1,0:T(8,128)S(1)} %get-tuple-element.68), channel_id=1, source_target_pairs={{0,64},{1,65},{16,80},{17,81},{32,96},{33,97},{48,112},{49,113},{2... | collective-permute-start | bytes 1572872 | tf_op jit(solution)/shard_map/ppermute | solution.py:30
  30.9 1.3 %collective-permute-start.3 = (f32[1024,128]{1,0:T(8,128)S(1)}, f32[1024,128]{1,0:T(8,128)S(1)}, u32[]{:S(2)}, u32[]{:S(2)}) collective-permute-start(f32[1024,128]{1,0:T(8,128)S(1)} %get-tuple-element.60), channel_id=1, source_target_pairs={{0,16},{1,17},{16,32},{17,33},{32,48},{33,49},{48,0},{49,1},{2,18}... | collective-permute-start | bytes 1572872 | tf_op jit(solution)/shard_map/ppermute | solution.py:30
  32.1 2.0 %collective-permute-start.4 = (f32[1024,128]{1,0:T(8,128)S(1)}, f32[1024,128]{1,0:T(8,128)S(1)}, u32[]{:S(2)}, u32[]{:S(2)}) collective-permute-start(f32[1024,128]{1,0:T(8,128)S(1)} %get-tuple-element.69), channel_id=1, source_target_pairs={{0,48},{1,49},{16,0},{17,1},{32,16},{33,17},{48,32},{49,33},{2,50}... | collective-permute-start | bytes 1572872 | tf_op jit(solution)/shard_map/ppermute | solution.py:30
  34.1 7.9 %contract.7 = (bf16[2048,2048]{1,0:T(8,128)(2,1)S(1)}, bf16[2048,2048]{1,0:T(8,128)(2,1)S(1)}, f32[256,8,128]{2,1,0:T(8,128)S(1)}, f32[256,8,128]{2,1,0:T(8,128)S(1)}) custom-call(bf16[2048,2048]{1,0:T(8,128)(2,1)S(1)} %get-tuple-element.53.vh_ref, bf16[2048,2048]{1,0:T(8,128)(2,1)S(1)} %get-tuple-element.54.vl_ref, ...), custom_call_target="tpu_custom_call", output_to_operand_aliasing={{0}: (0, {}), {1}: (1, {})} | custom-call | flops 6442450944 | tf_op jit(solution)/shard_map/contract/pallas_call | solution.py:127
  42.1 0.1 collective-permute-start.5
  42.2 3.2 %collective-permute-start.7 = (f32[1024,128]{1,0:T(8,128)S(1)}, f32[1024,128]{1,0:T(8,128)S(1)}, u32[]{:S(2)}, u32[]{:S(2)}) collective-permute-start(f32[1024,128]{1,0:T(8,128)S(1)} %pack.3), channel_id=1, source_target_pairs={{0,48},{1,49},{16,0},{17,1},{32,16},{33,17},{48,32},{49,33},{2,50}... | collective-permute-start | bytes 1572872 | tf_op jit(solution)/shard_map/ppermute | solution.py:30
  45.4 0.3 collective-permute-start.8
  45.7 7.9 %contract.8 = (bf16[2048,2048]{1,0:T(8,128)(2,1)S(1)}, bf16[2048,2048]{1,0:T(8,128)(2,1)S(1)}, f32[256,8,128]{2,1,0:T(8,128)S(1)}, f32[256,8,128]{2,1,0:T(8,128)S(1)}) custom-call(bf16[2048,2048]{1,0:T(8,128)(2,1)S(1)} %get-tuple-element.55.vh_ref, bf16[2048,2048]{1,0:T(8,128)(2,1)S(1)} %get-tuple-element.56.vl_ref, ...), custom_call_target="tpu_custom_call", output_to_operand_aliasing={{0}: (0, {}), {1}: (1, {})} | custom-call | flops 6442450944 | tf_op jit(solution)/shard_map/contract/pallas_call | solution.py:127
  53.6 2.5 %collective-permute-done.5.refs_0_ = f32[1024,128]{1,0:T(8,128)S(1)} collective-permute-done((f32[1024,128]{1,0:T(8,128)S(1)}, f32[1024,128]{1,0:T(8,128)S(1)}, u32[]{:S(2)}, u32[]{:S(2)}) %collective-permute-start.5) | collective-permute-done | bytes 524320 | tf_op jit(solution)/shard_map/ppermute | solution.py:30
  56.2 2.4 %collective-permute-done.8.refs_3_ = f32[1024,128]{1,0:T(8,128)S(1)} collective-permute-done((f32[1024,128]{1,0:T(8,128)S(1)}, f32[1024,128]{1,0:T(8,128)S(1)}, u32[]{:S(2)}, u32[]{:S(2)}) %collective-permute-start.8) | collective-permute-done | bytes 524320 | tf_op jit(solution)/shard_map/ppermute | solution.py:30
  58.6 0.8 collective-permute-start.10
  59.4 7.9 %contract.9 = (bf16[2048,2048]{1,0:T(8,128)(2,1)S(1)}, bf16[2048,2048]{1,0:T(8,128)(2,1)S(1)}, f32[256,8,128]{2,1,0:T(8,128)S(1)}, f32[256,8,128]{2,1,0:T(8,128)S(1)}) custom-call(bf16[2048,2048]{1,0:T(8,128)(2,1)S(1)} %get-tuple-element.62.vh_ref, bf16[2048,2048]{1,0:T(8,128)(2,1)S(1)} %get-tuple-element.63.vl_ref, ...), custom_call_target="tpu_custom_call", output_to_operand_aliasing={{0}: (0, {}), {1}: (1, {})} | custom-call | flops 6442450944 | tf_op jit(solution)/shard_map/contract/pallas_call | solution.py:127
  67.3 0.2 merge.2.refs_2_
  67.6 0.2 merge.3.refs_2_
  67.8 1.4 %collective-permute-done.9.refs_0_ = f32[1024,128]{1,0:T(8,128)S(1)} collective-permute-done((f32[1024,128]{1,0:T(8,128)S(1)}, f32[1024,128]{1,0:T(8,128)S(1)}, u32[]{:S(2)}, u32[]{:S(2)}) %collective-permute-start.9) | collective-permute-done | bytes 524320 | tf_op jit(solution)/shard_map/ppermute | solution.py:30
  69.2 0.2 collective-permute-done.10.refs_1_
  69.4 2.8 %contract.10 = (bf16[2048,2048]{1,0:T(8,128)(2,1)S(1)}, bf16[2048,2048]{1,0:T(8,128)(2,1)S(1)}, f32[1024,8,128]{2,1,0:T(8,128)S(1)}) custom-call(bf16[2048,2048]{1,0:T(8,128)(2,1)S(1)} %get-tuple-element.70.vh_ref, bf16[2048,2048]{1,0:T(8,128)(2,1)S(1)} %get-tuple-element.71.vl_ref, ...), custom_call_target="tpu_custom_call", output_to_operand_aliasing={{0}: (0, {}), {1}: (1, {}), {2}: (4, {})} | custom-call | flops 1610612736 | tf_op jit(solution)/shard_map/contract/pallas_call | solution.py:127
  72.2 1.4 %order.4 = f32[512,8,128]{2,1,0:T(8,128)S(1)} custom-call(s32[2048]{0:T(1024)S(1)} %find.1.at_ref, f32[1024,8,128]{2,1,0:T(8,128)S(1)} %get-tuple-element.77.products), custom_call_target="tpu_custom_call" | custom-call | tf_op jit(solution)/shard_map/order/pallas_call | solution.py:229
  73.7 2.8 %contract.11 = (bf16[2048,2048]{1,0:T(8,128)(2,1)S(1)}, bf16[2048,2048]{1,0:T(8,128)(2,1)S(1)}, f32[1024,8,128]{2,1,0:T(8,128)S(1)}) custom-call(bf16[2048,2048]{1,0:T(8,128)(2,1)S(1)} %get-tuple-element.84.vh_ref, bf16[2048,2048]{1,0:T(8,128)(2,1)S(1)} %get-tuple-element.85.vl_ref, ...), custom_call_target="tpu_custom_call", output_to_operand_aliasing={{0}: (0, {}), {1}: (1, {}), {2}: (4, {})} | custom-call | flops 1610612736 | tf_op jit(solution)/shard_map/contract/pallas_call | solution.py:127
  76.4 1.4 %order.6 = f32[512,8,128]{2,1,0:T(8,128)S(1)} custom-call(s32[2048]{0:T(1024)S(1)} %find.1.at_ref, f32[1024,8,128]{2,1,0:T(8,128)S(1)} %get-tuple-element.88.products), custom_call_target="tpu_custom_call" | custom-call | tf_op jit(solution)/shard_map/order/pallas_call | solution.py:229
  77.8 0.8 collective-permute-start.17
  78.7 1.4 %order.5 = (f32[256,8,128]{2,1,0:T(8,128)S(1)}, f32[256,8,128]{2,1,0:T(8,128)S(1)}) custom-call(s32[2048]{0:T(1024)S(1)} %find.1.at_ref, f32[1024,8,128]{2,1,0:T(8,128)S(1)} %get-tuple-element.77.products, f32[512,8,128]{2,1,0:T(8,128)S(1)} %collective-permute-done.11.refs_0_), custom_call_target="tpu_custom_call" | custom-call | tf_op jit(solution)/shard_map/order/pallas_call | solution.py:229
  80.1 0.8 collective-permute-start.12
  80.8 1.6 %collective-permute-done.17.refs_0_ = f32[512,8,128]{2,1,0:T(8,128)S(1)} collective-permute-done((f32[512,8,128]{2,1,0:T(8,128)S(1)}, f32[512,8,128]{2,1,0:T(8,128)S(1)}, u32[]{:S(2)}, u32[]{:S(2)}) %collective-permute-start.17) | collective-permute-done | bytes 2097184 | tf_op jit(solution)/shard_map/ppermute | solution.py:30
  82.5 1.4 %order.7 = (f32[128,8,128]{2,1,0:T(8,128)S(1)}, f32[128,8,128]{2,1,0:T(8,128)S(1)}, f32[64,8,128]{2,1,0:T(8,128)S(1)}, f32[64,8,128]{2,1,0:T(8,128)S(1)}, f32[128,8,128]{2,1,0:T(8,128)S(1)}) custom-call(s32[2048]{0:T(1024)S(1)} %find.1.at_ref, f32[1024,8,128]{2,1,0:T(8,128)S(1)} %get-tuple-element.88.products, f32[512,8,128]{2,1,0:T(8,128)S(1)} %collective-permute-done.17.refs_0_), custom_call_target="tpu_custom_call" | custom-call | tf_op jit(solution)/shard_map/order/pallas_call | solution.py:229
  83.8 1.6 %collective-permute-start.18 = (f32[64,8,128]{2,1,0:T(8,128)S(1)}, f32[64,8,128]{2,1,0:T(8,128)S(1)}, u32[]{:S(2)}, u32[]{:S(2)}) collective-permute-start(f32[64,8,128]{2,1,0:T(8,128)S(1)} %get-tuple-element.91), channel_id=1, source_target_pairs={{0,4},{1,5},{16,20},{17,21},{32,36},{33,37},{48,52},{49,53},{2,6},... | collective-permute-start | bytes 786440 | tf_op jit(solution)/shard_map/ppermute | solution.py:30
  85.4 1.8 %collective-permute-start.19 = (f32[64,8,128]{2,1,0:T(8,128)S(1)}, f32[64,8,128]{2,1,0:T(8,128)S(1)}, u32[]{:S(2)}, u32[]{:S(2)}) collective-permute-start(f32[64,8,128]{2,1,0:T(8,128)S(1)} %get-tuple-element.92), channel_id=1, source_target_pairs={{0,12},{1,13},{16,28},{17,29},{32,44},{33,45},{48,60},{49,61},{2,1... | collective-permute-start | bytes 786440 | tf_op jit(solution)/shard_map/ppermute | solution.py:30
  87.2 6.5 %collective-permute-done.18 = f32[64,8,128]{2,1,0:T(8,128)S(1)} collective-permute-done((f32[64,8,128]{2,1,0:T(8,128)S(1)}, f32[64,8,128]{2,1,0:T(8,128)S(1)}, u32[]{:S(2)}, u32[]{:S(2)}) %collective-permute-start.18) | collective-permute-done | bytes 262176 | tf_op jit(solution)/shard_map/ppermute | solution.py:30
  93.8 3.0 %collective-permute-start.21 = (f32[128,8,128]{2,1,0:T(8,128)S(1)}, f32[128,8,128]{2,1,0:T(8,128)S(1)}, u32[]{:S(2)}, u32[]{:S(2)}) collective-permute-start(f32[128,8,128]{2,1,0:T(8,128)S(1)} %add_dynamic-update-slice_fusion), channel_id=1, source_target_pairs={{0,12},{1,13},{16,28},{17,29},{32,44},{33,45},{48,60},{49,61},{2,1... | collective-permute-start | bytes 1572872 | tf_op jit(solution)/shard_map/ppermute | solution.py:30
  96.9 8.3 %collective-permute-done.12 = f32[256,8,128]{2,1,0:T(8,128)S(1)} collective-permute-done((f32[256,8,128]{2,1,0:T(8,128)S(1)}, f32[256,8,128]{2,1,0:T(8,128)S(1)}, u32[]{:S(2)}, u32[]{:S(2)}) %collective-permute-start.12) | collective-permute-done | bytes 1048608 | tf_op jit(solution)/shard_map/ppermute | solution.py:30
  105.4 1.6 %collective-permute-start.13 = (f32[32,8,128]{2,1,0:T(8,128)S(1)}, f32[32,8,128]{2,1,0:T(8,128)S(1)}, u32[]{:S(2)}, u32[]{:S(2)}) collective-permute-start(f32[32,8,128]{2,1,0:T(8,128)S(1)} %get-tuple-element.104), channel_id=1, source_target_pairs={{0,4},{1,5},{16,20},{17,21},{32,36},{33,37},{48,52},{49,53},{2,6},... | collective-permute-start | bytes 393224 | tf_op jit(solution)/shard_map/ppermute | solution.py:30
  107.0 1.8 %collective-permute-start.14 = (f32[32,8,128]{2,1,0:T(8,128)S(1)}, f32[32,8,128]{2,1,0:T(8,128)S(1)}, u32[]{:S(2)}, u32[]{:S(2)}) collective-permute-start(f32[32,8,128]{2,1,0:T(8,128)S(1)} %get-tuple-element.103), channel_id=1, source_target_pairs={{0,12},{1,13},{16,28},{17,29},{32,44},{33,45},{48,60},{49,61},{2,1... | collective-permute-start | bytes 393224 | tf_op jit(solution)/shard_map/ppermute | solution.py:30
  108.7 3.6 %collective-permute-done.20 = f32[128,8,128]{2,1,0:T(8,128)S(1)} collective-permute-done((f32[128,8,128]{2,1,0:T(8,128)S(1)}, f32[128,8,128]{2,1,0:T(8,128)S(1)}, u32[]{:S(2)}, u32[]{:S(2)}) %collective-permute-start.20) | collective-permute-done | bytes 524320 | tf_op jit(solution)/shard_map/ppermute | solution.py:30
  112.4 0.8 collective-permute-start.22
  113.2 0.5 collective-permute-done.13
  113.8 3.2 %collective-permute-start.16 = (f32[64,8,128]{2,1,0:T(8,128)S(1)}, f32[64,8,128]{2,1,0:T(8,128)S(1)}, u32[]{:S(2)}, u32[]{:S(2)}) collective-permute-start(f32[64,8,128]{2,1,0:T(8,128)S(1)} %get-tuple-element.100), channel_id=1, source_target_pairs={{0,12},{1,13},{16,28},{17,29},{32,44},{33,45},{48,60},{49,61},{2,1... | collective-permute-start | bytes 786440 | tf_op jit(solution)/shard_map/ppermute | solution.py:30
  117.1 1.8 %collective-permute-done.22 = f32[64,8,128]{2,1,0:T(8,128)S(1)} collective-permute-done((f32[64,8,128]{2,1,0:T(8,128)S(1)}, f32[64,8,128]{2,1,0:T(8,128)S(1)}, u32[]{:S(2)}, u32[]{:S(2)}) %collective-permute-start.22) | collective-permute-done | bytes 262176 | tf_op jit(solution)/shard_map/ppermute | solution.py:30
  119.0 2.4 %collective-permute-done.15 = f32[64,8,128]{2,1,0:T(8,128)S(1)} collective-permute-done((f32[64,8,128]{2,1,0:T(8,128)S(1)}, f32[64,8,128]{2,1,0:T(8,128)S(1)}, u32[]{:S(2)}, u32[]{:S(2)}) %collective-permute-start.15) | collective-permute-done | bytes 262176 | tf_op jit(solution)/shard_map/ppermute | solution.py:30
  121.5 0.8 pad_maximum_fusion
  (49 shorter events, 1.3 us)
Async XLA Ops:
  0.0 27.5 %collective-permute-start = (f32[2048,128]{1,0:T(8,128)}, f32[2048,128]{1,0:T(8,128)S(1)}, u32[]{:S(2)}, u32[]{:S(2)}) collective-permute-start(f32[2048,128]{1,0:T(8,128)} %a_ref.1), channel_id=1, source_target_pairs={{0,16},{1,17},{16,32},{17,33},{32,48},{33,49},{48,0},{49,1},{2,18}... | collective-permute-start | bytes 3145736 | tf_op jit(solution)/shard_map/ppermute | solution.py:30
  2.0 25.5 %collective-permute-start.1 = (f32[2048,128]{1,0:T(8,128)}, f32[2048,128]{1,0:T(8,128)S(1)}, u32[]{:S(2)}, u32[]{:S(2)}) collective-permute-start(f32[2048,128]{1,0:T(8,128)} %a_ref.1), channel_id=1, source_target_pairs={{0,48},{1,49},{16,0},{17,1},{32,16},{33,17},{48,32},{49,33},{2,50}... | collective-permute-start | bytes 3145736 | tf_op jit(solution)/shard_map/ppermute | solution.py:30
  4.1 37.9 %collective-permute-start.2 = (f32[2048,128]{1,0:T(8,128)}, f32[2048,128]{1,0:T(8,128)S(1)}, u32[]{:S(2)}, u32[]{:S(2)}) collective-permute-start(f32[2048,128]{1,0:T(8,128)} %a_ref.1), channel_id=1, source_target_pairs={{0,64},{1,65},{16,80},{17,81},{32,96},{33,97},{48,112},{49,113},{2... | collective-permute-start | bytes 3145736 | tf_op jit(solution)/shard_map/ppermute | solution.py:30
  15.7 1.2 %copy-start = (f32[2048,128]{1,0:T(8,128)S(1)}, f32[2048,128]{1,0:T(8,128)}, u32[]{:S(2)}) copy-start(f32[2048,128]{1,0:T(8,128)} %a_ref.1) | copy-start | bytes 3145732
  27.6 17.8 %collective-permute-start.6 = (f32[1024,128]{1,0:T(8,128)S(1)}, f32[1024,128]{1,0:T(8,128)S(1)}, u32[]{:S(2)}, u32[]{:S(2)}) collective-permute-start(f32[1024,128]{1,0:T(8,128)S(1)} %get-tuple-element.68), channel_id=1, source_target_pairs={{0,64},{1,65},{16,80},{17,81},{32,96},{33,97},{48,112},{49,113},{2... | collective-permute-start | bytes 1572872 | tf_op jit(solution)/shard_map/ppermute | solution.py:30
  30.9 14.9 %collective-permute-start.3 = (f32[1024,128]{1,0:T(8,128)S(1)}, f32[1024,128]{1,0:T(8,128)S(1)}, u32[]{:S(2)}, u32[]{:S(2)}) collective-permute-start(f32[1024,128]{1,0:T(8,128)S(1)} %get-tuple-element.60), channel_id=1, source_target_pairs={{0,16},{1,17},{16,32},{17,33},{32,48},{33,49},{48,0},{49,1},{2,18}... | collective-permute-start | bytes 1572872 | tf_op jit(solution)/shard_map/ppermute | solution.py:30
  32.1 13.6 %collective-permute-start.4 = (f32[1024,128]{1,0:T(8,128)S(1)}, f32[1024,128]{1,0:T(8,128)S(1)}, u32[]{:S(2)}, u32[]{:S(2)}) collective-permute-start(f32[1024,128]{1,0:T(8,128)S(1)} %get-tuple-element.69), channel_id=1, source_target_pairs={{0,48},{1,49},{16,0},{17,1},{32,16},{33,17},{48,32},{49,33},{2,50}... | collective-permute-start | bytes 1572872 | tf_op jit(solution)/shard_map/ppermute | solution.py:30
  42.1 14.1 %collective-permute-start.5 = (f32[1024,128]{1,0:T(8,128)S(1)}, f32[1024,128]{1,0:T(8,128)S(1)}, u32[]{:S(2)}, u32[]{:S(2)}) collective-permute-start(f32[1024,128]{1,0:T(8,128)S(1)} %pack.3), channel_id=1, source_target_pairs={{0,16},{1,17},{16,32},{17,33},{32,48},{33,49},{48,0},{49,1},{2,18}... | collective-permute-start | bytes 1572872 | tf_op jit(solution)/shard_map/ppermute | solution.py:30
  42.2 17.2 %collective-permute-start.7 = (f32[1024,128]{1,0:T(8,128)S(1)}, f32[1024,128]{1,0:T(8,128)S(1)}, u32[]{:S(2)}, u32[]{:S(2)}) collective-permute-start(f32[1024,128]{1,0:T(8,128)S(1)} %pack.3), channel_id=1, source_target_pairs={{0,48},{1,49},{16,0},{17,1},{32,16},{33,17},{48,32},{49,33},{2,50}... | collective-permute-start | bytes 1572872 | tf_op jit(solution)/shard_map/ppermute | solution.py:30
  45.4 13.2 %collective-permute-start.8 = (f32[1024,128]{1,0:T(8,128)S(1)}, f32[1024,128]{1,0:T(8,128)S(1)}, u32[]{:S(2)}, u32[]{:S(2)}) collective-permute-start(f32[1024,128]{1,0:T(8,128)S(1)} %get-tuple-element.69), channel_id=1, source_target_pairs={{0,64},{1,65},{16,80},{17,81},{32,96},{33,97},{48,112},{49,113},{2... | collective-permute-start | bytes 1572872 | tf_op jit(solution)/shard_map/ppermute | solution.py:30
  56.1 13.1 %collective-permute-start.9 = (f32[1024,128]{1,0:T(8,128)S(1)}, f32[1024,128]{1,0:T(8,128)S(1)}, u32[]{:S(2)}, u32[]{:S(2)}) collective-permute-start(f32[1024,128]{1,0:T(8,128)S(1)} %collective-permute-done.5.refs_0_), channel_id=1, source_target_pairs={{0,16},{1,17},{16,32},{17,33},{32,48},{33,49},{48,0},{49,1},{2,18}... | collective-permute-start | bytes 1572872 | tf_op jit(solution)/shard_map/ppermute | solution.py:30
  58.6 10.8 %collective-permute-start.10 = (f32[1024,128]{1,0:T(8,128)S(1)}, f32[1024,128]{1,0:T(8,128)S(1)}, u32[]{:S(2)}, u32[]{:S(2)}) collective-permute-start(f32[1024,128]{1,0:T(8,128)S(1)} %collective-permute-done.8.refs_3_), channel_id=1, source_target_pairs={{0,48},{1,49},{16,0},{17,1},{32,16},{33,17},{48,32},{49,33},{2,50}... | collective-permute-start | bytes 1572872 | tf_op jit(solution)/shard_map/ppermute | solution.py:30
  73.6 5.1 %collective-permute-start.11 = (f32[512,8,128]{2,1,0:T(8,128)S(1)}, f32[512,8,128]{2,1,0:T(8,128)S(1)}, u32[]{:S(2)}, u32[]{:S(2)}) collective-permute-start(f32[512,8,128]{2,1,0:T(8,128)S(1)} %order.4), channel_id=1, source_target_pairs={{0,1},{1,0},{16,17},{17,16},{32,33},{33,32},{48,49},{49,48},{2,3},... | collective-permute-start | bytes 6291464 | tf_op jit(solution)/shard_map/ppermute | solution.py:30
  77.8 4.6 %collective-permute-start.17 = (f32[512,8,128]{2,1,0:T(8,128)S(1)}, f32[512,8,128]{2,1,0:T(8,128)S(1)}, u32[]{:S(2)}, u32[]{:S(2)}) collective-permute-start(f32[512,8,128]{2,1,0:T(8,128)S(1)} %order.6), channel_id=1, source_target_pairs={{0,1},{1,0},{16,17},{17,16},{32,33},{33,32},{48,49},{49,48},{2,3},... | collective-permute-start | bytes 6291464 | tf_op jit(solution)/shard_map/ppermute | solution.py:30
  80.1 25.2 %collective-permute-start.12 = (f32[256,8,128]{2,1,0:T(8,128)S(1)}, f32[256,8,128]{2,1,0:T(8,128)S(1)}, u32[]{:S(2)}, u32[]{:S(2)}) collective-permute-start(f32[256,8,128]{2,1,0:T(8,128)S(1)} %get-tuple-element.79), channel_id=1, source_target_pairs={{0,2},{1,3},{16,18},{17,19},{32,34},{33,35},{48,50},{49,51},{2,0},... | collective-permute-start | bytes 3145736 | tf_op jit(solution)/shard_map/ppermute | solution.py:30
  83.8 9.9 %collective-permute-start.18 = (f32[64,8,128]{2,1,0:T(8,128)S(1)}, f32[64,8,128]{2,1,0:T(8,128)S(1)}, u32[]{:S(2)}, u32[]{:S(2)}) collective-permute-start(f32[64,8,128]{2,1,0:T(8,128)S(1)} %get-tuple-element.91), channel_id=1, source_target_pairs={{0,4},{1,5},{16,20},{17,21},{32,36},{33,37},{48,52},{49,53},{2,6},... | collective-permute-start | bytes 786440 | tf_op jit(solution)/shard_map/ppermute | solution.py:30
  85.4 8.3 %collective-permute-start.19 = (f32[64,8,128]{2,1,0:T(8,128)S(1)}, f32[64,8,128]{2,1,0:T(8,128)S(1)}, u32[]{:S(2)}, u32[]{:S(2)}) collective-permute-start(f32[64,8,128]{2,1,0:T(8,128)S(1)} %get-tuple-element.92), channel_id=1, source_target_pairs={{0,12},{1,13},{16,28},{17,29},{32,44},{33,45},{48,60},{49,61},{2,1... | collective-permute-start | bytes 786440 | tf_op jit(solution)/shard_map/ppermute | solution.py:30
  93.8 14.9 %collective-permute-start.21 = (f32[128,8,128]{2,1,0:T(8,128)S(1)}, f32[128,8,128]{2,1,0:T(8,128)S(1)}, u32[]{:S(2)}, u32[]{:S(2)}) collective-permute-start(f32[128,8,128]{2,1,0:T(8,128)S(1)} %add_dynamic-update-slice_fusion), channel_id=1, source_target_pairs={{0,12},{1,13},{16,28},{17,29},{32,44},{33,45},{48,60},{49,61},{2,1... | collective-permute-start | bytes 1572872 | tf_op jit(solution)/shard_map/ppermute | solution.py:30
  96.9 15.5 %collective-permute-start.20 = (f32[128,8,128]{2,1,0:T(8,128)S(1)}, f32[128,8,128]{2,1,0:T(8,128)S(1)}, u32[]{:S(2)}, u32[]{:S(2)}) collective-permute-start(f32[128,8,128]{2,1,0:T(8,128)S(1)} %add_dynamic-update-slice_fusion.1), channel_id=1, source_target_pairs={{0,4},{1,5},{16,20},{17,21},{32,36},{33,37},{48,52},{49,53},{2,6},... | collective-permute-start | bytes 1572872 | tf_op jit(solution)/shard_map/ppermute | solution.py:30
  105.4 8.3 %collective-permute-start.13 = (f32[32,8,128]{2,1,0:T(8,128)S(1)}, f32[32,8,128]{2,1,0:T(8,128)S(1)}, u32[]{:S(2)}, u32[]{:S(2)}) collective-permute-start(f32[32,8,128]{2,1,0:T(8,128)S(1)} %get-tuple-element.104), channel_id=1, source_target_pairs={{0,4},{1,5},{16,20},{17,21},{32,36},{33,37},{48,52},{49,53},{2,6},... | collective-permute-start | bytes 393224 | tf_op jit(solution)/shard_map/ppermute | solution.py:30
  107.0 6.8 %collective-permute-start.14 = (f32[32,8,128]{2,1,0:T(8,128)S(1)}, f32[32,8,128]{2,1,0:T(8,128)S(1)}, u32[]{:S(2)}, u32[]{:S(2)}) collective-permute-start(f32[32,8,128]{2,1,0:T(8,128)S(1)} %get-tuple-element.103), channel_id=1, source_target_pairs={{0,12},{1,13},{16,28},{17,29},{32,44},{33,45},{48,60},{49,61},{2,1... | collective-permute-start | bytes 393224 | tf_op jit(solution)/shard_map/ppermute | solution.py:30
  112.4 6.5 %collective-permute-start.22 = (f32[64,8,128]{2,1,0:T(8,128)S(1)}, f32[64,8,128]{2,1,0:T(8,128)S(1)}, u32[]{:S(2)}, u32[]{:S(2)}) collective-permute-start(f32[64,8,128]{2,1,0:T(8,128)S(1)} %slice.94), channel_id=1, source_target_pairs={{0,2},{1,3},{16,18},{17,19},{32,34},{33,35},{48,50},{49,51},{2,0},... | collective-permute-start | bytes 786440 | tf_op jit(solution)/shard_map/ppermute | solution.py:30
  113.8 7.7 %collective-permute-start.15 = (f32[64,8,128]{2,1,0:T(8,128)S(1)}, f32[64,8,128]{2,1,0:T(8,128)S(1)}, u32[]{:S(2)}, u32[]{:S(2)}) collective-permute-start(f32[64,8,128]{2,1,0:T(8,128)S(1)} %get-tuple-element.99), channel_id=1, source_target_pairs={{0,4},{1,5},{16,20},{17,21},{32,36},{33,37},{48,52},{49,53},{2,6},... | collective-permute-start | bytes 786440 | tf_op jit(solution)/shard_map/ppermute | solution.py:30
  113.8 7.6 %collective-permute-start.16 = (f32[64,8,128]{2,1,0:T(8,128)S(1)}, f32[64,8,128]{2,1,0:T(8,128)S(1)}, u32[]{:S(2)}, u32[]{:S(2)}) collective-permute-start(f32[64,8,128]{2,1,0:T(8,128)S(1)} %get-tuple-element.100), channel_id=1, source_target_pairs={{0,12},{1,13},{16,28},{17,29},{32,44},{33,45},{48,60},{49,61},{2,1... | collective-permute-start | bytes 786440 | tf_op jit(solution)/shard_map/ppermute | solution.py:30
